TPU v7x, 32 devices: a whole 2x2x4 slice. The times are simulated.
32 devices in a mesh: groups: 2 (over x), frames: 16 (over z, y, core).
Axes of the slice: x: 2, y: 2, z: 4, core: 2. Of those that a mesh axis runs over, the one named last changes fastest.
Arguments:
- video: float32 [4, 16, 256, 256], P('groups', 'frames'), parts along dimension 0, may hold values from -9 to 9
- clip_start: int32 [4], P('groups'), parts along dimension 0, may hold values from 0 to 7
- gain_space: float32 [256], replicated, may hold values from 0.1 to 1.9
- qkv_space: float32 [256, 768], replicated, may hold values from -0.375 to 0.375
- out_space: float32 [256, 256], replicated, may hold values from -0.375 to 0.375
- gain_time: float32 [256], replicated, may hold values from 0.1 to 1.9
- qkv_time: float32 [256, 768], replicated, may hold values from -0.375 to 0.375
- out_time: float32 [256, 256], replicated, may hold values from -0.375 to 0.375
- code_sums: float32 [8192, 256], P(('groups', 'frames')), parts along dimension 0, may hold values from -12 to 12
- code_counts: float32 [8192], P(('groups', 'frames')), parts along dimension 0, may hold values from 1 to 10
Outputs:
- latents: float32 [4, 16, 256, 256], P('groups', None, 'frames'), parts along dimension 0
- new_sums: float32 [8192, 256], P(('groups', 'frames')), parts along dimension 0
- new_counts: float32 [8192], P(('groups', 'frames')), parts along dimension 0
- new_codebook: float32 [8192, 256], P(('groups', 'frames')), parts along dimension 0
There are 2 independent parts, one for each index of `groups`. A program takes and returns all parts, laid end to end along the dimension named above; an argument that names none is the same for every part. Nothing has to cross between parts.
All inputs are finite; a program needn't handle non-finite values.
Results may differ from a plain program's by a relative error of at most 0.0003.
Values sent between devices are 32-bit elements; how exact they have to be, the bound alone decides.
No kernel may reach another device: no remote copies, remote signals or barrier semaphores. Data moves between devices by JAX's collectives and lax.ppermute only.
A program may use at most 64 MiB of HBM per device.

v0:
```python
import jax
import jax.numpy as jnp
from jax import lax
from jax.sharding import PartitionSpec as P

HEADS = 4


ATTN_SCALE = 10.0
SOFTMAX_WARMTH = 0.05
DECAY_RATE = 0.9
EPSILON = 1e-06
TOP_PRECISION = lax.Precision.HIGHEST


def rms_norm(values, gain_vec):
    return values * lax.rsqrt(jnp.mean(values * values, -1, keepdims=True) + EPSILON) * gain_vec


def unit_vec(values):
    return values * lax.rsqrt(jnp.sum(values * values, -1, keepdims=True) + EPSILON)


def spatial_block(one_frame, gain_vec, w_qkv, w_out):
    width = one_frame.shape[-1]
    normed = rms_norm(one_frame, gain_vec)
    packed = jnp.dot(normed, w_qkv, precision=TOP_PRECISION)
    queries = unit_vec(packed[:, :width].reshape(-1, HEADS, width // HEADS))
    key_vecs = unit_vec(packed[:, width : 2 * width].reshape(-1, HEADS, width // HEADS))
    values = packed[:, 2 * width :].reshape(-1, HEADS, width // HEADS)
    scores = ATTN_SCALE * jnp.einsum("qhd,khd->hqk", queries, key_vecs, precision=TOP_PRECISION)
    assignment_weights = jnp.exp(scores)
    totals = jnp.sum(assignment_weights, -1).T[:, :, None]
    mixed = jnp.einsum("hqk,khd->qhd", assignment_weights, values, precision=TOP_PRECISION) / totals
    return one_frame + jnp.dot(mixed.reshape(-1, width), w_out, precision=TOP_PRECISION)


def time_block(spaced, clip_start, gain_vec, w_qkv, w_out):
    clips, frames, places, width = spaced.shape
    normed = rms_norm(spaced, gain_vec)
    packed = jnp.einsum("ctpd,de->ctpe", normed, w_qkv, precision=TOP_PRECISION)
    shape_heads = (clips, frames, places, HEADS, width // HEADS)
    queries = unit_vec(packed[..., :width].reshape(shape_heads))
    key_vecs = unit_vec(packed[..., width : 2 * width].reshape(shape_heads))
    values = packed[..., 2 * width :].reshape(shape_heads)
    scores = ATTN_SCALE * jnp.einsum(
        "ctphd,csphd->cphts", queries, key_vecs, precision=TOP_PRECISION
    )
    later = jnp.arange(frames, dtype=jnp.int32)[:, None]
    earlier = jnp.arange(frames, dtype=jnp.int32)[None, :]
    allowed = (earlier <= later)[None] & (
        (earlier[None] >= clip_start[:, None, None]) | (earlier == later)[None]
    )
    assignment_weights = jnp.exp(scores) * allowed[:, None, None, :, :].astype(jnp.float32)
    totals = jnp.transpose(jnp.sum(assignment_weights, -1), (0, 3, 1, 2))[..., None]
    mixed = (
        jnp.einsum("cphts,csphd->ctphd", assignment_weights, values, precision=TOP_PRECISION)
        / totals
    )
    return spaced + jnp.einsum(
        "ctpd,de->ctpe", mixed.reshape(clips, frames, places, width), w_out, precision=TOP_PRECISION
    )


def local(
    video,
    clip_start,
    gain_space,
    qkv_space,
    out_space,
    gain_time,
    qkv_time,
    out_time,
    code_sums,
    code_counts,
):
    clips, local_frames, places, width = video.shape
    flat_frames = video.reshape(clips * local_frames, places, width)
    spaced = lax.map(
        lambda one_frame: spatial_block(one_frame, gain_space, qkv_space, out_space), flat_frames
    )
    spaced = spaced.reshape(clips, local_frames, places, width)
    by_place = lax.all_to_all(spaced, "frames", split_axis=2, concat_axis=1, tiled=True)
    latents = time_block(by_place, clip_start, gain_time, qkv_time, out_time)
    unit_token_vectors = unit_vec(latents.reshape(-1, width))
    local_codes = unit_vec(code_sums / code_counts[:, None])
    codebook_matrix = lax.all_gather(local_codes, "frames", axis=0, tiled=True)
    assignment_weights = jnp.exp(
        jnp.dot(unit_token_vectors, codebook_matrix.T, precision=TOP_PRECISION) / SOFTMAX_WARMTH
    )
    probs = assignment_weights / jnp.sum(assignment_weights, 1, keepdims=True)
    term_sums = lax.dot_general(
        probs, unit_token_vectors, (((0,), (0,)), ((), ())), precision=TOP_PRECISION
    )
    term_counts = jnp.sum(probs, 0)
    got_sums, got_counts = (
        lax.psum_scatter(term_sums, "frames", scatter_dimension=0, tiled=True),
        lax.psum_scatter(term_counts, "frames", scatter_dimension=0, tiled=True),
    )
    new_sums = DECAY_RATE * code_sums + (1.0 - DECAY_RATE) * got_sums
    new_counts = DECAY_RATE * code_counts + (1.0 - DECAY_RATE) * got_counts
    new_codebook = new_sums / new_counts[:, None]
    return (latents, new_sums, new_counts, new_codebook)


def solution(mesh):
    in_specs = (
        P("groups", "frames", None, None),
        P("groups"),
        P(),
        P(),
        P(),
        P(),
        P(),
        P(),
        P(("groups", "frames"), None),
        P(("groups", "frames")),
    )
    out_specs = (
        P("groups", None, "frames", None),
        P(("groups", "frames"), None),
        P(("groups", "frames")),
        P(("groups", "frames"), None),
    )
    return jax.shard_map(local, mesh=mesh, in_specs=in_specs, out_specs=out_specs, check_vma=False)
```

profile of v0, /device:TPU:0, one launch (start us, length us, event | category | flops | bytes accessed | tf_op | source)
XLA Modules:
  0.0 198.6 jit_solution(9034979632726046601)
XLA Ops:
  7.2 1.2 multiply_reduce_fusion.6
  8.4 1.8 broadcast_multiply_fusion.2
  10.3 25.9 %while.10 = (s32[]{:T(128)}, f32[2,256,256]{2,0,1:T(2,128)}, f32[2,256,256]{2,1,0:T(8,128)}, f32[256]{0:T(256)}, f32[256,768]{1,0:T(8,128)}, /*index=5*/f32[256,256]{1,0:T(8,128)}, s32[]{:T(128)}, s32[]{:T(128)}) while((s32[]{:T(128)}, f32[2,256,256]{2,0,1:T(2,128)}, f32[2,256,256]{2,1,0:T(8,128)}, f32[256]{0:T(256)}, f32[256,768]{1,0:T(8,128)}, ...), condition=%wide.region_5.6_spmd, body=%wide.region_0.5_spmd.sunk | while | flops 1209269504 | bytes 14202521 | solution.py:79
  10.3 1.1 fusion.67
  11.5 2.1 %fusion.68 = f32[256,768]{1,0:T(8,128)S(1)} fusion(f32[256,768]{1,0:T(8,128)} %get-tuple-element.142, f32[2,256,256]{2,1,0:T(8,128)} %get-tuple-element.140, s32[]{:T(128)} %get-tuple-element.130, f32[256]{0:T(256)} %get-tuple-element.141, f32[256]{0:T(256)S(1)} %add_rsqrt_fusion.10), kind=kOutput, calls=%fused_computation.10.clone.1 | convolution fusion | flops 604110848 | bytes 1837568 | tf_op jit(solution)/shard_map/while/body/eval_jaxpr/dot_general | solution.py:27
  14.0 1.1 fusion.70
  15.3 0.8 fusion.71
  16.9 6.3 %dynamic_update_slice.5 = f32[2,256,256]{2,0,1:T(2,128)} dynamic-update-slice(f32[2,256,256]{2,0,1:T(2,128)} %get-tuple-element.131, f32[1,256,256]{2,0,1:T(1,128)S(1)} %copy.85, s32[]{:T(128)} %get-tuple-element.130, s32[]{:T(128)} %constant.22.clone.1..sunk, s32[]{:T(128)} %constant.22.clone.1..sunk) | dynamic-update-slice | bytes 524292 | tf_op jit(solution)/shard_map/while/body/jit(dynamic_update_index_in_dim)/dynamic_update_slice | solution.py:79
  23.3 1.1 fusion.67
  24.4 2.1 %fusion.68 = f32[256,768]{1,0:T(8,128)S(1)} fusion(f32[256,768]{1,0:T(8,128)} %get-tuple-element.142, f32[2,256,256]{2,1,0:T(8,128)} %get-tuple-element.140, s32[]{:T(128)} %get-tuple-element.130, f32[256]{0:T(256)} %get-tuple-element.141, f32[256]{0:T(256)S(1)} %add_rsqrt_fusion.10), kind=kOutput, calls=%fused_computation.10.clone.1 | convolution fusion | flops 604110848 | bytes 1837568 | tf_op jit(solution)/shard_map/while/body/eval_jaxpr/dot_general | solution.py:27
  26.9 1.1 fusion.70
  28.2 0.8 fusion.71
  29.9 6.3 %dynamic_update_slice.5 = f32[2,256,256]{2,0,1:T(2,128)} dynamic-update-slice(f32[2,256,256]{2,0,1:T(2,128)} %get-tuple-element.131, f32[1,256,256]{2,0,1:T(1,128)S(1)} %copy.85, s32[]{:T(128)} %get-tuple-element.130, s32[]{:T(128)} %constant.22.clone.1..sunk, s32[]{:T(128)} %constant.22.clone.1..sunk) | dynamic-update-slice | bytes 524292 | tf_op jit(solution)/shard_map/while/body/jit(dynamic_update_index_in_dim)/dynamic_update_slice | solution.py:79
  36.2 7.4 %all-to-all-start = ((f32[2,1,256,256]{3,0,1,2:T(2,128)}), f32[2,1,256,256]{3,0,1,2:T(2,128)S(1)}, u32[]{:S(2)}, u32[]{:S(2)}) async-start(f32[2,1,256,256]{3,0,1,2:T(2,128)} %bitcast.103), calls=%async_computation | async-start | bytes 1048576 | tf_op jit(solution)/shard_map/all_to_all | solution.py:83
  43.8 22.8 %all-to-all-done = f32[2,1,256,256]{3,0,1,2:T(2,128)S(1)} async-done(((f32[2,1,256,256]{3,0,1,2:T(2,128)}), f32[2,1,256,256]{3,0,1,2:T(2,128)S(1)}, u32[]{:S(2)}, u32[]{:S(2)}) %all-to-all-start) | async-done | bytes 524320 | tf_op jit(solution)/shard_map/all_to_all | solution.py:83
  67.2 1.5 fusion.23
  68.7 1.2 fusion.37
  70.3 1.5 reshape.171
  71.8 2.5 %reshape.170 = f32[2,16,16,4,64]{4,3,2,1,0:T(4,128)} reshape(f32[2,16,16,256]{3,2,1,0:T(8,128)} %get-tuple-element.58) | data formatting | bytes 1048576 | tf_op jit(solution)/shard_map/reshape | solution.py:45
  74.9 0.6 multiply_reduce_fusion.3
  75.6 1.5 broadcast_multiply_fusion
  77.1 3.1 %fusion.38 = (f32[2,16,4,16]{3,2,1,0:T(4,128)S(1)}, f32[2,16,4,16,16]{3,4,2,1,0:T(8,128)S(1)}) fusion(f32[2,16,16]{1,2,0:T(8,128)S(1)} %and_convert_fusion, f32[2,16,16,4,64]{4,3,2,1,0:T(4,128)S(1)} %get-tuple-element.69, f32[2,16,16,4,64]{4,3,2,1,0:T(4,128)S(1)} %get-tuple-element.70), kind=kOutput, calls=%fused_computation.72 | convolution fusion | flops 25262080 | bytes 1189888 | tf_op jit(solution)/shard_map/ctphd,csphd->cphts/dot_general | solution.py:46
  80.2 2.5 %fusion.17 = f32[2,16,16,4,64]{4,1,3,2,0:T(8,128)S(1)} fusion(f32[2,16,4,16,16]{3,4,2,1,0:T(8,128)S(1)} %get-tuple-element.62, f32[2,16,16,4,64]{4,3,2,1,0:T(4,128)S(1)} %copy-done.6, f32[2,16,16,4]{1,3,2,0:T(4,128)S(1)} %bitcast.106), kind=kOutput, calls=%fused_computation.28 | convolution fusion | flops 25296896 | bytes 1187840 | tf_op jit(solution)/shard_map/cphts,csphd->ctphd/dot_general | solution.py:57
  83.2 0.6 reshape.173
  83.8 1.6 multiply_reduce_fusion.4
  85.7 9.9 %fusion.16 = (f32[512]{0:T(512)S(1)}, f32[512,4096]{1,0:T(8,128)S(1)}) fusion(f32[512,256]{1,0:T(8,128)S(1)} %bitcast_multiply_fusion.2, f32[4096,256]{1,0:T(8,128)} %all-gather.2.cloned.1.call-done), kind=kOutput, calls=%fused_computation.26 | convolution fusion | flops 6446644736 | bytes 13109248 | tf_op jit(solution)/shard_map/dot_general | solution.py:89
  95.6 3.2 %copy-done.1 = f32[512,4096]{1,0:T(8,128)} copy-done((f32[512,4096]{1,0:T(8,128)}, f32[512,4096]{1,0:T(8,128)S(1)}, u32[]{:S(2)}) %copy-start.1) | copy-done | bytes 8388632
  98.8 15.0 %fusion.28 = f32[4096,256]{1,0:T(8,128)} fusion(f32[512,256]{1,0:T(8,128)S(1)} %bitcast_multiply_fusion.2, f32[512,4096]{1,0:T(8,128)S(1)} %get-tuple-element.66, f32[512]{0:T(512)S(1)} %get-tuple-element.65), kind=kOutput, calls=%fused_computation.48 | convolution fusion | flops 6446645248 | bytes 13109248 | tf_op jit(solution)/shard_map/dot_general | solution.py:92
  115.2 4.3 %fusion.27 = f32[4096]{0:T(1024)S(1)} fusion(f32[512]{0:T(512)S(1)} %get-tuple-element.65, f32[512,4096]{1,0:T(8,128)} %copy-done.1), kind=kLoop, calls=%fused_computation.47 | loop fusion | flops 6287360 | bytes 8407040 | tf_op jit(solution)/shard_map/reduce_sum | solution.py:95
  119.4 64.4 %all-reduce = f32[4096]{0:T(1024)S(1)} all-reduce(f32[4096]{0:T(1024)S(1)} %fusion.27), channel_id=3, replica_groups=mesh['groups'=2,'frames'=16] {'frames'}, use_global_device_ids=true, to_apply=%region_15.16.clone | all-reduce | flops 4096 | bytes 32768
  183.9 6.0 %reduce-scatter.2.cloned.1.call-done = f32[256,256]{1,0:T(8,128)} async-done(((f32[4096,256]{1,0:T(8,128)}), f32[256,256]{1,0:T(8,128)}) %reduce-scatter.2.cloned.1.call-update) | async-done | bytes 262160 | tf_op jit(solution)/shard_map/reduce_scatter | solution.py:97
  190.0 1.8 broadcast_divide_fusion
  (71 shorter events, 6.2 us)
Async XLA Ops:
  7.2 60.0 %copy-start = (f32[256,768]{1,0:T(8,128)S(1)}, f32[256,768]{1,0:T(8,128)}, u32[]{:S(2)}) copy-start(f32[256,768]{1,0:T(8,128)} %param.18) | copy-start | bytes 2359300
  7.2 78.5 %all-gather.2.cloned.1.call-start = ((), (), s32[]{:S(2)}) async-start(), calls=%async_computation.2 | async-start | bytes 4456448 | tf_op jit(solution)/shard_map/all_gather | solution.py:87
  10.3 33.4 %copy-start.10 = (s32[2]{0:T(128)S(1)}, s32[2]{0:T(128)}, u32[]{:S(2)}) copy-start(s32[2]{0:T(128)} %param.13) | copy-start | bytes 28
  10.3 56.9 %copy-start.9 = (f32[256]{0:T(256)S(1)}, f32[256]{0:T(256)}, u32[]{:S(2)}) copy-start(f32[256]{0:T(256)} %param.17) | copy-start | bytes 3076
  10.3 5.7 %copy-start.2 = (f32[2,256,256]{2,1,0:T(8,128)S(1)}, f32[2,256,256]{2,1,0:T(8,128)}, u32[]{:S(2)}) copy-start(f32[2,256,256]{2,1,0:T(8,128)} %get-tuple-element.140) | copy-start | bytes 1572868 | tf_op jit(solution)/shard_map/while
  10.3 5.7 %copy-start.3 = (f32[256,256]{1,0:T(8,128)S(1)}, f32[256,256]{1,0:T(8,128)}, u32[]{:S(2)}) copy-start(f32[256,256]{1,0:T(8,128)} %get-tuple-element.143) | copy-start | bytes 786436 | tf_op jit(solution)/shard_map/while
  23.3 5.7 %copy-start.2 = (f32[2,256,256]{2,1,0:T(8,128)S(1)}, f32[2,256,256]{2,1,0:T(8,128)}, u32[]{:S(2)}) copy-start(f32[2,256,256]{2,1,0:T(8,128)} %get-tuple-element.140) | copy-start | bytes 1572868 | tf_op jit(solution)/shard_map/while
  23.3 5.7 %copy-start.3 = (f32[256,256]{1,0:T(8,128)S(1)}, f32[256,256]{1,0:T(8,128)}, u32[]{:S(2)}) copy-start(f32[256,256]{1,0:T(8,128)} %get-tuple-element.143) | copy-start | bytes 786436 | tf_op jit(solution)/shard_map/while
  36.2 30.4 %all-to-all-start = ((f32[2,1,256,256]{3,0,1,2:T(2,128)}), f32[2,1,256,256]{3,0,1,2:T(2,128)S(1)}, u32[]{:S(2)}, u32[]{:S(2)}) async-start(f32[2,1,256,256]{3,0,1,2:T(2,128)} %bitcast.103), calls=%async_computation | async-start | bytes 1048576 | tf_op jit(solution)/shard_map/all_to_all | solution.py:83
  43.6 146.4 %reduce-scatter.2.cloned.1.call-start = ((), (), s32[]{:S(2)}) async-start(), calls=%async_computation.3 | async-start | bytes 4456448 | tf_op jit(solution)/shard_map/reduce_scatter | solution.py:97
  74.2 6.0 %copy-start.6 = (f32[2,16,16,4,64]{4,3,2,1,0:T(4,128)S(1)}, f32[2,16,16,4,64]{4,3,2,1,0:T(4,128)}, u32[]{:S(2)}) copy-start(f32[2,16,16,4,64]{4,3,2,1,0:T(4,128)} %reshape.170) | copy-start | bytes 1572868
  85.4 28.5 %copy-start.5 = (f32[2,16,16,256]{3,2,1,0:T(8,128)}, f32[2,16,16,256]{3,2,1,0:T(8,128)S(1)}, u32[]{:S(2)}) copy-start(f32[2,16,16,256]{3,2,1,0:T(8,128)S(1)} %get-tuple-element.64) | copy-start | bytes 1572868
  95.6 3.2 %copy-start.1 = (f32[512,4096]{1,0:T(8,128)}, f32[512,4096]{1,0:T(8,128)S(1)}, u32[]{:S(2)}) copy-start(f32[512,4096]{1,0:T(8,128)S(1)} %get-tuple-element.66) | copy-start | bytes 25165828
  98.8 15.1 %copy-start.11 = (u32[32]{0:T(128)S(1)}, u32[32]{0:T(128)}, u32[]{:S(2)}) copy-start(u32[32]{0:T(128)} %constant.46) | copy-start | bytes 388
  113.9 70.0 %copy-start.7 = (f32[256]{0:T(256)S(1)}, f32[256]{0:T(256)}, u32[]{:S(2)}) copy-start(f32[256]{0:T(256)} %param.21) | copy-start | bytes 3076
  113.9 76.1 %copy-start.4 = (f32[256,256]{1,0:T(8,128)S(1)}, f32[256,256]{1,0:T(8,128)}, u32[]{:S(2)}) copy-start(f32[256,256]{1,0:T(8,128)} %param.20) | copy-start | bytes 786436
  183.9 7.8 %copy-start.8 = (f32[256]{0:T(256)}, f32[256]{0:T(256)S(1)}, u32[]{:S(2)}) copy-start(f32[256]{0:T(256)S(1)} %fusion.33) | copy-start | bytes 3076
Sparse Core Ops, SparseCore 0:
  10.8 62.1 all-gather.1
  114.0 75.8 reduce-scatter.1
where the time goes:
time: 200 us; the launch traced here: 199 us
  blocking collectives  64.4 us (32%)
  matrix products  42.9 us (21%)
  waiting for transfers between devices  28.9 us (14%)
  local copies, waits for them, and re-layouts  24.8 us (12%)
  other arithmetic  15 us (8%)
  between operations  14.9 us (7%)
  starting transfers between devices  7.47 us (4%)
    unnamed x1, blocking collectives  64.4 us
    all_to_all x1, waiting for transfers between devices, local(): lax.all_to_all(spaced, 'frames', split_axis=2, concat_axis=1, tiled=True)  22.8 us
    dot_general x1, matrix products, local(): lax.dot_general(probs, unit_token_vectors, (((0,), (0,)), ((), ())), prec...  15 us
    dynamic_update_slice x4, local copies, waits for them, and re-layouts, local(): lax.map(lambda one_frame: spatial_block(one_frame, gain_space, qkv_space,...  13.2 us
    dot_general x1, matrix products, local(): jnp.dot(unit_token_vectors, codebook_matrix.T, precision=TOP_PRECISION)  9.91 us
    all_to_all x1, starting transfers between devices, local(): lax.all_to_all(spaced, 'frames', split_axis=2, concat_axis=1, tiled=True)  7.39 us
    reduce_scatter x1, waiting for transfers between devices, local(): lax.psum_scatter(term_sums, 'frames', scatter_dimension=0, tiled=True)  6.03 us
    reduce_sum x1, other arithmetic, local(): term_counts = jnp.sum(probs, 0)  4.27 us
  transfers between devices with their start and end apart: 3, of which 2 were waited for; matrix products, arithmetic and copies ran while one was open for 25% of the time, Pallas kernels for 0%

commit v1 on v0

v1 whole, which is shorter than its diff:
```python
import math

import jax
import jax.numpy as jnp
from jax import lax
from jax.experimental import pallas as pl
from jax.experimental.pallas import tpu as pltpu
from jax.sharding import PartitionSpec as P

HEADS = 4
ATTN_SCALE = 10.0
SOFTMAX_WARMTH = 0.05
DECAY_RATE = 0.9
EPSILON = 1e-06
SHARERS = 4
VMEM_BYTES = 40 * 1024 * 1024
BF16 = jnp.bfloat16
F32 = jnp.float32


def params(**kw):
    return pltpu.CompilerParams(vmem_limit_bytes=VMEM_BYTES, **kw)


def split(x):
    high = x.astype(BF16)
    return high, (x - high.astype(F32)).astype(BF16)


def dot(a, b):
    return jnp.dot(a, b, preferred_element_type=F32)


def dot_t(a, b):
    return lax.dot_general(a, b, (((1,), (1,)), ((), ())), preferred_element_type=F32)


def dot3(a, b, product=dot):
    ah, al = a
    bh, bl = b
    return product(ah, bh) + (product(al, bh) + product(ah, bl))


def attend(x, gain, w_qkv, w_out, mask):
    tokens, width = x.shape
    head = width // HEADS
    h = x * lax.rsqrt(jnp.mean(x * x, -1, keepdims=True) + EPSILON) * gain
    packed = dot3(split(h), split(w_qkv))
    row_head = lax.broadcasted_iota(jnp.int32, (width, width), 0) // head
    lane_head = lax.broadcasted_iota(jnp.int32, (width, width), 1) // head
    same_head = (row_head == lane_head).astype(BF16)

    def unit_heads(v):
        high, low = split(v * v)
        return v * lax.rsqrt(dot(high, same_head) + dot(low, same_head) + EPSILON)

    q = split(unit_heads(packed[:, :width]) * ATTN_SCALE)
    k = split(unit_heads(packed[:, width : 2 * width]))
    v = split(packed[:, 2 * width :])
    lanes = lax.broadcasted_iota(jnp.int32, (tokens, width), 1) // head
    mixed = jnp.zeros((tokens, width), F32)
    for i in range(HEADS):
        mine = lanes == i
        qi = [jnp.where(mine, part, jnp.zeros_like(part)) for part in q]
        weights = jnp.exp(dot3(qi, k, dot_t))
        if mask is not None:
            weights = jnp.where(mask, weights, 0.0)
        vi = [jnp.where(mine, part, jnp.full_like(part, fill)) for part, fill in zip(v, (1.0, 0.0))]
        r = dot3(split(weights), vi)
        totals = jnp.concatenate([r[:, width // 2 :], r[:, : width // 2]], axis=1)
        mixed = jnp.where(mine, r / totals, mixed)
    return x + dot3(split(mixed), split(w_out))


def space_kernel(x_ref, gain_ref, w_qkv_ref, w_out_ref, out_ref):
    y = attend(x_ref[0], gain_ref[...], w_qkv_ref[...], w_out_ref[...], None)
    out_ref[...] = y.reshape(out_ref.shape)


def time_kernel(start_ref, x_ref, gain_ref, w_qkv_ref, w_out_ref, latents_ref, unit_ref):
    senders, _, local_frames, places, width = x_ref.shape
    tokens = senders * local_frames * places
    x = x_ref[...].reshape(tokens, width)
    rows = lax.broadcasted_iota(jnp.int32, (tokens, tokens), 0)
    cols = lax.broadcasted_iota(jnp.int32, (tokens, tokens), 1)
    later, earlier = rows // places, cols // places
    start = start_ref[pl.program_id(0)]
    mask = ((rows - later * places) == (cols - earlier * places)) & (
        (earlier == later) | ((earlier < later) & (earlier >= start))
    )
    y = attend(x, gain_ref[...], w_qkv_ref[...], w_out_ref[...], mask)
    latents_ref[...] = y.reshape(latents_ref.shape)
    unit_ref[...] = y * lax.rsqrt(jnp.sum(y * y, -1, keepdims=True) + EPSILON)


def column(row, lanes):
    return jnp.transpose(jnp.broadcast_to(row, (lanes, row.shape[1])))


def code_kernel(sums_ref, counts_ref, out_ref):
    book = sums_ref[...] / column(counts_ref[...], sums_ref.shape[1])
    unit = book * lax.rsqrt(jnp.sum(book * book, -1, keepdims=True) + EPSILON)
    out_ref[...] = unit * (math.log2(math.e) / SOFTMAX_WARMTH)


def score_kernel(*refs, blocks, chunks):
    codes, units = refs[:blocks], refs[blocks : blocks + chunks]
    w_ref, totals_ref = refs[blocks + chunks :]
    rows = codes[0].shape[0]
    for j in range(chunks):
        u = units[j][...].astype(BF16)
        totals = None
        for r in range(blocks):
            high, low = split(codes[r][...])
            w = jnp.exp2(dot_t(high, u) + dot_t(low, u)).astype(BF16)
            w_ref[j, r * rows : (r + 1) * rows, :] = w
            part = jnp.sum(w.astype(F32), 0, keepdims=True)
            totals = part if totals is None else totals + part
        totals_ref[j] = totals


def term_kernel(*refs, blocks, chunks, calls):
    ws, refs = refs[:calls], refs[calls:]
    units, refs = refs[:chunks], refs[chunks:]
    totals, (out_ref,) = refs[: SHARERS * calls], refs[SHARERS * calls :]
    each = chunks // calls
    rows = ws[0].shape[1] // blocks
    width = units[0].shape[1]
    scaled, shares = [], []
    for j in range(chunks):
        total = None
        for m in range(SHARERS):
            source = j ^ m
            part = totals[m * calls + source // each][source % each]
            total = part if total is None else total + part
        share = 1.0 / total
        column_share = column(share, 128)
        column_share = jnp.concatenate([column_share] * (width // 128), axis=1)
        scaled.append((units[j][...] * column_share).astype(BF16))
        high, low = split(share)
        index = lax.broadcasted_iota(jnp.int32, (16, share.shape[1]), 0)
        shares.append(
            jnp.where(index == 0, high.astype(F32), jnp.where(index == 1, low.astype(F32), 0.0)).astype(BF16)
        )
    for r in range(blocks):
        sums = jnp.zeros((rows, width), F32)
        counts = jnp.zeros((16, rows), F32)
        for j in range(chunks):
            w = ws[j // each][j % each, r * rows : (r + 1) * rows, :]
            sums = sums + dot(w, scaled[j])
            counts = counts + dot_t(shares[j], w)
        out_ref[r, :rows, :] = sums
        counts = jnp.sum(counts, 0, keepdims=True)
        if rows < width:
            counts = jnp.concatenate([counts, jnp.zeros((1, width - rows), F32)], axis=1)
        out_ref[r, rows:, :] = jnp.broadcast_to(counts, (8, width))


def update_kernel(*refs, blocks):
    sums_ref, counts_ref = refs[:2]
    terms = refs[2 : 2 + blocks]
    new_sums_ref, new_counts_ref, new_book_ref = refs[2 + blocks :]
    rows, width = sums_ref.shape
    term = terms[0][...]
    for other in terms[1:]:
        term = term + other[...]
    sums = DECAY_RATE * sums_ref[...] + (1.0 - DECAY_RATE) * term[:rows]
    counts = DECAY_RATE * counts_ref[...] + (1.0 - DECAY_RATE) * term[rows : rows + 1, :rows]
    new_sums_ref[...] = sums
    new_counts_ref[...] = counts
    new_book_ref[...] = sums / column(counts, width)


def whole(a):
    return pl.BlockSpec(a.shape, lambda *_: (0,) * a.ndim)


def cost(flops, *arrays):
    return pl.CostEstimate(
        flops=int(flops), bytes_accessed=int(sum(a.size * a.dtype.itemsize for a in arrays)), transcendentals=0
    )


def shape(*dims, dtype=F32):
    return jax.ShapeDtypeStruct(dims, dtype)


def simple_call(kernel, outs, *args, flops=0, name=None):
    return pl.pallas_call(
        kernel,
        out_shape=outs,
        compiler_params=params(),
        cost_estimate=cost(flops, *args, *(outs if isinstance(outs, (tuple, list)) else [outs])),
        name=name,
    )(*args)


def make_local(devices):
    sharers, blocks = SHARERS, devices // SHARERS

    def swap(x, bits):
        return lax.ppermute(x, "frames", [(i, i ^ bits) for i in range(devices)])

    def local(
        video,
        clip_start,
        gain_space,
        qkv_space,
        out_space,
        gain_time,
        qkv_time,
        out_time,
        code_sums,
        code_counts,
    ):
        clips, local_frames, all_places, width = video.shape
        places = all_places // devices
        frames = local_frames * devices
        code_rows = code_sums.shape[0]
        tiles = clips * local_frames
        tokens = frames * places
        flat = video.reshape(tiles, all_places, width)
        gain_space, gain_time = gain_space[None], gain_time[None]
        counts_row = code_counts[None]

        codes = simple_call(code_kernel, shape(code_rows, width), code_sums, counts_row, name="unit_codes")
        code_blocks = [codes] + [swap(codes, r * sharers) for r in range(1, blocks)]

        spaced = pl.pallas_call(
            space_kernel,
            grid=(tiles,),
            in_specs=[
                pl.BlockSpec((1, all_places, width), lambda i: (i, 0, 0)),
                whole(gain_space),
                whole(qkv_space),
                whole(out_space),
            ],
            out_specs=pl.BlockSpec((devices, 1, places, width), lambda i: (0, i, 0, 0)),
            out_shape=shape(devices, tiles, places, width),
            compiler_params=params(),
            cost_estimate=cost(tiles * 4e9, flat, qkv_space),
            name="space_attention",
        )(flat, gain_space, qkv_space, out_space)

        by_place = lax.all_to_all(spaced, "frames", split_axis=0, concat_axis=0, tiled=True)
        by_place = by_place.reshape(devices, clips, local_frames, places, width)

        latents, unit = pl.pallas_call(
            time_kernel,
            grid=(clips,),
            in_specs=[
                pl.BlockSpec(memory_space=pltpu.SMEM),
                pl.BlockSpec((devices, 1, local_frames, places, width), lambda i: (0, i, 0, 0, 0)),
                whole(gain_time),
                whole(qkv_time),
                whole(out_time),
            ],
            out_specs=(
                pl.BlockSpec((1, frames, places, width), lambda i: (i, 0, 0, 0)),
                pl.BlockSpec((tokens, width), lambda i: (i, 0)),
            ),
            out_shape=(shape(clips, frames, places, width), shape(clips * tokens, width)),
            compiler_params=params(),
            cost_estimate=cost(clips * 4e9, spaced, qkv_time),
            name="time_attention",
        )(clip_start, by_place, gain_time, qkv_time, out_time)

        far = swap(unit, 2)
        units = [unit, swap(unit, 1), far, swap(far, 1)]
        chunk_tokens = clips * tokens

        def score(chunk_units):
            n = len(chunk_units)
            return simple_call(
                lambda *refs: score_kernel(*refs, blocks=blocks, chunks=n),
                (
                    shape(n, blocks * code_rows, chunk_tokens, dtype=BF16),
                    shape(n, 1, chunk_tokens),
                ),
                *code_blocks,
                *chunk_units,
                flops=n * 4 * blocks * code_rows * chunk_tokens * width,
                name="scores",
            )

        near_w, near_totals = score(units[:2])
        far_w, far_totals = score(units[2:])
        totals = [near_totals, far_totals]
        for m in range(1, sharers):
            totals += [swap(near_totals, m), swap(far_totals, m)]

        terms = simple_call(
            lambda *refs: term_kernel(*refs, blocks=blocks, chunks=sharers, calls=2),
            shape(blocks, code_rows + 8, width),
            near_w,
            far_w,
            *units,
            *totals,
            flops=2 * sharers * blocks * code_rows * chunk_tokens * width,
            name="terms",
        )
        arrived = [terms[0]] + [swap(terms[r], r * sharers) for r in range(1, blocks)]
        new_sums, new_counts, new_codebook = simple_call(
            lambda *refs: update_kernel(*refs, blocks=blocks),
            (shape(code_rows, width), shape(1, code_rows), shape(code_rows, width)),
            code_sums,
            counts_row,
            *arrived,
            name="update",
        )
        return (latents, new_sums, new_counts[0], new_codebook)

    return local


def solution(mesh):
    in_specs = (
        P("groups", "frames", None, None),
        P("groups"),
        P(),
        P(),
        P(),
        P(),
        P(),
        P(),
        P(("groups", "frames"), None),
        P(("groups", "frames")),
    )
    out_specs = (
        P("groups", None, "frames", None),
        P(("groups", "frames"), None),
        P(("groups", "frames")),
        P(("groups", "frames"), None),
    )
    local = make_local(mesh.shape["frames"])
    return jax.shard_map(local, mesh=mesh, in_specs=in_specs, out_specs=out_specs, check_vma=False)
```

time: 200 us -> 113 us (0.56)
  matrix products: 42.9 us -> 0 us
  blocking collectives: 64.4 us -> 21.7 us
  waiting for transfers between devices: 28.9 us -> 56.2 us
  local copies, waits for them, and re-layouts: 24.8 us -> 3.9 us
  Pallas kernels: 0 us -> 17 us
  other arithmetic: 15 us -> 0 us
  between operations: 14.9 us -> 0.74 us
  starting transfers between devices: 7.47 us -> 13.6 us
    unnamed x1 -> x0, blocking collectives: 64.4 us -> none
    ppermute x0 -> x15, waiting for transfers between devices: none -> 56.2 us  [swap(): return lax.ppermute(x, 'frames', [(i, i ^ bits) for i in range(devices)])]
    dot_general x14 -> x0, matrix products: 42.9 us -> none  [the longest x1 15 us: local(): lax.dot_general(probs, unit_token_vectors, (((0,), (0,)), ((), ())), prec...]
    all_to_all x1 -> x0, waiting for transfers between devices: 22.8 us -> none  [local(): lax.all_to_all(spaced, 'frames', split_axis=2, concat_axis=1, tiled=True)]
    all_to_all x0 -> x1, blocking collectives: none -> 21.7 us  [local(): lax.all_to_all(spaced, 'frames', split_axis=0, concat_axis=0, tiled=True)]
    pallas_call x0 -> x7, Pallas kernels: none -> 17 us  [the longest x5 6.2 us: simple_call(): pl.pallas_call(kernel, out_shape=outs, compiler_params=params(), cost_est...]
    ppermute x0 -> x15, starting transfers between devices: none -> 13.6 us  [swap(): return lax.ppermute(x, 'frames', [(i, i ^ bits) for i in range(devices)])]
    dynamic_update_slice x4 -> x0, local copies, waits for them, and re-layouts: 13.2 us -> none  [local(): lax.map(lambda one_frame: spatial_block(one_frame, gain_space, qkv_space,...]
  transfers between devices with their start and end apart: 3 -> 15, of which waited for: 2 -> 7; matrix products, arithmetic and copies ran while one was open for 25% -> 0% of each run, Pallas kernels for 0% -> 3%
where the time goes in v1:
time: 113 us
  waiting for transfers between devices  56.2 us (50%)
  blocking collectives  21.7 us (19%)
  Pallas kernels  17 us (15%)
  starting transfers between devices  13.6 us (12%)
  local copies, waits for them, and re-layouts  3.9 us (3%)
    ppermute x15, waiting for transfers between devices, swap(): return lax.ppermute(x, 'frames', [(i, i ^ bits) for i in range(devices)])  56.2 us
    all_to_all x1, blocking collectives, local(): lax.all_to_all(spaced, 'frames', split_axis=0, concat_axis=0, tiled=True)  21.7 us
    ppermute x15, starting transfers between devices, swap(): return lax.ppermute(x, 'frames', [(i, i ^ bits) for i in range(devices)])  13.6 us
    pallas_call x5, Pallas kernels, simple_call(): pl.pallas_call(kernel, out_shape=outs, compiler_params=params(), cost_est...  6.2 us
    pallas_call x1, Pallas kernels, local(): pl.pallas_call(time_kernel, grid=(clips,), in_specs=[pl.BlockSpec(memory_...  6.14 us
    pallas_call x1, Pallas kernels, local(): pl.pallas_call(space_kernel, grid=(tiles,), in_specs=[pl.BlockSpec((1, al...  4.7 us
    unnamed x20, local copies, waits for them, and re-layouts  3.82 us
  transfers between devices with their start and end apart: 15, of which 7 were waited for; matrix products, arithmetic and copies ran while one was open for 0% of the time, Pallas kernels for 3%

profile of v1, /device:TPU:0, one launch (start us, length us, event | category | flops | bytes accessed | tf_op | source)
XLA Modules:
  0.0 113.2 jit_solution(1187271491770006555)
XLA Ops:
  0.6 1.1 copy-done.2
  1.8 1.0 copy-done.4
  2.8 0.9 copy-done.5
  3.8 0.7 copy-done.7
  4.5 4.7 %space_attention.1 = f32[16,2,16,256]{3,2,1,0:T(8,128)S(1)} custom-call(f32[2,256,256]{2,1,0:T(8,128)S(1)} %bitcast.17, f32[1,256]{1,0:T(1,128)S(1)} %bitcast.18, f32[256,768]{1,0:T(8,128)S(1)} %copy-done.2, f32[256,256]{1,0:T(8,128)S(1)} %copy-done.5), custom_call_target="tpu_custom_call" | custom-call | flops 8000000000 | bytes 1310720 | tf_op jit(solution)/shard_map/space_attention/pallas_call | solution.py:229
  9.2 21.7 %all_to_all.5 = f32[16,2,16,256]{3,2,1,0:T(8,128)S(1)} all-to-all(f32[16,2,16,256]{3,2,1,0:T(8,128)S(1)} %space_attention.1), channel_id=1, replica_groups=mesh['groups'=2,'frames'=16] {'frames'}, dimensions={0} | all-to-all | bytes 1048576 | tf_op jit(solution)/shard_map/all_to_all | solution.py:245
  30.9 6.1 %time_attention.1 = (f32[2,16,16,256]{3,2,1,0:T(8,128)}, f32[512,256]{1,0:T(8,128)S(1)}) custom-call(s32[2]{0:T(128)S(1)} %copy-done.9, f32[16,2,1,16,256]{4,3,2,1,0:T(8,128)S(1)} %bitcast.14, f32[1,256]{1,0:T(1,128)S(1)} %bitcast.19, f32[256,768]{1,0:T(8,128)S(1)} %copy-done.3, f32[256,256]{1,0:T(8,128)S(1)} %copy-done.6), custom_call_target="tpu_custom_call" | custom-call | flops 8000000000 | bytes 1310720 | tf_op jit(solution)/shard_map/time_attention/pallas_call | solution.py:248
  37.0 0.4 collective-permute-start.4
  37.4 0.5 collective-permute-start.3
  37.9 13.0 %collective-permute-done.4.refs_4_ = f32[512,256]{1,0:T(8,128)S(1)} collective-permute-done((f32[512,256]{1,0:T(8,128)S(1)}, f32[512,256]{1,0:T(8,128)S(1)}, u32[]{:S(2)}, u32[]{:S(2)}) %collective-permute-start.4) | collective-permute-done | bytes 524320 | tf_op jit(solution)/shard_map/ppermute | solution.py:202
  50.9 0.2 unit_codes.1.refs_0_
  51.1 2.0 %collective-permute-start.2 = (f32[256,256]{1,0:T(8,128)S(1)}, f32[256,256]{1,0:T(8,128)S(1)}, u32[]{:S(2)}, u32[]{:S(2)}) collective-permute-start(f32[256,256]{1,0:T(8,128)S(1)} %unit_codes.1.refs_0_), channel_id=1, source_target_pairs={{0,12},{1,13},{2,14},{3,15},{4,8},{5,9},{6,10},{7,11},{8,4},{9,5},... | collective-permute-start | bytes 786440 | tf_op jit(solution)/shard_map/ppermute | solution.py:202
  53.1 1.3 %collective-permute-start.1 = (f32[256,256]{1,0:T(8,128)S(1)}, f32[256,256]{1,0:T(8,128)S(1)}, u32[]{:S(2)}, u32[]{:S(2)}) collective-permute-start(f32[256,256]{1,0:T(8,128)S(1)} %unit_codes.1.refs_0_), channel_id=1, source_target_pairs={{0,8},{1,9},{2,10},{3,11},{4,12},{5,13},{6,14},{7,15},{8,0},{9,1},... | collective-permute-start | bytes 786440 | tf_op jit(solution)/shard_map/ppermute | solution.py:202
  54.3 1.2 %collective-permute-start = (f32[256,256]{1,0:T(8,128)S(1)}, f32[256,256]{1,0:T(8,128)S(1)}, u32[]{:S(2)}, u32[]{:S(2)}) collective-permute-start(f32[256,256]{1,0:T(8,128)S(1)} %unit_codes.1.refs_0_), channel_id=1, source_target_pairs={{0,4},{1,5},{2,6},{3,7},{4,0},{5,1},{6,2},{7,3},{8,12},{9,13},{10,... | collective-permute-start | bytes 786440 | tf_op jit(solution)/shard_map/ppermute | solution.py:202
  55.5 6.7 %collective-permute-done.2.refs_3_ = f32[256,256]{1,0:T(8,128)S(1)} collective-permute-done((f32[256,256]{1,0:T(8,128)S(1)}, f32[256,256]{1,0:T(8,128)S(1)}, u32[]{:S(2)}, u32[]{:S(2)}) %collective-permute-start.2) | collective-permute-done | bytes 262176 | tf_op jit(solution)/shard_map/ppermute | solution.py:202
  62.2 15.7 %collective-permute-done.1.refs_2_ = f32[256,256]{1,0:T(8,128)S(1)} collective-permute-done((f32[256,256]{1,0:T(8,128)S(1)}, f32[256,256]{1,0:T(8,128)S(1)}, u32[]{:S(2)}, u32[]{:S(2)}) %collective-permute-start.1) | collective-permute-done | bytes 262176 | tf_op jit(solution)/shard_map/ppermute | solution.py:202
  77.9 1.3 %scores.2 = (bf16[2,1024,512]{2,1,0:T(8,128)(2,1)S(1)}, f32[2,1,512]{2,1,0:T(1,128)S(1)}) custom-call(f32[256,256]{1,0:T(8,128)S(1)} %unit_codes.1.refs_0_, f32[256,256]{1,0:T(8,128)S(1)} %collective-permute-done.refs_1_, f32[256,256]{1,0:T(8,128)S(1)} %collective-permute-done.1.refs_2_, f32[256,256]{1,0:T(8,128)S(1)} %collective-permute-done.2.refs_3_, ...), custom_call_target="tpu_custom_call" | custom-call | flops 1073741824 | bytes 4198400 | tf_op jit(solution)/shard_map/scores/pallas_call | solution.py:189
  79.2 0.3 collective-permute-start.10
  79.6 1.1 collective-permute-start.8
  80.7 0.5 collective-permute-start.6
  81.2 1.3 %scores.3 = (bf16[2,1024,512]{2,1,0:T(8,128)(2,1)S(1)}, f32[2,1,512]{2,1,0:T(1,128)S(1)}) custom-call(f32[256,256]{1,0:T(8,128)S(1)} %unit_codes.1.refs_0_, f32[256,256]{1,0:T(8,128)S(1)} %collective-permute-done.refs_1_, f32[256,256]{1,0:T(8,128)S(1)} %collective-permute-done.1.refs_2_, f32[256,256]{1,0:T(8,128)S(1)} %collective-permute-done.2.refs_3_, ...), custom_call_target="tpu_custom_call" | custom-call | flops 1073741824 | bytes 4198400 | tf_op jit(solution)/shard_map/scores/pallas_call | solution.py:189
  82.5 0.6 collective-permute-start.11
  83.1 1.1 collective-permute-start.9
  84.2 0.2 collective-permute-start.7
  84.4 1.2 %collective-permute-done.11.refs_13_ = f32[2,1,512]{2,1,0:T(1,128)S(1)} collective-permute-done((f32[2,1,512]{2,1,0:T(1,128)S(1)}, f32[2,1,512]{2,1,0:T(1,128)S(1)}, u32[]{:S(2)}, u32[]{:S(2)}) %collective-permute-start.11) | collective-permute-done | bytes 4128 | tf_op jit(solution)/shard_map/ppermute | solution.py:202
  85.6 1.1 collective-permute-done.9.refs_11_
  86.7 2.4 %terms.1 = f32[4,264,256]{2,1,0:T(8,128)S(1)} custom-call(bf16[2,1024,512]{2,1,0:T(8,128)(2,1)S(1)} %get-tuple-element.15.refs_0_, bf16[2,1024,512]{2,1,0:T(8,128)(2,1)S(1)} %get-tuple-element.16.refs_1_, f32[512,256]{1,0:T(8,128)S(1)} %get-tuple-element.14.refs_4_.refs_2_, f32[512,256]{1,0:T(8,128)S(1)} %collective-permute-done.3.refs_5_.refs_3_, ...), custom_call_target="tpu_custom_call" | custom-call | flops 1073741824 | bytes 7405568 | tf_op jit(solution)/shard_map/terms/pallas_call | solution.py:189
  89.2 1.5 %collective-permute-start.14 = (f32[264,256]{1,0:T(8,128)S(1)}, f32[264,256]{1,0:T(8,128)S(1)}, u32[]{:S(2)}, u32[]{:S(2)}) collective-permute-start(f32[264,256]{1,0:T(8,128)S(1)} %get-tuple-element.22), channel_id=1, source_target_pairs={{0,12},{1,13},{2,14},{3,15},{4,8},{5,9},{6,10},{7,11},{8,4},{9,5},... | collective-permute-start | bytes 811016 | tf_op jit(solution)/shard_map/ppermute | solution.py:202
  90.7 3.0 %collective-permute-start.12 = (f32[264,256]{1,0:T(8,128)S(1)}, f32[264,256]{1,0:T(8,128)S(1)}, u32[]{:S(2)}, u32[]{:S(2)}) collective-permute-start(f32[264,256]{1,0:T(8,128)S(1)} %get-tuple-element.24), channel_id=1, source_target_pairs={{0,4},{1,5},{2,6},{3,7},{4,0},{5,1},{6,2},{7,3},{8,12},{9,13},{10,... | collective-permute-start | bytes 811016 | tf_op jit(solution)/shard_map/ppermute | solution.py:202
  93.7 6.9 %collective-permute-done.14.refs_5_ = f32[264,256]{1,0:T(8,128)S(1)} collective-permute-done((f32[264,256]{1,0:T(8,128)S(1)}, f32[264,256]{1,0:T(8,128)S(1)}, u32[]{:S(2)}, u32[]{:S(2)}) %collective-permute-start.14) | collective-permute-done | bytes 270368 | tf_op jit(solution)/shard_map/ppermute | solution.py:202
  100.6 11.7 %collective-permute-done.13.refs_4_ = f32[264,256]{1,0:T(8,128)S(1)} collective-permute-done((f32[264,256]{1,0:T(8,128)S(1)}, f32[264,256]{1,0:T(8,128)S(1)}, u32[]{:S(2)}, u32[]{:S(2)}) %collective-permute-start.13) | collective-permute-done | bytes 270368 | tf_op jit(solution)/shard_map/ppermute | solution.py:202
  112.3 0.9 update.1
  (27 shorter events, 0.1 us)
Async XLA Ops:
  0.6 1.1 %copy-start.2 = (f32[256,768]{1,0:T(8,128)S(1)}, f32[256,768]{1,0:T(8,128)}, u32[]{:S(2)}) copy-start(f32[256,768]{1,0:T(8,128)} %w_qkv_ref.2) | copy-start | bytes 2359300
  1.8 1.0 copy-start.4
  2.8 0.9 copy-start.5
  3.8 0.7 copy-start.7
  4.4 26.4 %copy-start.3 = (f32[256,768]{1,0:T(8,128)S(1)}, f32[256,768]{1,0:T(8,128)}, u32[]{:S(2)}) copy-start(f32[256,768]{1,0:T(8,128)} %w_qkv_ref.3) | copy-start | bytes 2359300
  4.4 26.4 %copy-start.6 = (f32[256,256]{1,0:T(8,128)S(1)}, f32[256,256]{1,0:T(8,128)}, u32[]{:S(2)}) copy-start(f32[256,256]{1,0:T(8,128)} %w_out_ref.3) | copy-start | bytes 786436
  4.4 26.4 %copy-start.8 = (f32[256]{0:T(256)S(1)}, f32[256]{0:T(256)}, u32[]{:S(2)}) copy-start(f32[256]{0:T(256)} %param.15) | copy-start | bytes 3076
  4.4 26.4 %copy-start.9 = (s32[2]{0:T(128)S(1)}, s32[2]{0:T(128)}, u32[]{:S(2)}) copy-start(s32[2]{0:T(128)} %start_ref.1) | copy-start | bytes 28
  30.9 20.0 %copy-start = (f32[256,256]{1,0:T(8,128)S(1)}, f32[256,256]{1,0:T(8,128)}, u32[]{:S(2)}) copy-start(f32[256,256]{1,0:T(8,128)} %refs_0_.1) | copy-start | bytes 786436
  30.9 20.0 %copy-start.1 = (f32[256]{0:T(256)S(1)}, f32[256]{0:T(256)}, u32[]{:S(2)}) copy-start(f32[256]{0:T(256)} %param.19) | copy-start | bytes 3076
  37.0 13.8 %collective-permute-start.4 = (f32[512,256]{1,0:T(8,128)S(1)}, f32[512,256]{1,0:T(8,128)S(1)}, u32[]{:S(2)}, u32[]{:S(2)}) collective-permute-start(f32[512,256]{1,0:T(8,128)S(1)} %get-tuple-element.14.refs_4_.refs_2_), channel_id=1, source_target_pairs={{0,2},{1,3},{2,0},{3,1},{4,6},{5,7},{6,4},{7,5},{8,10},{9,11},{10,... | collective-permute-start | bytes 1572872 | tf_op jit(solution)/shard_map/ppermute | solution.py:202
  37.4 40.5 %collective-permute-start.3 = (f32[512,256]{1,0:T(8,128)S(1)}, f32[512,256]{1,0:T(8,128)S(1)}, u32[]{:S(2)}, u32[]{:S(2)}) collective-permute-start(f32[512,256]{1,0:T(8,128)S(1)} %get-tuple-element.14.refs_4_.refs_2_), channel_id=1, source_target_pairs={{0,1},{1,0},{2,3},{3,2},{4,5},{5,4},{6,7},{7,6},{8,9},{9,8},{10,11... | collective-permute-start | bytes 1572872 | tf_op jit(solution)/shard_map/ppermute | solution.py:202
  50.9 30.3 %collective-permute-start.5 = (f32[512,256]{1,0:T(8,128)S(1)}, f32[512,256]{1,0:T(8,128)S(1)}, u32[]{:S(2)}, u32[]{:S(2)}) collective-permute-start(f32[512,256]{1,0:T(8,128)S(1)} %collective-permute-done.4.refs_4_), channel_id=1, source_target_pairs={{0,1},{1,0},{2,3},{3,2},{4,5},{5,4},{6,7},{7,6},{8,9},{9,8},{10,11... | collective-permute-start | bytes 1572872 | tf_op jit(solution)/shard_map/ppermute | solution.py:202
  51.1 11.1 %collective-permute-start.2 = (f32[256,256]{1,0:T(8,128)S(1)}, f32[256,256]{1,0:T(8,128)S(1)}, u32[]{:S(2)}, u32[]{:S(2)}) collective-permute-start(f32[256,256]{1,0:T(8,128)S(1)} %unit_codes.1.refs_0_), channel_id=1, source_target_pairs={{0,12},{1,13},{2,14},{3,15},{4,8},{5,9},{6,10},{7,11},{8,4},{9,5},... | collective-permute-start | bytes 786440 | tf_op jit(solution)/shard_map/ppermute | solution.py:202
  53.1 24.8 %collective-permute-start.1 = (f32[256,256]{1,0:T(8,128)S(1)}, f32[256,256]{1,0:T(8,128)S(1)}, u32[]{:S(2)}, u32[]{:S(2)}) collective-permute-start(f32[256,256]{1,0:T(8,128)S(1)} %unit_codes.1.refs_0_), channel_id=1, source_target_pairs={{0,8},{1,9},{2,10},{3,11},{4,12},{5,13},{6,14},{7,15},{8,0},{9,1},... | collective-permute-start | bytes 786440 | tf_op jit(solution)/shard_map/ppermute | solution.py:202
  54.3 23.5 %collective-permute-start = (f32[256,256]{1,0:T(8,128)S(1)}, f32[256,256]{1,0:T(8,128)S(1)}, u32[]{:S(2)}, u32[]{:S(2)}) collective-permute-start(f32[256,256]{1,0:T(8,128)S(1)} %unit_codes.1.refs_0_), channel_id=1, source_target_pairs={{0,4},{1,5},{2,6},{3,7},{4,0},{5,1},{6,2},{7,3},{8,12},{9,13},{10,... | collective-permute-start | bytes 786440 | tf_op jit(solution)/shard_map/ppermute | solution.py:202
  79.2 5.0 %collective-permute-start.10 = (f32[2,1,512]{2,1,0:T(1,128)S(1)}, f32[2,1,512]{2,1,0:T(1,128)S(1)}, u32[]{:S(2)}, u32[]{:S(2)}) collective-permute-start(f32[2,1,512]{2,1,0:T(1,128)S(1)} %get-tuple-element.17.refs_6_), channel_id=1, source_target_pairs={{0,3},{1,2},{2,1},{3,0},{4,7},{5,6},{6,5},{7,4},{8,11},{9,10},{10,... | collective-permute-start | bytes 12296 | tf_op jit(solution)/shard_map/ppermute | solution.py:202
  79.6 4.9 %collective-permute-start.8 = (f32[2,1,512]{2,1,0:T(1,128)S(1)}, f32[2,1,512]{2,1,0:T(1,128)S(1)}, u32[]{:S(2)}, u32[]{:S(2)}) collective-permute-start(f32[2,1,512]{2,1,0:T(1,128)S(1)} %get-tuple-element.17.refs_6_), channel_id=1, source_target_pairs={{0,2},{1,3},{2,0},{3,1},{4,6},{5,7},{6,4},{7,5},{8,10},{9,11},{10,... | collective-permute-start | bytes 12296 | tf_op jit(solution)/shard_map/ppermute | solution.py:202
  80.7 3.8 %collective-permute-start.6 = (f32[2,1,512]{2,1,0:T(1,128)S(1)}, f32[2,1,512]{2,1,0:T(1,128)S(1)}, u32[]{:S(2)}, u32[]{:S(2)}) collective-permute-start(f32[2,1,512]{2,1,0:T(1,128)S(1)} %get-tuple-element.17.refs_6_), channel_id=1, source_target_pairs={{0,1},{1,0},{2,3},{3,2},{4,5},{5,4},{6,7},{7,6},{8,9},{9,8},{10,11... | collective-permute-start | bytes 12296 | tf_op jit(solution)/shard_map/ppermute | solution.py:202
  82.5 3.1 %collective-permute-start.11 = (f32[2,1,512]{2,1,0:T(1,128)S(1)}, f32[2,1,512]{2,1,0:T(1,128)S(1)}, u32[]{:S(2)}, u32[]{:S(2)}) collective-permute-start(f32[2,1,512]{2,1,0:T(1,128)S(1)} %get-tuple-element.18.refs_7_), channel_id=1, source_target_pairs={{0,3},{1,2},{2,1},{3,0},{4,7},{5,6},{6,5},{7,4},{8,11},{9,10},{10,... | collective-permute-start | bytes 12296 | tf_op jit(solution)/shard_map/ppermute | solution.py:202
  83.1 3.6 %collective-permute-start.9 = (f32[2,1,512]{2,1,0:T(1,128)S(1)}, f32[2,1,512]{2,1,0:T(1,128)S(1)}, u32[]{:S(2)}, u32[]{:S(2)}) collective-permute-start(f32[2,1,512]{2,1,0:T(1,128)S(1)} %get-tuple-element.18.refs_7_), channel_id=1, source_target_pairs={{0,2},{1,3},{2,0},{3,1},{4,6},{5,7},{6,4},{7,5},{8,10},{9,11},{10,... | collective-permute-start | bytes 12296 | tf_op jit(solution)/shard_map/ppermute | solution.py:202
  84.2 2.5 %collective-permute-start.7 = (f32[2,1,512]{2,1,0:T(1,128)S(1)}, f32[2,1,512]{2,1,0:T(1,128)S(1)}, u32[]{:S(2)}, u32[]{:S(2)}) collective-permute-start(f32[2,1,512]{2,1,0:T(1,128)S(1)} %get-tuple-element.18.refs_7_), channel_id=1, source_target_pairs={{0,1},{1,0},{2,3},{3,2},{4,5},{5,4},{6,7},{7,6},{8,9},{9,8},{10,11... | collective-permute-start | bytes 12296 | tf_op jit(solution)/shard_map/ppermute | solution.py:202
  89.2 11.4 %collective-permute-start.14 = (f32[264,256]{1,0:T(8,128)S(1)}, f32[264,256]{1,0:T(8,128)S(1)}, u32[]{:S(2)}, u32[]{:S(2)}) collective-permute-start(f32[264,256]{1,0:T(8,128)S(1)} %get-tuple-element.22), channel_id=1, source_target_pairs={{0,12},{1,13},{2,14},{3,15},{4,8},{5,9},{6,10},{7,11},{8,4},{9,5},... | collective-permute-start | bytes 811016 | tf_op jit(solution)/shard_map/ppermute | solution.py:202
  90.7 21.6 %collective-permute-start.13 = (f32[264,256]{1,0:T(8,128)S(1)}, f32[264,256]{1,0:T(8,128)S(1)}, u32[]{:S(2)}, u32[]{:S(2)}) collective-permute-start(f32[264,256]{1,0:T(8,128)S(1)} %get-tuple-element.23), channel_id=1, source_target_pairs={{0,8},{1,9},{2,10},{3,11},{4,12},{5,13},{6,14},{7,15},{8,0},{9,1},... | collective-permute-start | bytes 811016 | tf_op jit(solution)/shard_map/ppermute | solution.py:202
  90.7 21.6 %collective-permute-start.12 = (f32[264,256]{1,0:T(8,128)S(1)}, f32[264,256]{1,0:T(8,128)S(1)}, u32[]{:S(2)}, u32[]{:S(2)}) collective-permute-start(f32[264,256]{1,0:T(8,128)S(1)} %get-tuple-element.24), channel_id=1, source_target_pairs={{0,4},{1,5},{2,6},{3,7},{4,0},{5,1},{6,2},{7,3},{8,12},{9,13},{10,... | collective-permute-start | bytes 811016 | tf_op jit(solution)/shard_map/ppermute | solution.py:202

commit v2 on v1

v2 whole, which is shorter than its diff:
```python
import math

import jax
import jax.numpy as jnp
from jax import lax
from jax.experimental import pallas as pl
from jax.experimental.pallas import tpu as pltpu
from jax.sharding import PartitionSpec as P

HEADS = 4
ATTN_SCALE = 10.0
SOFTMAX_WARMTH = 0.05
DECAY_RATE = 0.9
EPSILON = 1e-06
SHARERS = 4
VMEM_BYTES = 40 * 1024 * 1024
FIRST_VMEM_BYTES = 62 * 1024 * 1024
BF16 = jnp.bfloat16
F32 = jnp.float32


def params(limit=VMEM_BYTES):
    return pltpu.CompilerParams(vmem_limit_bytes=limit)


def split(x):
    high = x.astype(BF16)
    return high, (x - high.astype(F32)).astype(BF16)


def dot(a, b):
    return jnp.dot(a, b, preferred_element_type=F32)


def dot_t(a, b):
    return lax.dot_general(a, b, (((1,), (1,)), ((), ())), preferred_element_type=F32)


def dot3(a, b, product=dot):
    ah, al = a
    bh, bl = b
    return product(ah, bh) + (product(al, bh) + product(ah, bl))


def attend(x, gain, w_qkv, w_out, mask):
    tokens, width = x.shape
    head = width // HEADS
    h = x * lax.rsqrt(jnp.mean(x * x, -1, keepdims=True) + EPSILON) * gain
    packed = dot3(split(h), split(w_qkv))
    row_head = lax.broadcasted_iota(jnp.int32, (width, width), 0) // head
    lane_head = lax.broadcasted_iota(jnp.int32, (width, width), 1) // head
    same_head = (row_head == lane_head).astype(BF16)

    def unit_heads(v):
        high, low = split(v * v)
        return v * lax.rsqrt(dot(high, same_head) + dot(low, same_head) + EPSILON)

    q = split(unit_heads(packed[:, :width]) * ATTN_SCALE)
    k = split(unit_heads(packed[:, width : 2 * width]))
    v = split(packed[:, 2 * width :])
    lanes = lax.broadcasted_iota(jnp.int32, (tokens, width), 1) // head
    mixed = jnp.zeros((tokens, width), F32)
    for i in range(HEADS):
        mine = lanes == i
        qi = [jnp.where(mine, part, jnp.zeros_like(part)) for part in q]
        weights = jnp.exp(dot3(qi, k, dot_t))
        if mask is not None:
            weights = jnp.where(mask, weights, 0.0)
        vi = [jnp.where(mine, part, jnp.full_like(part, fill)) for part, fill in zip(v, (1.0, 0.0))]
        r = dot3(split(weights), vi)
        totals = jnp.concatenate([r[:, width // 2 :], r[:, : width // 2]], axis=1)
        mixed = jnp.where(mine, r / totals, mixed)
    return x + dot3(split(mixed), split(w_out))


def space_kernel(me_ref, x_ref, gain_ref, w_qkv_ref, w_out_ref, *rest):
    *out_refs, by_device = rest
    for f in range(x_ref.shape[0]):
        y = attend(x_ref[f], gain_ref[...], w_qkv_ref[...], w_out_ref[...], None)
        by_device[...] = y.reshape(by_device.shape)
        for r, out_ref in enumerate(out_refs):
            for m in range(SHARERS):
                out_ref[m, f] = by_device[me_ref[0] ^ (m + SHARERS * r)]


def first_kernel(me_ref, video, gain, w_qkv, w_out, sums, counts, codes_ref, *rest, blocks):
    out_refs, refs, (by_device, sem) = rest[:blocks], rest[blocks:-2], rest[-2:]
    sources = (sums, counts, video.at[0], gain, w_qkv, w_out)
    copies = [pltpu.make_async_copy(a, b, sem.at[i]) for i, (a, b) in enumerate(zip(sources, refs))]
    for copy in copies:
        copy.start()
    for copy in copies[:2]:
        copy.wait()
    sums, counts, x, gain, w_qkv, w_out = refs
    code_kernel(sums, counts, codes_ref)
    for copy in copies[2:]:
        copy.wait()
    space_kernel(me_ref, x, gain, w_qkv, w_out, *out_refs, by_device)


def merge_kernel(*refs, blocks):
    arrived, out_refs = refs[:blocks], refs[blocks:]
    for m, out_ref in enumerate(out_refs):
        for r in range(blocks):
            out_ref[r] = arrived[r][m]


def time_kernel(me_ref, start_ref, gain_ref, w_qkv_ref, w_out_ref, *rest, clip):
    x_refs, (latents_ref, unit_ref) = rest[:SHARERS], rest[-2:]
    blocks, local_frames, places, width = x_refs[0].shape
    group = blocks * local_frames * places
    tokens = SHARERS * group
    x = jnp.concatenate([ref[...].reshape(group, width) for ref in x_refs], axis=0)
    me, start = me_ref[0], start_ref[clip]

    def place_and_frame(index):
        slot = index // places
        place, frame, slot = index - slot * places, slot % local_frames, slot // local_frames
        sender = (slot // blocks + SHARERS * (slot % blocks)) ^ me
        return place, sender * local_frames + frame

    place, later = place_and_frame(lax.broadcasted_iota(jnp.int32, (tokens, 1), 0))
    other, earlier = place_and_frame(lax.broadcasted_iota(jnp.int32, (1, tokens), 1))
    mask = (place == other) & ((earlier == later) | ((earlier < later) & (earlier >= start)))
    y = attend(x, gain_ref[...], w_qkv_ref[...], w_out_ref[...], mask)
    unit_ref[...] = y * lax.rsqrt(jnp.sum(y * y, -1, keepdims=True) + EPSILON)
    for slot in range(SHARERS * blocks):
        sender = (slot // blocks + SHARERS * (slot % blocks)) ^ me
        for f in range(local_frames):
            row = (slot * local_frames + f) * places
            latents_ref[0, sender * local_frames + f] = y[row : row + places]


def column(row, lanes):
    return jnp.transpose(jnp.broadcast_to(row, (lanes, row.shape[1])))


def code_kernel(sums_ref, counts_ref, out_ref):
    book = sums_ref[...] / column(counts_ref[...], sums_ref.shape[1])
    unit = book * lax.rsqrt(jnp.sum(book * book, -1, keepdims=True) + EPSILON)
    out_ref[...] = unit * (math.log2(math.e) / SOFTMAX_WARMTH)


def score_kernel(*refs, blocks, chunks, before):
    codes, units = refs[:blocks], refs[blocks : blocks + chunks]
    w_ref, totals_ref = refs[-2:]
    rows = codes[0].shape[0]
    if before:
        totals_ref[:before] = refs[blocks + chunks][...]
    for j in range(chunks):
        u = units[j][...].astype(BF16)
        totals = None
        for r in range(blocks):
            high, low = split(codes[r][...])
            w = jnp.exp2(dot_t(high, u) + dot_t(low, u)).astype(BF16)
            w_ref[j, r * rows : (r + 1) * rows, :] = w
            part = jnp.sum(w.astype(F32), 0, keepdims=True)
            totals = part if totals is None else totals + part
        totals_ref[before + j] = totals


def term_kernel(*refs, blocks, clips):
    each = 2 + 2 * SHARERS
    out_refs = refs[each * clips :]
    width = refs[2].shape[1]
    rows = refs[0].shape[1] // blocks
    scaled, shares, ws = [], [], []
    for c in range(clips):
        near, far = refs[each * c : each * c + 2]
        units = refs[each * c + 2 : each * c + 2 + SHARERS]
        totals = refs[each * c + 2 + SHARERS : each * (c + 1)]
        for j in range(SHARERS):
            total = totals[0][j]
            for m in range(1, SHARERS):
                total = total + totals[m][j ^ m]
            share = 1.0 / total
            column_share = jnp.concatenate([column(share, 128)] * (width // 128), axis=1)
            scaled.append((units[j][...] * column_share).astype(BF16))
            high, low = split(share)
            index = lax.broadcasted_iota(jnp.int32, (16, share.shape[1]), 0)
            pair = jnp.where(index == 0, high.astype(F32), jnp.where(index == 1, low.astype(F32), 0.0))
            shares.append(pair.astype(BF16))
            ws.append((near, far)[j // 2].at[j % 2])
    for r in reversed(range(blocks)):
        pieces = out_refs[:1] if r == 0 else out_refs[1:2] if r == 1 else out_refs[2 * r - 2 : 2 * r]
        sums = jnp.zeros((rows, width), F32)
        counts = jnp.zeros((16, rows), F32)
        for w_ref, unit, share in zip(ws, scaled, shares):
            w = w_ref[r * rows : (r + 1) * rows, :]
            sums = sums + dot(w, unit)
            counts = counts + dot_t(share, w)
        counts = jnp.sum(counts, 0, keepdims=True)
        if rows < width:
            counts = jnp.concatenate([counts, jnp.zeros((1, width - rows), F32)], axis=1)
        term = jnp.concatenate([sums, jnp.broadcast_to(counts, (8, width))], axis=0)
        row = 0
        for piece in pieces:
            piece[...] = term[row : row + piece.shape[0]]
            row += piece.shape[0]


def update_kernel(*refs, arrivals):
    sums_ref, counts_ref = refs[:2]
    new_sums_ref, new_counts_ref, new_book_ref = refs[-3:]
    rows, width = sums_ref.shape
    refs, term = refs[2:-3], None
    for pieces in arrivals:
        part = jnp.concatenate([ref[...] for ref in refs[:pieces]], axis=0)
        refs = refs[pieces:]
        term = part if term is None else term + part
    sums = DECAY_RATE * sums_ref[...] + (1.0 - DECAY_RATE) * term[:rows]
    counts = DECAY_RATE * counts_ref[...] + (1.0 - DECAY_RATE) * term[rows : rows + 1, :rows]
    new_sums_ref[...] = sums
    new_counts_ref[...] = counts
    new_book_ref[...] = sums / column(counts, width)


def whole(a):
    return pl.BlockSpec(a.shape, lambda *_: (0,) * a.ndim)


def cost(flops, *arrays):
    return pl.CostEstimate(
        flops=int(flops), bytes_accessed=int(sum(a.size * a.dtype.itemsize for a in arrays)), transcendentals=0
    )


def shape(*dims, dtype=F32):
    return jax.ShapeDtypeStruct(dims, dtype)


def simple_call(kernel, outs, *args, flops=0, name=None):
    return pl.pallas_call(
        kernel,
        out_shape=outs,
        compiler_params=params(),
        cost_estimate=cost(flops, *args, *(outs if isinstance(outs, (tuple, list)) else [outs])),
        name=name,
    )(*args)


def make_local(devices):
    sharers, blocks = SHARERS, devices // SHARERS

    def swap(x, bits):
        return lax.ppermute(x, "frames", [(i, i ^ bits) for i in range(devices)])

    def local(
        video,
        clip_start,
        gain_space,
        qkv_space,
        out_space,
        gain_time,
        qkv_time,
        out_time,
        code_sums,
        code_counts,
    ):
        clips, local_frames, all_places, width = video.shape
        places = all_places // devices
        frames = local_frames * devices
        code_rows = code_sums.shape[0]
        tokens = frames * places
        gain_space, gain_time = gain_space[None], gain_time[None]
        counts_row = code_counts[None]
        me = lax.axis_index("frames").astype(jnp.int32)[None]
        sent = [shape(sharers, local_frames, places, width)] * blocks
        by_device = pltpu.VMEM((devices, places, width), F32)

        hbm = pl.BlockSpec(memory_space=pltpu.HBM)
        smem = pl.BlockSpec(memory_space=pltpu.SMEM)
        operands = (video, gain_space, qkv_space, out_space, code_sums, counts_row)
        held = (code_sums, counts_row, video[0], gain_space, qkv_space, out_space)
        codes, *first = pl.pallas_call(
            lambda *refs: first_kernel(*refs, blocks=blocks),
            in_specs=[smem] + [hbm] * len(operands),
            out_shape=[shape(code_rows, width)] + sent,
            scratch_shapes=[pltpu.VMEM(a.shape, a.dtype) for a in held]
            + [by_device, pltpu.SemaphoreType.DMA((len(held),))],
            compiler_params=params(FIRST_VMEM_BYTES),
            cost_estimate=cost(2e9, *held),
            name="first_space",
        )(me, *operands)

        spaced = [first]
        for c in range(1, clips):
            spaced.append(
                pl.pallas_call(
                    space_kernel,
                    grid=(1,),
                    in_specs=[
                        smem,
                        pl.BlockSpec((None, local_frames, all_places, width), lambda i, c=c: (c, 0, 0, 0)),
                        whole(gain_space),
                        whole(qkv_space),
                        whole(out_space),
                    ],
                    out_specs=[whole(a) for a in sent],
                    out_shape=sent,
                    scratch_shapes=[by_device],
                    compiler_params=params(),
                    cost_estimate=cost(2e9, *held),
                    name="space_attention",
                )(me, video, gain_space, qkv_space, out_space)
            )

        by_sender = []
        for c in range(clips):
            arrived = [spaced[c][0]] + [swap(spaced[c][r], r * sharers) for r in range(1, blocks)]
            merged = simple_call(
                lambda *refs: merge_kernel(*refs, blocks=blocks),
                [shape(blocks, local_frames, places, width)] * sharers,
                *arrived,
                name="merge",
            )
            if c == clips - 1:
                codes, *merged = lax.optimization_barrier((codes, *merged))
            by_sender.append([merged[0]] + [swap(merged[m], m) for m in range(1, sharers)])

        code_blocks = {0: codes}
        for bit in reversed(range((blocks - 1).bit_length())):
            step = 1 << bit
            code_blocks |= {r ^ step: swap(block, step * sharers) for r, block in code_blocks.items()}
        code_blocks = [code_blocks[r] for r in range(blocks)]

        latents = None
        units = []
        for c in range(clips):
            before = [] if latents is None else [latents]
            latents, unit = pl.pallas_call(
                lambda *refs, c=c: time_kernel(*refs, clip=c),
                grid=(1,),
                in_specs=[smem, smem, whole(gain_time), whole(qkv_time), whole(out_time)]
                + [whole(a) for a in by_sender[c]]
                + [pl.BlockSpec(memory_space=pl.ANY)] * len(before),
                out_specs=(
                    pl.BlockSpec((1, frames, places, width), lambda i, c=c: (c, 0, 0, 0)),
                    pl.BlockSpec((tokens, width), lambda i: (0, 0)),
                ),
                out_shape=(shape(clips, frames, places, width), shape(tokens, width)),
                input_output_aliases={5 + sharers: 0} if before else {},
                compiler_params=params(),
                cost_estimate=cost(2e9, *held),
                name="time_attention",
            )(me, clip_start, gain_time, qkv_time, out_time, *by_sender[c], *before)

            if units:
                unit, units[-1][2] = lax.optimization_barrier((unit, units[-1][2]))
            far = swap(unit, 2)
            units.append([unit, swap(unit, 1), far, swap(far, 1)])

        def score(chunk_units, *before):
            n, m = len(chunk_units), len(before) * 2
            return simple_call(
                lambda *refs: score_kernel(*refs, blocks=blocks, chunks=n, before=m),
                (shape(n, blocks * code_rows, tokens, dtype=BF16), shape(m + n, 1, tokens)),
                *code_blocks,
                *chunk_units,
                *before,
                flops=n * 4 * blocks * code_rows * tokens * width,
                name="scores",
            )

        operands = []
        for c in range(clips):
            if c:
                units[c][2], clip_totals = lax.optimization_barrier((units[c][2], clip_totals))
            near_w, near_totals = score(units[c][:2])
            far_w, clip_totals = score(units[c][2:], near_totals)
            operands += [near_w, far_w, *units[c], clip_totals]
            operands += [swap(clip_totals, m) for m in range(1, sharers)]

        half = code_rows // 2
        one, two = [shape(code_rows + 8, width)], [shape(half, width), shape(code_rows + 8 - half, width)]
        terms = simple_call(
            lambda *refs: term_kernel(*refs, blocks=blocks, clips=clips),
            one * 2 + two * (blocks - 2),
            *operands,
            flops=2 * sharers * blocks * code_rows * clips * tokens * width,
            name="terms",
        )
        terms = [[terms[0]], [terms[1]]] + [list(terms[2 * r - 2 : 2 * r]) for r in range(2, blocks)]

        arrivals = [terms[0]]
        for bit in range((blocks - 1).bit_length()):
            step = 1 << bit
            for r in reversed(range(step, blocks, 2 * step)):
                came = [swap(piece, step * sharers) for piece in terms[r]]
                if r == step:
                    arrivals.append(came)
                else:
                    terms[r - step] = [a + b for a, b in zip(terms[r - step], came)]
        new_sums, new_counts, new_codebook = simple_call(
            lambda *refs: update_kernel(*refs, arrivals=[len(pieces) for pieces in arrivals]),
            (shape(code_rows, width), shape(1, code_rows), shape(code_rows, width)),
            code_sums,
            counts_row,
            *[piece for pieces in arrivals for piece in pieces],
            name="update",
        )
        return (latents, new_sums, new_counts[0], new_codebook)

    return local


def solution(mesh):
    in_specs = (
        P("groups", "frames", None, None),
        P("groups"),
        P(),
        P(),
        P(),
        P(),
        P(),
        P(),
        P(("groups", "frames"), None),
        P(("groups", "frames")),
    )
    out_specs = (
        P("groups", None, "frames", None),
        P(("groups", "frames"), None),
        P(("groups", "frames")),
        P(("groups", "frames"), None),
    )
    local = make_local(mesh.shape["frames"])
    return jax.shard_map(local, mesh=mesh, in_specs=in_specs, out_specs=out_specs, check_vma=False)
```

time: 113 us -> 93.8 us (0.83)
  blocking collectives: 21.7 us -> 0 us
  starting transfers between devices: 13.6 us -> 27.2 us
  waiting for transfers between devices: 56.2 us -> 43 us
  Pallas kernels: 17 us -> 21 us
  local copies, waits for them, and re-layouts: 3.9 us -> 1.53 us
    all_to_all x1 -> x0, blocking collectives: 21.7 us -> none  [local(): lax.all_to_all(spaced, 'frames', split_axis=0, concat_axis=0, tiled=True)]
    ppermute x15 -> x32, starting transfers between devices: 13.6 us -> 27.2 us  [swap(): return lax.ppermute(x, 'frames', [(i, i ^ bits) for i in range(devices)])]
    ppermute x15 -> x32, waiting for transfers between devices: 56.2 us -> 43 us  [swap(): return lax.ppermute(x, 'frames', [(i, i ^ bits) for i in range(devices)])]
    pallas_call x2 -> x4, Pallas kernels: 10.8 us -> 14.2 us  [the longest x2 7.29 us: local(): pl.pallas_call(lambda *refs, c=c: time_kernel(*refs, clip=c), grid=(1,),...]
    unnamed x20 -> x24, local copies, waits for them, and re-layouts: 3.82 us -> 1.53 us
    pallas_call x5 -> x8, Pallas kernels: 6.2 us -> 6.8 us  [simple_call(): pl.pallas_call(kernel, out_shape=outs, compiler_params=params(), cost_est...]
  transfers between devices with their start and end apart: 15 -> 32, of which waited for: 7 -> 12; matrix products, arithmetic and copies ran while one was open for 0% -> 0% of each run, Pallas kernels for 3% -> 14%
where the time goes in v2:
time: 93.8 us; the launch traced here: 93.6 us
  waiting for transfers between devices  43 us (46%)
  starting transfers between devices  27.2 us (29%)
  Pallas kernels  21 us (22%)
  local copies, waits for them, and re-layouts  1.53 us (2%)
    ppermute x32, waiting for transfers between devices, swap(): return lax.ppermute(x, 'frames', [(i, i ^ bits) for i in range(devices)])  43 us
    ppermute x32, starting transfers between devices, swap(): return lax.ppermute(x, 'frames', [(i, i ^ bits) for i in range(devices)])  27.2 us
    pallas_call x2, Pallas kernels, local(): pl.pallas_call(lambda *refs, c=c: time_kernel(*refs, clip=c), grid=(1,),...  7.29 us
    pallas_call x8, Pallas kernels, simple_call(): pl.pallas_call(kernel, out_shape=outs, compiler_params=params(), cost_est...  6.8 us
    pallas_call x1, Pallas kernels, local(): pl.pallas_call(lambda *refs: first_kernel(*refs, blocks=blocks), in_specs...  4.56 us
    pallas_call x1, Pallas kernels, local(): pl.pallas_call(space_kernel, grid=(1,), in_specs=[smem, pl.BlockSpec((Non...  2.34 us
  transfers between devices with their start and end apart: 32, of which 12 were waited for; matrix products, arithmetic and copies ran while one was open for 0% of the time, Pallas kernels for 14%

profile of v2, /device:TPU:0, one launch (start us, length us, event | category | flops | bytes accessed | tf_op | source)
XLA Modules:
  0.0 93.6 jit_solution(12057789289170148520)
XLA Ops:
  0.7 4.6 %first_space.1 = (f32[256,256]{1,0:T(8,128)}, f32[4,1,16,256]{3,2,1,0:T(8,128)}, f32[4,1,16,256]{3,2,1,0:T(8,128)}, f32[4,1,16,256]{3,2,1,0:T(8,128)}, f32[4,1,16,256]{3,2,1,0:T(8,128)}) custom-call(s32[1]{0:T(128)} %bitcast.refs_0_.me_ref, f32[2,1,256,256]{3,2,1,0:T(8,128)} %x_ref.1, f32[1,256]{1,0:T(1,128)} %bitcast.7, f32[256,768]{1,0:T(8,128)} %w_qkv_ref.1, ...), custom_call_target="tpu_custom_call" | custom-call | flops 2000000000 | bytes 1574912 | tf_op jit(solution)/shard_map/first_space/pallas_call | solution.py:275
  5.2 3.1 %collective-permute-start.6 = (f32[4,1,16,256]{3,2,1,0:T(8,128)}, f32[4,1,16,256]{3,2,1,0:T(8,128)S(1)}, u32[]{:S(2)}, u32[]{:S(2)}) collective-permute-start(f32[4,1,16,256]{3,2,1,0:T(8,128)} %get-tuple-element.64), channel_id=1, source_target_pairs={{0,4},{1,5},{2,6},{3,7},{4,0},{5,1},{6,2},{7,3},{8,12},{9,13},{10,... | collective-permute-start | bytes 196616 | tf_op jit(solution)/shard_map/ppermute | solution.py:246
  8.3 2.6 %collective-permute-start.7 = (f32[4,1,16,256]{3,2,1,0:T(8,128)}, f32[4,1,16,256]{3,2,1,0:T(8,128)S(1)}, u32[]{:S(2)}, u32[]{:S(2)}) collective-permute-start(f32[4,1,16,256]{3,2,1,0:T(8,128)} %get-tuple-element.65), channel_id=1, source_target_pairs={{0,8},{1,9},{2,10},{3,11},{4,12},{5,13},{6,14},{7,15},{8,0},{9,1},... | collective-permute-start | bytes 196616 | tf_op jit(solution)/shard_map/ppermute | solution.py:246
  10.9 4.9 %collective-permute-done.7.refs_2_ = f32[4,1,16,256]{3,2,1,0:T(8,128)S(1)} collective-permute-done((f32[4,1,16,256]{3,2,1,0:T(8,128)}, f32[4,1,16,256]{3,2,1,0:T(8,128)S(1)}, u32[]{:S(2)}, u32[]{:S(2)}) %collective-permute-start.7) | collective-permute-done | bytes 65568 | tf_op jit(solution)/shard_map/ppermute | solution.py:246
  15.8 1.4 %collective-permute-done.8.refs_3_ = f32[4,1,16,256]{3,2,1,0:T(8,128)S(1)} collective-permute-done((f32[4,1,16,256]{3,2,1,0:T(8,128)}, f32[4,1,16,256]{3,2,1,0:T(8,128)S(1)}, u32[]{:S(2)}, u32[]{:S(2)}) %collective-permute-start.8) | collective-permute-done | bytes 65568 | tf_op jit(solution)/shard_map/ppermute | solution.py:246
  18.2 1.6 %collective-permute-start.10 = (f32[4,1,16,256]{3,2,1,0:T(8,128)S(1)}, f32[4,1,16,256]{3,2,1,0:T(8,128)S(1)}, u32[]{:S(2)}, u32[]{:S(2)}) collective-permute-start(f32[4,1,16,256]{3,2,1,0:T(8,128)S(1)} %get-tuple-element.69), channel_id=1, source_target_pairs={{0,2},{1,3},{2,0},{3,1},{4,6},{5,7},{6,4},{7,5},{8,10},{9,11},{10,... | collective-permute-start | bytes 196616 | tf_op jit(solution)/shard_map/ppermute | solution.py:246
  20.0 2.3 %space_attention.1 = (f32[4,1,16,256]{3,2,1,0:T(8,128)S(1)}, f32[4,1,16,256]{3,2,1,0:T(8,128)S(1)}, f32[4,1,16,256]{3,2,1,0:T(8,128)S(1)}, f32[4,1,16,256]{3,2,1,0:T(8,128)S(1)}) custom-call(s32[1]{0:T(128)} %bitcast.refs_0_.me_ref, f32[2,1,256,256]{3,2,1,0:T(8,128)S(1)} %copy-done.5, f32[1,256]{1,0:T(1,128)S(1)} %bitcast.8, f32[256,768]{1,0:T(8,128)S(1)} %copy-done.3, ...), custom_call_target="tpu_custom_call" | custom-call | flops 2000000000 | bytes 1574912 | tf_op jit(solution)/shard_map/space_attention/pallas_call | solution.py:289
  22.5 2.3 %collective-permute-start.1 = (f32[4,1,16,256]{3,2,1,0:T(8,128)S(1)}, f32[4,1,16,256]{3,2,1,0:T(8,128)S(1)}, u32[]{:S(2)}, u32[]{:S(2)}) collective-permute-start(f32[4,1,16,256]{3,2,1,0:T(8,128)S(1)} %get-tuple-element.53), channel_id=1, source_target_pairs={{0,8},{1,9},{2,10},{3,11},{4,12},{5,13},{6,14},{7,15},{8,0},{9,1},... | collective-permute-start | bytes 196616 | tf_op jit(solution)/shard_map/ppermute | solution.py:246
  24.8 2.0 %collective-permute-start.2 = (f32[4,1,16,256]{3,2,1,0:T(8,128)S(1)}, f32[4,1,16,256]{3,2,1,0:T(8,128)S(1)}, u32[]{:S(2)}, u32[]{:S(2)}) collective-permute-start(f32[4,1,16,256]{3,2,1,0:T(8,128)S(1)} %get-tuple-element.54), channel_id=1, source_target_pairs={{0,12},{1,13},{2,14},{3,15},{4,8},{5,9},{6,10},{7,11},{8,4},{9,5},... | collective-permute-start | bytes 196616 | tf_op jit(solution)/shard_map/ppermute | solution.py:246
  27.5 3.6 %time_attention.2 = (f32[2,16,16,256]{3,2,1,0:T(8,128)}, f32[256,256]{1,0:T(8,128)S(1)}) custom-call(s32[1]{0:T(128)} %bitcast.refs_0_.me_ref, s32[2]{0:T(128)S(1)} %copy-done.11, f32[1,256]{1,0:T(1,128)S(1)} %bitcast.9, f32[256,768]{1,0:T(8,128)S(1)} %copy-done.4, f32[256,256]{1,0:T(8,128)S(1)} %copy-done.7, ...), custom_call_target="tpu_custom_call" | custom-call | flops 2000000000 | bytes 1574912 | tf_op jit(solution)/shard_map/time_attention/pallas_call | solution.py:331
  31.2 1.5 %collective-permute-start.16 = (f32[256,256]{1,0:T(8,128)S(1)}, f32[256,256]{1,0:T(8,128)S(1)}, u32[]{:S(2)}, u32[]{:S(2)}) collective-permute-start(f32[256,256]{1,0:T(8,128)S(1)} %get-tuple-element.74.refs_4_.refs_2_), channel_id=1, source_target_pairs={{0,2},{1,3},{2,0},{3,1},{4,6},{5,7},{6,4},{7,5},{8,10},{9,11},{10,... | collective-permute-start | bytes 786440 | tf_op jit(solution)/shard_map/ppermute | solution.py:246
  33.4 1.3 %collective-permute-start.5 = (f32[4,1,16,256]{3,2,1,0:T(8,128)S(1)}, f32[4,1,16,256]{3,2,1,0:T(8,128)S(1)}, u32[]{:S(2)}, u32[]{:S(2)}) collective-permute-start(f32[4,1,16,256]{3,2,1,0:T(8,128)S(1)} %get-tuple-element.62), channel_id=1, source_target_pairs={{0,3},{1,2},{2,1},{3,0},{4,7},{5,6},{6,5},{7,4},{8,11},{9,10},{10,... | collective-permute-start | bytes 196616 | tf_op jit(solution)/shard_map/ppermute | solution.py:246
  34.7 1.0 %collective-permute-start.13 = (f32[256,256]{1,0:T(8,128)S(1)}, f32[256,256]{1,0:T(8,128)S(1)}, u32[]{:S(2)}, u32[]{:S(2)}) collective-permute-start(f32[256,256]{1,0:T(8,128)S(1)} %copy-done.8), channel_id=1, source_target_pairs={{0,8},{1,9},{2,10},{3,11},{4,12},{5,13},{6,14},{7,15},{8,0},{9,1},... | collective-permute-start | bytes 786440 | tf_op jit(solution)/shard_map/ppermute | solution.py:246
  35.7 1.3 %collective-permute-start.12 = (f32[256,256]{1,0:T(8,128)S(1)}, f32[256,256]{1,0:T(8,128)S(1)}, u32[]{:S(2)}, u32[]{:S(2)}) collective-permute-start(f32[256,256]{1,0:T(8,128)S(1)} %copy-done.8), channel_id=1, source_target_pairs={{0,4},{1,5},{2,6},{3,7},{4,0},{5,1},{6,2},{7,3},{8,12},{9,13},{10,... | collective-permute-start | bytes 786440 | tf_op jit(solution)/shard_map/ppermute | solution.py:246
  37.0 4.0 %collective-permute-done.4.refs_7_ = f32[4,1,16,256]{3,2,1,0:T(8,128)S(1)} collective-permute-done((f32[4,1,16,256]{3,2,1,0:T(8,128)S(1)}, f32[4,1,16,256]{3,2,1,0:T(8,128)S(1)}, u32[]{:S(2)}, u32[]{:S(2)}) %collective-permute-start.4) | collective-permute-done | bytes 65568 | tf_op jit(solution)/shard_map/ppermute | solution.py:246
  41.0 3.6 %time_attention.3 = (f32[2,16,16,256]{3,2,1,0:T(8,128)}, f32[256,256]{1,0:T(8,128)S(1)}) custom-call(s32[1]{0:T(128)} %bitcast.refs_0_.me_ref, s32[2]{0:T(128)S(1)} %copy-done.11, f32[1,256]{1,0:T(1,128)S(1)} %bitcast.10, f32[256,768]{1,0:T(8,128)S(1)} %copy-done.4, f32[256,256]{1,0:T(8,128)S(1)} %copy-done.7, ...), custom_call_target="tpu_custom_call", output_to_operand_aliasing={{0}: (9, {})} | custom-call | flops 2000000000 | bytes 1574912 | tf_op jit(solution)/shard_map/time_attention/pallas_call | solution.py:331
  44.7 1.5 %collective-permute-start.22 = (f32[256,256]{1,0:T(8,128)S(1)}, f32[256,256]{1,0:T(8,128)S(1)}, u32[]{:S(2)}, u32[]{:S(2)}) collective-permute-start(f32[256,256]{1,0:T(8,128)S(1)} %get-tuple-element.81.refs_4_.refs_12_), channel_id=1, source_target_pairs={{0,2},{1,3},{2,0},{3,1},{4,6},{5,7},{6,4},{7,5},{8,10},{9,11},{10,... | collective-permute-start | bytes 786440 | tf_op jit(solution)/shard_map/ppermute | solution.py:246
  46.7 2.5 %collective-permute-done.13.refs_2_ = f32[256,256]{1,0:T(8,128)S(1)} collective-permute-done((f32[256,256]{1,0:T(8,128)S(1)}, f32[256,256]{1,0:T(8,128)S(1)}, u32[]{:S(2)}, u32[]{:S(2)}) %collective-permute-start.13) | collective-permute-done | bytes 262176 | tf_op jit(solution)/shard_map/ppermute | solution.py:246
  49.7 4.0 %collective-permute-done.22.refs_4_.refs_14_ = f32[256,256]{1,0:T(8,128)S(1)} collective-permute-done((f32[256,256]{1,0:T(8,128)S(1)}, f32[256,256]{1,0:T(8,128)S(1)}, u32[]{:S(2)}, u32[]{:S(2)}) %collective-permute-start.22) | collective-permute-done | bytes 262176 | tf_op jit(solution)/shard_map/ppermute | solution.py:246
  53.7 3.7 %collective-permute-done.14.refs_3_ = f32[256,256]{1,0:T(8,128)S(1)} collective-permute-done((f32[256,256]{1,0:T(8,128)S(1)}, f32[256,256]{1,0:T(8,128)S(1)}, u32[]{:S(2)}, u32[]{:S(2)}) %collective-permute-start.14) | collective-permute-done | bytes 262176 | tf_op jit(solution)/shard_map/ppermute | solution.py:246
  59.1 0.9 %collective-permute-start.19 = (f32[4,1,256]{2,1,0:T(1,128)S(1)}, f32[4,1,256]{2,1,0:T(1,128)S(1)}, u32[]{:S(2)}, u32[]{:S(2)}) collective-permute-start(f32[4,1,256]{2,1,0:T(1,128)S(1)} %get-tuple-element.80.refs_6_), channel_id=1, source_target_pairs={{0,2},{1,3},{2,0},{3,1},{4,6},{5,7},{6,4},{7,5},{8,10},{9,11},{10,... | collective-permute-start | bytes 12296 | tf_op jit(solution)/shard_map/ppermute | solution.py:246
  60.0 0.9 collective-permute-start.18
  61.8 1.0 %scores.7 = (bf16[2,1024,256]{2,1,0:T(8,128)(2,1)S(1)}, f32[4,1,256]{2,1,0:T(1,128)S(1)}) custom-call(f32[256,256]{1,0:T(8,128)S(1)} %copy-done.8, f32[256,256]{1,0:T(8,128)S(1)} %collective-permute-done.12.refs_1_, f32[256,256]{1,0:T(8,128)S(1)} %collective-permute-done.13.refs_2_, f32[256,256]{1,0:T(8,128)S(1)} %collective-permute-done.14.refs_3_, ...), custom_call_target="tpu_custom_call" | custom-call | flops 536870912 | bytes 2627584 | tf_op jit(solution)/shard_map/scores/pallas_call | solution.py:233
  63.3 1.1 %collective-permute-start.25 = (f32[4,1,256]{2,1,0:T(1,128)S(1)}, f32[4,1,256]{2,1,0:T(1,128)S(1)}, u32[]{:S(2)}, u32[]{:S(2)}) collective-permute-start(f32[4,1,256]{2,1,0:T(1,128)S(1)} %get-tuple-element.86.refs_16_), channel_id=1, source_target_pairs={{0,2},{1,3},{2,0},{3,1},{4,6},{5,7},{6,4},{7,5},{8,10},{9,11},{10,... | collective-permute-start | bytes 12296 | tf_op jit(solution)/shard_map/ppermute | solution.py:246
  64.7 1.2 %collective-permute-done.26.refs_19_ = f32[4,1,256]{2,1,0:T(1,128)S(1)} collective-permute-done((f32[4,1,256]{2,1,0:T(1,128)S(1)}, f32[4,1,256]{2,1,0:T(1,128)S(1)}, u32[]{:S(2)}, u32[]{:S(2)}) %collective-permute-start.26) | collective-permute-done | bytes 4128 | tf_op jit(solution)/shard_map/ppermute | solution.py:246
  65.9 1.1 %collective-permute-done.25.refs_18_ = f32[4,1,256]{2,1,0:T(1,128)S(1)} collective-permute-done((f32[4,1,256]{2,1,0:T(1,128)S(1)}, f32[4,1,256]{2,1,0:T(1,128)S(1)}, u32[]{:S(2)}, u32[]{:S(2)}) %collective-permute-start.25) | collective-permute-done | bytes 4128 | tf_op jit(solution)/shard_map/ppermute | solution.py:246
  66.9 2.5 %terms.1 = (f32[264,256]{1,0:T(8,128)S(1)}, f32[264,256]{1,0:T(8,128)S(1)}, f32[128,256]{1,0:T(8,128)S(1)}, f32[136,256]{1,0:T(8,128)S(1)}, f32[128,256]{1,0:T(8,128)S(1)}, /*index=5*/f32[136,256]{1,0:T(8,128)S(1)}) custom-call(bf16[2,1024,256]{2,1,0:T(8,128)(2,1)S(1)} %get-tuple-element.75.refs_0_, bf16[2,1024,256]{2,1,0:T(8,128)(2,1)S(1)} %get-tuple-element.79.refs_1_, ...), custom_call_target="tpu_custom_call" | custom-call | flops 1073741824 | bytes 7405568 | tf_op jit(solution)/shard_map/terms/pallas_call | solution.py:233
  69.8 1.7 %collective-permute-start.27 = (f32[264,256]{1,0:T(8,128)S(1)}, f32[264,256]{1,0:T(8,128)S(1)}, u32[]{:S(2)}, u32[]{:S(2)}) collective-permute-start(f32[264,256]{1,0:T(8,128)S(1)} %get-tuple-element.88), channel_id=1, source_target_pairs={{0,4},{1,5},{2,6},{3,7},{4,0},{5,1},{6,2},{7,3},{8,12},{9,13},{10,... | collective-permute-start | bytes 811016 | tf_op jit(solution)/shard_map/ppermute | solution.py:246
  71.8 4.3 %collective-permute-done.30 = f32[136,256]{1,0:T(8,128)S(1)} collective-permute-done((f32[136,256]{1,0:T(8,128)S(1)}, f32[136,256]{1,0:T(8,128)S(1)}, u32[]{:S(2)}, u32[]{:S(2)}) %collective-permute-start.30) | collective-permute-done | bytes 139296 | tf_op jit(solution)/shard_map/ppermute | solution.py:246
  76.1 0.9 %collective-permute-start.31 = (f32[136,256]{1,0:T(8,128)S(1)}, f32[136,256]{1,0:T(8,128)S(1)}, u32[]{:S(2)}, u32[]{:S(2)}) collective-permute-start(f32[136,256]{1,0:T(8,128)S(1)} %add.7), channel_id=1, source_target_pairs={{0,8},{1,9},{2,10},{3,11},{4,12},{5,13},{6,14},{7,15},{8,0},{9,1},... | collective-permute-start | bytes 417800 | tf_op jit(solution)/shard_map/ppermute | solution.py:246
  77.1 8.9 %collective-permute-done.28 = f32[128,256]{1,0:T(8,128)S(1)} collective-permute-done((f32[128,256]{1,0:T(8,128)S(1)}, f32[128,256]{1,0:T(8,128)S(1)}, u32[]{:S(2)}, u32[]{:S(2)}) %collective-permute-start.28) | collective-permute-done | bytes 131104 | tf_op jit(solution)/shard_map/ppermute | solution.py:246
  86.1 6.6 %collective-permute-done.29.refs_4_ = f32[128,256]{1,0:T(8,128)S(1)} collective-permute-done((f32[128,256]{1,0:T(8,128)S(1)}, f32[128,256]{1,0:T(8,128)S(1)}, u32[]{:S(2)}, u32[]{:S(2)}) %collective-permute-start.29) | collective-permute-done | bytes 131104 | tf_op jit(solution)/shard_map/ppermute | solution.py:246
  (70 shorter events, 8.6 us)
Async XLA Ops:
  5.2 5.7 %collective-permute-start.6 = (f32[4,1,16,256]{3,2,1,0:T(8,128)}, f32[4,1,16,256]{3,2,1,0:T(8,128)S(1)}, u32[]{:S(2)}, u32[]{:S(2)}) collective-permute-start(f32[4,1,16,256]{3,2,1,0:T(8,128)} %get-tuple-element.64), channel_id=1, source_target_pairs={{0,4},{1,5},{2,6},{3,7},{4,0},{5,1},{6,2},{7,3},{8,12},{9,13},{10,... | collective-permute-start | bytes 196616 | tf_op jit(solution)/shard_map/ppermute | solution.py:246
  8.3 7.5 %collective-permute-start.7 = (f32[4,1,16,256]{3,2,1,0:T(8,128)}, f32[4,1,16,256]{3,2,1,0:T(8,128)S(1)}, u32[]{:S(2)}, u32[]{:S(2)}) collective-permute-start(f32[4,1,16,256]{3,2,1,0:T(8,128)} %get-tuple-element.65), channel_id=1, source_target_pairs={{0,8},{1,9},{2,10},{3,11},{4,12},{5,13},{6,14},{7,15},{8,0},{9,1},... | collective-permute-start | bytes 196616 | tf_op jit(solution)/shard_map/ppermute | solution.py:246
  10.9 6.3 %collective-permute-start.8 = (f32[4,1,16,256]{3,2,1,0:T(8,128)}, f32[4,1,16,256]{3,2,1,0:T(8,128)S(1)}, u32[]{:S(2)}, u32[]{:S(2)}) collective-permute-start(f32[4,1,16,256]{3,2,1,0:T(8,128)} %get-tuple-element.66), channel_id=1, source_target_pairs={{0,12},{1,13},{2,14},{3,15},{4,8},{5,9},{6,10},{7,11},{8,4},{9,5},... | collective-permute-start | bytes 196616 | tf_op jit(solution)/shard_map/ppermute | solution.py:246
  18.1 6.7 %collective-permute-start.9 = (f32[4,1,16,256]{3,2,1,0:T(8,128)S(1)}, f32[4,1,16,256]{3,2,1,0:T(8,128)S(1)}, u32[]{:S(2)}, u32[]{:S(2)}) collective-permute-start(f32[4,1,16,256]{3,2,1,0:T(8,128)S(1)} %get-tuple-element.68), channel_id=1, source_target_pairs={{0,1},{1,0},{2,3},{3,2},{4,5},{5,4},{6,7},{7,6},{8,9},{9,8},{10,11... | collective-permute-start | bytes 196616 | tf_op jit(solution)/shard_map/ppermute | solution.py:246
  18.2 8.7 %collective-permute-start.10 = (f32[4,1,16,256]{3,2,1,0:T(8,128)S(1)}, f32[4,1,16,256]{3,2,1,0:T(8,128)S(1)}, u32[]{:S(2)}, u32[]{:S(2)}) collective-permute-start(f32[4,1,16,256]{3,2,1,0:T(8,128)S(1)} %get-tuple-element.69), channel_id=1, source_target_pairs={{0,2},{1,3},{2,0},{3,1},{4,6},{5,7},{6,4},{7,5},{8,10},{9,11},{10,... | collective-permute-start | bytes 196616 | tf_op jit(solution)/shard_map/ppermute | solution.py:246
  19.7 7.1 %collective-permute-start.11 = (f32[4,1,16,256]{3,2,1,0:T(8,128)S(1)}, f32[4,1,16,256]{3,2,1,0:T(8,128)S(1)}, u32[]{:S(2)}, u32[]{:S(2)}) collective-permute-start(f32[4,1,16,256]{3,2,1,0:T(8,128)S(1)} %get-tuple-element.70), channel_id=1, source_target_pairs={{0,3},{1,2},{2,1},{3,0},{4,7},{5,6},{6,5},{7,4},{8,11},{9,10},{10,... | collective-permute-start | bytes 196616 | tf_op jit(solution)/shard_map/ppermute | solution.py:246
  22.4 10.3 %collective-permute-start = (f32[4,1,16,256]{3,2,1,0:T(8,128)S(1)}, f32[4,1,16,256]{3,2,1,0:T(8,128)S(1)}, u32[]{:S(2)}, u32[]{:S(2)}) collective-permute-start(f32[4,1,16,256]{3,2,1,0:T(8,128)S(1)} %get-tuple-element.52), channel_id=1, source_target_pairs={{0,4},{1,5},{2,6},{3,7},{4,0},{5,1},{6,2},{7,3},{8,12},{9,13},{10,... | collective-permute-start | bytes 196616 | tf_op jit(solution)/shard_map/ppermute | solution.py:246
  22.5 10.3 %collective-permute-start.1 = (f32[4,1,16,256]{3,2,1,0:T(8,128)S(1)}, f32[4,1,16,256]{3,2,1,0:T(8,128)S(1)}, u32[]{:S(2)}, u32[]{:S(2)}) collective-permute-start(f32[4,1,16,256]{3,2,1,0:T(8,128)S(1)} %get-tuple-element.53), channel_id=1, source_target_pairs={{0,8},{1,9},{2,10},{3,11},{4,12},{5,13},{6,14},{7,15},{8,0},{9,1},... | collective-permute-start | bytes 196616 | tf_op jit(solution)/shard_map/ppermute | solution.py:246
  24.8 7.9 %collective-permute-start.2 = (f32[4,1,16,256]{3,2,1,0:T(8,128)S(1)}, f32[4,1,16,256]{3,2,1,0:T(8,128)S(1)}, u32[]{:S(2)}, u32[]{:S(2)}) collective-permute-start(f32[4,1,16,256]{3,2,1,0:T(8,128)S(1)} %get-tuple-element.54), channel_id=1, source_target_pairs={{0,12},{1,13},{2,14},{3,15},{4,8},{5,9},{6,10},{7,11},{8,4},{9,5},... | collective-permute-start | bytes 196616 | tf_op jit(solution)/shard_map/ppermute | solution.py:246
  31.2 13.5 %collective-permute-start.16 = (f32[256,256]{1,0:T(8,128)S(1)}, f32[256,256]{1,0:T(8,128)S(1)}, u32[]{:S(2)}, u32[]{:S(2)}) collective-permute-start(f32[256,256]{1,0:T(8,128)S(1)} %get-tuple-element.74.refs_4_.refs_2_), channel_id=1, source_target_pairs={{0,2},{1,3},{2,0},{3,1},{4,6},{5,7},{6,4},{7,5},{8,10},{9,11},{10,... | collective-permute-start | bytes 786440 | tf_op jit(solution)/shard_map/ppermute | solution.py:246
  32.7 3.0 %collective-permute-start.3 = (f32[4,1,16,256]{3,2,1,0:T(8,128)S(1)}, f32[4,1,16,256]{3,2,1,0:T(8,128)S(1)}, u32[]{:S(2)}, u32[]{:S(2)}) collective-permute-start(f32[4,1,16,256]{3,2,1,0:T(8,128)S(1)} %get-tuple-element.60), channel_id=1, source_target_pairs={{0,1},{1,0},{2,3},{3,2},{4,5},{5,4},{6,7},{7,6},{8,9},{9,8},{10,11... | collective-permute-start | bytes 196616 | tf_op jit(solution)/shard_map/ppermute | solution.py:246
  32.8 8.2 %collective-permute-start.4 = (f32[4,1,16,256]{3,2,1,0:T(8,128)S(1)}, f32[4,1,16,256]{3,2,1,0:T(8,128)S(1)}, u32[]{:S(2)}, u32[]{:S(2)}) collective-permute-start(f32[4,1,16,256]{3,2,1,0:T(8,128)S(1)} %get-tuple-element.61), channel_id=1, source_target_pairs={{0,2},{1,3},{2,0},{3,1},{4,6},{5,7},{6,4},{7,5},{8,10},{9,11},{10,... | collective-permute-start | bytes 196616 | tf_op jit(solution)/shard_map/ppermute | solution.py:246
  33.4 7.6 %collective-permute-start.5 = (f32[4,1,16,256]{3,2,1,0:T(8,128)S(1)}, f32[4,1,16,256]{3,2,1,0:T(8,128)S(1)}, u32[]{:S(2)}, u32[]{:S(2)}) collective-permute-start(f32[4,1,16,256]{3,2,1,0:T(8,128)S(1)} %get-tuple-element.62), channel_id=1, source_target_pairs={{0,3},{1,2},{2,1},{3,0},{4,7},{5,6},{6,5},{7,4},{8,11},{9,10},{10,... | collective-permute-start | bytes 196616 | tf_op jit(solution)/shard_map/ppermute | solution.py:246
  34.7 14.5 %collective-permute-start.13 = (f32[256,256]{1,0:T(8,128)S(1)}, f32[256,256]{1,0:T(8,128)S(1)}, u32[]{:S(2)}, u32[]{:S(2)}) collective-permute-start(f32[256,256]{1,0:T(8,128)S(1)} %copy-done.8), channel_id=1, source_target_pairs={{0,8},{1,9},{2,10},{3,11},{4,12},{5,13},{6,14},{7,15},{8,0},{9,1},... | collective-permute-start | bytes 786440 | tf_op jit(solution)/shard_map/ppermute | solution.py:246
  35.7 13.9 %collective-permute-start.12 = (f32[256,256]{1,0:T(8,128)S(1)}, f32[256,256]{1,0:T(8,128)S(1)}, u32[]{:S(2)}, u32[]{:S(2)}) collective-permute-start(f32[256,256]{1,0:T(8,128)S(1)} %copy-done.8), channel_id=1, source_target_pairs={{0,4},{1,5},{2,6},{3,7},{4,0},{5,1},{6,2},{7,3},{8,12},{9,13},{10,... | collective-permute-start | bytes 786440 | tf_op jit(solution)/shard_map/ppermute | solution.py:246
  44.7 9.0 %collective-permute-start.22 = (f32[256,256]{1,0:T(8,128)S(1)}, f32[256,256]{1,0:T(8,128)S(1)}, u32[]{:S(2)}, u32[]{:S(2)}) collective-permute-start(f32[256,256]{1,0:T(8,128)S(1)} %get-tuple-element.81.refs_4_.refs_12_), channel_id=1, source_target_pairs={{0,2},{1,3},{2,0},{3,1},{4,6},{5,7},{6,4},{7,5},{8,10},{9,11},{10,... | collective-permute-start | bytes 786440 | tf_op jit(solution)/shard_map/ppermute | solution.py:246
  46.2 7.5 %collective-permute-start.15 = (f32[256,256]{1,0:T(8,128)S(1)}, f32[256,256]{1,0:T(8,128)S(1)}, u32[]{:S(2)}, u32[]{:S(2)}) collective-permute-start(f32[256,256]{1,0:T(8,128)S(1)} %get-tuple-element.74.refs_4_.refs_2_), channel_id=1, source_target_pairs={{0,1},{1,0},{2,3},{3,2},{4,5},{5,4},{6,7},{7,6},{8,9},{9,8},{10,11... | collective-permute-start | bytes 786440 | tf_op jit(solution)/shard_map/ppermute | solution.py:246
  49.2 8.2 %collective-permute-start.14 = (f32[256,256]{1,0:T(8,128)S(1)}, f32[256,256]{1,0:T(8,128)S(1)}, u32[]{:S(2)}, u32[]{:S(2)}) collective-permute-start(f32[256,256]{1,0:T(8,128)S(1)} %collective-permute-done.13.refs_2_), channel_id=1, source_target_pairs={{0,4},{1,5},{2,6},{3,7},{4,0},{5,1},{6,2},{7,3},{8,12},{9,13},{10,... | collective-permute-start | bytes 786440 | tf_op jit(solution)/shard_map/ppermute | solution.py:246
  49.2 9.0 %collective-permute-start.17 = (f32[256,256]{1,0:T(8,128)S(1)}, f32[256,256]{1,0:T(8,128)S(1)}, u32[]{:S(2)}, u32[]{:S(2)}) collective-permute-start(f32[256,256]{1,0:T(8,128)S(1)} %collective-permute-done.16.refs_4_), channel_id=1, source_target_pairs={{0,1},{1,0},{2,3},{3,2},{4,5},{5,4},{6,7},{7,6},{8,9},{9,8},{10,11... | collective-permute-start | bytes 786440 | tf_op jit(solution)/shard_map/ppermute | solution.py:246
  49.6 11.3 %collective-permute-start.21 = (f32[256,256]{1,0:T(8,128)S(1)}, f32[256,256]{1,0:T(8,128)S(1)}, u32[]{:S(2)}, u32[]{:S(2)}) collective-permute-start(f32[256,256]{1,0:T(8,128)S(1)} %get-tuple-element.81.refs_4_.refs_12_), channel_id=1, source_target_pairs={{0,1},{1,0},{2,3},{3,2},{4,5},{5,4},{6,7},{7,6},{8,9},{9,8},{10,11... | collective-permute-start | bytes 786440 | tf_op jit(solution)/shard_map/ppermute | solution.py:246
  53.7 8.1 %collective-permute-start.23 = (f32[256,256]{1,0:T(8,128)S(1)}, f32[256,256]{1,0:T(8,128)S(1)}, u32[]{:S(2)}, u32[]{:S(2)}) collective-permute-start(f32[256,256]{1,0:T(8,128)S(1)} %collective-permute-done.22.refs_4_.refs_14_), channel_id=1, source_target_pairs={{0,1},{1,0},{2,3},{3,2},{4,5},{5,4},{6,7},{7,6},{8,9},{9,8},{10,11... | collective-permute-start | bytes 786440 | tf_op jit(solution)/shard_map/ppermute | solution.py:246
  59.0 5.5 %collective-permute-start.20 = (f32[4,1,256]{2,1,0:T(1,128)S(1)}, f32[4,1,256]{2,1,0:T(1,128)S(1)}, u32[]{:S(2)}, u32[]{:S(2)}) collective-permute-start(f32[4,1,256]{2,1,0:T(1,128)S(1)} %get-tuple-element.80.refs_6_), channel_id=1, source_target_pairs={{0,3},{1,2},{2,1},{3,0},{4,7},{5,6},{6,5},{7,4},{8,11},{9,10},{10,... | collective-permute-start | bytes 12296 | tf_op jit(solution)/shard_map/ppermute | solution.py:246
  59.1 5.6 %collective-permute-start.19 = (f32[4,1,256]{2,1,0:T(1,128)S(1)}, f32[4,1,256]{2,1,0:T(1,128)S(1)}, u32[]{:S(2)}, u32[]{:S(2)}) collective-permute-start(f32[4,1,256]{2,1,0:T(1,128)S(1)} %get-tuple-element.80.refs_6_), channel_id=1, source_target_pairs={{0,2},{1,3},{2,0},{3,1},{4,6},{5,7},{6,4},{7,5},{8,10},{9,11},{10,... | collective-permute-start | bytes 12296 | tf_op jit(solution)/shard_map/ppermute | solution.py:246
  60.0 4.7 %collective-permute-start.18 = (f32[4,1,256]{2,1,0:T(1,128)S(1)}, f32[4,1,256]{2,1,0:T(1,128)S(1)}, u32[]{:S(2)}, u32[]{:S(2)}) collective-permute-start(f32[4,1,256]{2,1,0:T(1,128)S(1)} %get-tuple-element.80.refs_6_), channel_id=1, source_target_pairs={{0,1},{1,0},{2,3},{3,2},{4,5},{5,4},{6,7},{7,6},{8,9},{9,8},{10,11... | collective-permute-start | bytes 12296 | tf_op jit(solution)/shard_map/ppermute | solution.py:246
  62.8 3.1 %collective-permute-start.26 = (f32[4,1,256]{2,1,0:T(1,128)S(1)}, f32[4,1,256]{2,1,0:T(1,128)S(1)}, u32[]{:S(2)}, u32[]{:S(2)}) collective-permute-start(f32[4,1,256]{2,1,0:T(1,128)S(1)} %get-tuple-element.86.refs_16_), channel_id=1, source_target_pairs={{0,3},{1,2},{2,1},{3,0},{4,7},{5,6},{6,5},{7,4},{8,11},{9,10},{10,... | collective-permute-start | bytes 12296 | tf_op jit(solution)/shard_map/ppermute | solution.py:246
  63.3 3.6 %collective-permute-start.25 = (f32[4,1,256]{2,1,0:T(1,128)S(1)}, f32[4,1,256]{2,1,0:T(1,128)S(1)}, u32[]{:S(2)}, u32[]{:S(2)}) collective-permute-start(f32[4,1,256]{2,1,0:T(1,128)S(1)} %get-tuple-element.86.refs_16_), channel_id=1, source_target_pairs={{0,2},{1,3},{2,0},{3,1},{4,6},{5,7},{6,4},{7,5},{8,10},{9,11},{10,... | collective-permute-start | bytes 12296 | tf_op jit(solution)/shard_map/ppermute | solution.py:246
  64.5 2.5 %collective-permute-start.24 = (f32[4,1,256]{2,1,0:T(1,128)S(1)}, f32[4,1,256]{2,1,0:T(1,128)S(1)}, u32[]{:S(2)}, u32[]{:S(2)}) collective-permute-start(f32[4,1,256]{2,1,0:T(1,128)S(1)} %get-tuple-element.86.refs_16_), channel_id=1, source_target_pairs={{0,1},{1,0},{2,3},{3,2},{4,5},{5,4},{6,7},{7,6},{8,9},{9,8},{10,11... | collective-permute-start | bytes 12296 | tf_op jit(solution)/shard_map/ppermute | solution.py:246
  69.4 6.7 %collective-permute-start.30 = (f32[136,256]{1,0:T(8,128)S(1)}, f32[136,256]{1,0:T(8,128)S(1)}, u32[]{:S(2)}, u32[]{:S(2)}) collective-permute-start(f32[136,256]{1,0:T(8,128)S(1)} %get-tuple-element.92), channel_id=1, source_target_pairs={{0,4},{1,5},{2,6},{3,7},{4,0},{5,1},{6,2},{7,3},{8,12},{9,13},{10,... | collective-permute-start | bytes 417800 | tf_op jit(solution)/shard_map/ppermute | solution.py:246
  69.8 23.0 %collective-permute-start.27 = (f32[264,256]{1,0:T(8,128)S(1)}, f32[264,256]{1,0:T(8,128)S(1)}, u32[]{:S(2)}, u32[]{:S(2)}) collective-permute-start(f32[264,256]{1,0:T(8,128)S(1)} %get-tuple-element.88), channel_id=1, source_target_pairs={{0,4},{1,5},{2,6},{3,7},{4,0},{5,1},{6,2},{7,3},{8,12},{9,13},{10,... | collective-permute-start | bytes 811016 | tf_op jit(solution)/shard_map/ppermute | solution.py:246
  71.5 14.5 %collective-permute-start.28 = (f32[128,256]{1,0:T(8,128)S(1)}, f32[128,256]{1,0:T(8,128)S(1)}, u32[]{:S(2)}, u32[]{:S(2)}) collective-permute-start(f32[128,256]{1,0:T(8,128)S(1)} %get-tuple-element.90), channel_id=1, source_target_pairs={{0,4},{1,5},{2,6},{3,7},{4,0},{5,1},{6,2},{7,3},{8,12},{9,13},{10,... | collective-permute-start | bytes 393224 | tf_op jit(solution)/shard_map/ppermute | solution.py:246
  76.1 16.6 %collective-permute-start.31 = (f32[136,256]{1,0:T(8,128)S(1)}, f32[136,256]{1,0:T(8,128)S(1)}, u32[]{:S(2)}, u32[]{:S(2)}) collective-permute-start(f32[136,256]{1,0:T(8,128)S(1)} %add.7), channel_id=1, source_target_pairs={{0,8},{1,9},{2,10},{3,11},{4,12},{5,13},{6,14},{7,15},{8,0},{9,1},... | collective-permute-start | bytes 417800 | tf_op jit(solution)/shard_map/ppermute | solution.py:246
  86.0 6.7 %collective-permute-start.29 = (f32[128,256]{1,0:T(8,128)S(1)}, f32[128,256]{1,0:T(8,128)S(1)}, u32[]{:S(2)}, u32[]{:S(2)}) collective-permute-start(f32[128,256]{1,0:T(8,128)S(1)} %add.6), channel_id=1, source_target_pairs={{0,8},{1,9},{2,10},{3,11},{4,12},{5,13},{6,14},{7,15},{8,0},{9,1},... | collective-permute-start | bytes 393224 | tf_op jit(solution)/shard_map/ppermute | solution.py:246
  (12 other events, 103.3 us)

commit v3 on v2

--- a/solution.py
+++ b/solution.py
@@ -46,7 +46,7 @@
     tokens, width = x.shape
     head = width // HEADS
     h = x * lax.rsqrt(jnp.mean(x * x, -1, keepdims=True) + EPSILON) * gain
-    packed = dot3(split(h), split(w_qkv))
+    packed = dot3(split(h), w_qkv)
     row_head = lax.broadcasted_iota(jnp.int32, (width, width), 0) // head
     lane_head = lax.broadcasted_iota(jnp.int32, (width, width), 1) // head
     same_head = (row_head == lane_head).astype(BF16)
@@ -59,7 +59,7 @@
     k = split(unit_heads(packed[:, width : 2 * width]))
     v = split(packed[:, 2 * width :])
     lanes = lax.broadcasted_iota(jnp.int32, (tokens, width), 1) // head
-    mixed = jnp.zeros((tokens, width), F32)
+    sums = totals = None
     for i in range(HEADS):
         mine = lanes == i
         qi = [jnp.where(mine, part, jnp.zeros_like(part)) for part in q]
@@ -68,24 +68,15 @@
             weights = jnp.where(mask, weights, 0.0)
         vi = [jnp.where(mine, part, jnp.full_like(part, fill)) for part, fill in zip(v, (1.0, 0.0))]
         r = dot3(split(weights), vi)
-        totals = jnp.concatenate([r[:, width // 2 :], r[:, : width // 2]], axis=1)
-        mixed = jnp.where(mine, r / totals, mixed)
-    return x + dot3(split(mixed), split(w_out))
-
-
-def space_kernel(me_ref, x_ref, gain_ref, w_qkv_ref, w_out_ref, *rest):
-    *out_refs, by_device = rest
-    for f in range(x_ref.shape[0]):
-        y = attend(x_ref[f], gain_ref[...], w_qkv_ref[...], w_out_ref[...], None)
-        by_device[...] = y.reshape(by_device.shape)
-        for r, out_ref in enumerate(out_refs):
-            for m in range(SHARERS):
-                out_ref[m, f] = by_device[me_ref[0] ^ (m + SHARERS * r)]
-
-
-def first_kernel(me_ref, video, gain, w_qkv, w_out, sums, counts, codes_ref, *rest, blocks):
-    out_refs, refs, (by_device, sem) = rest[:blocks], rest[blocks:-2], rest[-2:]
-    sources = (sums, counts, video.at[0], gain, w_qkv, w_out)
+        sums = r if i == 0 else jnp.where(mine, r, sums)
+        totals = r if i == 0 else jnp.where(lanes == (i + HEADS // 2) % HEADS, r, totals)
+    totals = jnp.concatenate([totals[:, width // 2 :], totals[:, : width // 2]], axis=1)
+    return x + dot3(split(sums / totals), w_out)
+
+
+def first_kernel(video, gain, w_qkv, w_out, sums, counts, codes_ref, out_ref, *scratch):
+    refs, sem = scratch[:-1], scratch[-1]
+    sources = (sums, counts, video, gain, w_qkv, w_out)
     copies = [pltpu.make_async_copy(a, b, sem.at[i]) for i, (a, b) in enumerate(zip(sources, refs))]
     for copy in copies:
         copy.start()
@@ -95,40 +86,29 @@
     code_kernel(sums, counts, codes_ref)
     for copy in copies[2:]:
         copy.wait()
-    space_kernel(me_ref, x, gain, w_qkv, w_out, *out_refs, by_device)
-
-
-def merge_kernel(*refs, blocks):
-    arrived, out_refs = refs[:blocks], refs[blocks:]
-    for m, out_ref in enumerate(out_refs):
-        for r in range(blocks):
-            out_ref[r] = arrived[r][m]
-
-
-def time_kernel(me_ref, start_ref, gain_ref, w_qkv_ref, w_out_ref, *rest, clip):
-    x_refs, (latents_ref, unit_ref) = rest[:SHARERS], rest[-2:]
-    blocks, local_frames, places, width = x_refs[0].shape
-    group = blocks * local_frames * places
-    tokens = SHARERS * group
-    x = jnp.concatenate([ref[...].reshape(group, width) for ref in x_refs], axis=0)
-    me, start = me_ref[0], start_ref[clip]
-
-    def place_and_frame(index):
-        slot = index // places
-        place, frame, slot = index - slot * places, slot % local_frames, slot // local_frames
-        sender = (slot // blocks + SHARERS * (slot % blocks)) ^ me
-        return place, sender * local_frames + frame
-
-    place, later = place_and_frame(lax.broadcasted_iota(jnp.int32, (tokens, 1), 0))
-    other, earlier = place_and_frame(lax.broadcasted_iota(jnp.int32, (1, tokens), 1))
-    mask = (place == other) & ((earlier == later) | ((earlier < later) & (earlier >= start)))
-    y = attend(x, gain_ref[...], w_qkv_ref[...], w_out_ref[...], mask)
+    clips, local_frames = x.shape[:2]
+    places, width = out_ref.shape[2:]
+    w_qkv, w_out = split(w_qkv[...]), split(w_out[...])
+    for c in range(clips):
+        for f in range(local_frames):
+            y = attend(x[c, f], gain[...], w_qkv, w_out, None)
+            out_ref[:, c * local_frames + f] = y.reshape(-1, places, width)
+
+
+def time_kernel(start_ref, x_ref, gain_ref, w_qkv_ref, w_out_ref, *rest, clip):
+    latents_ref, unit_ref = rest[-2:]
+    senders, _, local_frames, places, width = x_ref.shape
+    tokens = senders * local_frames * places
+    x = x_ref[...].reshape(tokens, width)
+    row = lax.broadcasted_iota(jnp.int32, (tokens, 1), 0)
+    col = lax.broadcasted_iota(jnp.int32, (1, tokens), 1)
+    later, earlier = row // places, col // places
+    mask = ((row - later * places) == (col - earlier * places)) & (
+        (earlier == later) | ((earlier < later) & (earlier >= start_ref[clip]))
+    )
+    y = attend(x, gain_ref[...], split(w_qkv_ref[...]), split(w_out_ref[...]), mask)
+    latents_ref[...] = y.reshape(latents_ref.shape)
     unit_ref[...] = y * lax.rsqrt(jnp.sum(y * y, -1, keepdims=True) + EPSILON)
-    for slot in range(SHARERS * blocks):
-        sender = (slot // blocks + SHARERS * (slot % blocks)) ^ me
-        for f in range(local_frames):
-            row = (slot * local_frames + f) * places
-            latents_ref[0, sender * local_frames + f] = y[row : row + places]
 
 
 def column(row, lanes):
@@ -241,6 +221,8 @@
 
 def make_local(devices):
     sharers, blocks = SHARERS, devices // SHARERS
+    sharer_bits = [(m & 1) | (m >> 1) << 2 for m in range(sharers)]
+    block_bits = [(r & 1) << 1 | (r >> 1) << 3 for r in range(blocks)]
 
     def swap(x, bits):
         return lax.ppermute(x, "frames", [(i, i ^ bits) for i in range(devices)])
@@ -264,65 +246,31 @@
         tokens = frames * places
         gain_space, gain_time = gain_space[None], gain_time[None]
         counts_row = code_counts[None]
-        me = lax.axis_index("frames").astype(jnp.int32)[None]
-        sent = [shape(sharers, local_frames, places, width)] * blocks
-        by_device = pltpu.VMEM((devices, places, width), F32)
 
         hbm = pl.BlockSpec(memory_space=pltpu.HBM)
-        smem = pl.BlockSpec(memory_space=pltpu.SMEM)
         operands = (video, gain_space, qkv_space, out_space, code_sums, counts_row)
-        held = (code_sums, counts_row, video[0], gain_space, qkv_space, out_space)
-        codes, *first = pl.pallas_call(
-            lambda *refs: first_kernel(*refs, blocks=blocks),
-            in_specs=[smem] + [hbm] * len(operands),
-            out_shape=[shape(code_rows, width)] + sent,
+        held = (code_sums, counts_row, video, gain_space, qkv_space, out_space)
+        codes, spaced = pl.pallas_call(
+            first_kernel,
+            in_specs=[hbm] * len(operands),
+            out_shape=[shape(code_rows, width), shape(devices, clips * local_frames, places, width)],
             scratch_shapes=[pltpu.VMEM(a.shape, a.dtype) for a in held]
-            + [by_device, pltpu.SemaphoreType.DMA((len(held),))],
+            + [pltpu.SemaphoreType.DMA((len(held),))],
             compiler_params=params(FIRST_VMEM_BYTES),
-            cost_estimate=cost(2e9, *held),
+            cost_estimate=cost(clips * 2e9, *held),
             name="first_space",
-        )(me, *operands)
-
-        spaced = [first]
-        for c in range(1, clips):
-            spaced.append(
-                pl.pallas_call(
-                    space_kernel,
-                    grid=(1,),
-                    in_specs=[
-                        smem,
-                        pl.BlockSpec((None, local_frames, all_places, width), lambda i, c=c: (c, 0, 0, 0)),
-                        whole(gain_space),
-                        whole(qkv_space),
-                        whole(out_space),
-                    ],
-                    out_specs=[whole(a) for a in sent],
-                    out_shape=sent,
-                    scratch_shapes=[by_device],
-                    compiler_params=params(),
-                    cost_estimate=cost(2e9, *held),
-                    name="space_attention",
-                )(me, video, gain_space, qkv_space, out_space)
-            )
-
-        by_sender = []
-        for c in range(clips):
-            arrived = [spaced[c][0]] + [swap(spaced[c][r], r * sharers) for r in range(1, blocks)]
-            merged = simple_call(
-                lambda *refs: merge_kernel(*refs, blocks=blocks),
-                [shape(blocks, local_frames, places, width)] * sharers,
-                *arrived,
-                name="merge",
-            )
-            if c == clips - 1:
-                codes, *merged = lax.optimization_barrier((codes, *merged))
-            by_sender.append([merged[0]] + [swap(merged[m], m) for m in range(1, sharers)])
-
-        code_blocks = {0: codes}
+        )(*operands)
+
+        by_place = lax.all_to_all(spaced, "frames", split_axis=0, concat_axis=0, tiled=True)
+        codes, by_place = lax.optimization_barrier((codes, by_place))
+        by_place = by_place.reshape(devices, clips, local_frames, places, width)
+
+        half = code_rows // 2
+        halves = {0: [codes[:half], codes[half:]]}
         for bit in reversed(range((blocks - 1).bit_length())):
             step = 1 << bit
-            code_blocks |= {r ^ step: swap(block, step * sharers) for r, block in code_blocks.items()}
-        code_blocks = [code_blocks[r] for r in range(blocks)]
+            halves |= {r ^ step: [swap(part, block_bits[step]) for part in block] for r, block in halves.items()}
+        code_blocks = [part for r in range(blocks) for part in halves[r]]
 
         latents = None
         units = []
@@ -331,29 +279,34 @@
             latents, unit = pl.pallas_call(
                 lambda *refs, c=c: time_kernel(*refs, clip=c),
                 grid=(1,),
-                in_specs=[smem, smem, whole(gain_time), whole(qkv_time), whole(out_time)]
-                + [whole(a) for a in by_sender[c]]
+                in_specs=[
+                    pl.BlockSpec(memory_space=pltpu.SMEM),
+                    pl.BlockSpec((devices, 1, local_frames, places, width), lambda i, c=c: (0, c, 0, 0, 0)),
+                    whole(gain_time),
+                    whole(qkv_time),
+                    whole(out_time),
+                ]
                 + [pl.BlockSpec(memory_space=pl.ANY)] * len(before),
                 out_specs=(
                     pl.BlockSpec((1, frames, places, width), lambda i, c=c: (c, 0, 0, 0)),
                     pl.BlockSpec((tokens, width), lambda i: (0, 0)),
                 ),
                 out_shape=(shape(clips, frames, places, width), shape(tokens, width)),
-                input_output_aliases={5 + sharers: 0} if before else {},
+                input_output_aliases={5: 0} if before else {},
                 compiler_params=params(),
                 cost_estimate=cost(2e9, *held),
                 name="time_attention",
-            )(me, clip_start, gain_time, qkv_time, out_time, *by_sender[c], *before)
+            )(clip_start, by_place, gain_time, qkv_time, out_time, *before)
 
             if units:
                 unit, units[-1][2] = lax.optimization_barrier((unit, units[-1][2]))
-            far = swap(unit, 2)
+            far = swap(unit, sharer_bits[2])
             units.append([unit, swap(unit, 1), far, swap(far, 1)])
 
         def score(chunk_units, *before):
             n, m = len(chunk_units), len(before) * 2
             return simple_call(
-                lambda *refs: score_kernel(*refs, blocks=blocks, chunks=n, before=m),
+                lambda *refs: score_kernel(*refs, blocks=2 * blocks, chunks=n, before=m),
                 (shape(n, blocks * code_rows, tokens, dtype=BF16), shape(m + n, 1, tokens)),
                 *code_blocks,
                 *chunk_units,
@@ -369,7 +322,7 @@
             near_w, near_totals = score(units[c][:2])
             far_w, clip_totals = score(units[c][2:], near_totals)
             operands += [near_w, far_w, *units[c], clip_totals]
-            operands += [swap(clip_totals, m) for m in range(1, sharers)]
+            operands += [swap(clip_totals, sharer_bits[m]) for m in range(1, sharers)]
 
         half = code_rows // 2
         one, two = [shape(code_rows + 8, width)], [shape(half, width), shape(code_rows + 8 - half, width)]
@@ -386,7 +339,7 @@
         for bit in range((blocks - 1).bit_length()):
             step = 1 << bit
             for r in reversed(range(step, blocks, 2 * step)):
-                came = [swap(piece, step * sharers) for piece in terms[r]]
+                came = [swap(piece, block_bits[step]) for piece in terms[r]]
                 if r == step:
                     arrivals.append(came)
                 else:

time: 93.8 us -> 97.8 us (1.043)
  blocking collectives: 0 us -> 22 us
  waiting for transfers between devices: 43 us -> 29.5 us
  starting transfers between devices: 27.2 us -> 21.3 us
  Pallas kernels: 21 us -> 23.2 us
    all_to_all x0 -> x1, blocking collectives: none -> 22 us  [local(): lax.all_to_all(spaced, 'frames', split_axis=0, concat_axis=0, tiled=True)]
    ppermute x32 -> x23, waiting for transfers between devices: 43 us -> 29.5 us  [swap(): return lax.ppermute(x, 'frames', [(i, i ^ bits) for i in range(devices)])]
    ppermute x32 -> x23, starting transfers between devices: 27.2 us -> 21.3 us  [swap(): return lax.ppermute(x, 'frames', [(i, i ^ bits) for i in range(devices)])]
    pallas_call x8 -> x6, Pallas kernels: 6.8 us -> 9.51 us  [simple_call(): pl.pallas_call(kernel, out_shape=outs, compiler_params=params(), cost_est...]
    pallas_call x2 -> x1, Pallas kernels: 6.9 us -> 6.49 us  [local(): pl.pallas_call(first_kernel, in_specs=[hbm] * len(operands), out_shape=[s...]
  transfers between devices with their start and end apart: 32 -> 23, of which waited for: 12 -> 10; matrix products, arithmetic and copies ran while one was open for 0% -> 0% of each run, Pallas kernels for 14% -> 10%
where the time goes in v3:
time: 97.8 us; the launch traced here: 97.6 us
  waiting for transfers between devices  29.5 us (30%)
  Pallas kernels  23.2 us (24%)
  blocking collectives  22 us (22%)
  starting transfers between devices  21.3 us (22%)
    ppermute x23, waiting for transfers between devices, swap(): return lax.ppermute(x, 'frames', [(i, i ^ bits) for i in range(devices)])  29.5 us
    all_to_all x1, blocking collectives, local(): lax.all_to_all(spaced, 'frames', split_axis=0, concat_axis=0, tiled=True)  22 us
    ppermute x23, starting transfers between devices, swap(): return lax.ppermute(x, 'frames', [(i, i ^ bits) for i in range(devices)])  21.3 us
    pallas_call x6, Pallas kernels, simple_call(): pl.pallas_call(kernel, out_shape=outs, compiler_params=params(), cost_est...  9.51 us
    pallas_call x2, Pallas kernels, local(): pl.pallas_call(lambda *refs, c=c: time_kernel(*refs, clip=c), grid=(1,),...  7.19 us
    pallas_call x1, Pallas kernels, local(): pl.pallas_call(first_kernel, in_specs=[hbm] * len(operands), out_shape=[s...  6.49 us
  transfers between devices with their start and end apart: 23, of which 10 were waited for; matrix products, arithmetic and copies ran while one was open for 0% of the time, Pallas kernels for 10%

profile of v3, /device:TPU:0, one launch (start us, length us, event | category | flops | bytes accessed | tf_op | source)
XLA Modules:
  0.0 97.6 jit_solution(3484517701781226219)
XLA Ops:
  0.6 6.5 %first_space.1 = (f32[256,256]{1,0:T(8,128)}, f32[16,2,16,256]{3,2,1,0:T(8,128)}) custom-call(f32[2,1,256,256]{3,2,1,0:T(8,128)} %video.1, f32[1,256]{1,0:T(1,128)} %bitcast.11, f32[256,768]{1,0:T(8,128)} %w_qkv.1, f32[256,256]{1,0:T(8,128)} %w_out.1, f32[256,256]{1,0:T(8,128)} %refs_0_.5, f32[1,256]{1,0:T(1,128)} %bitcast.7), custom_call_target="tpu_custom_call" | custom-call | flops 4000000000 | bytes 1837056 | tf_op jit(solution)/shard_map/first_space/pallas_call | solution.py:253
  7.1 22.0 %all_to_all.5 = f32[16,2,16,256]{3,2,1,0:T(8,128)S(1)} all-to-all(f32[16,2,16,256]{3,2,1,0:T(8,128)} %get-tuple-element.33), channel_id=1, replica_groups=mesh['groups'=2,'frames'=16] {'frames'}, dimensions={0} | all-to-all | bytes 1048576 | tf_op jit(solution)/shard_map/all_to_all | solution.py:264
  29.8 3.6 %time_attention.2 = (f32[2,16,16,256]{3,2,1,0:T(8,128)}, f32[256,256]{1,0:T(8,128)S(1)}) custom-call(s32[2]{0:T(128)S(1)} %copy-done.5, f32[16,2,1,16,256]{4,3,2,1,0:T(8,128)S(1)} %bitcast.5, f32[1,256]{1,0:T(1,128)S(1)} %bitcast.9, f32[256,768]{1,0:T(8,128)S(1)} %copy-done.2, f32[256,256]{1,0:T(8,128)S(1)} %copy-done.3), custom_call_target="tpu_custom_call" | custom-call | flops 2000000000 | bytes 1837056 | tf_op jit(solution)/shard_map/time_attention/pallas_call | solution.py:279
  33.4 1.1 %collective-permute-start.7 = (f32[256,256]{1,0:T(8,128)S(1)}, f32[256,256]{1,0:T(8,128)S(1)}, u32[]{:S(2)}, u32[]{:S(2)}) collective-permute-start(f32[256,256]{1,0:T(8,128)S(1)} %get-tuple-element.38.refs_8_.refs_2_), channel_id=1, source_target_pairs={{0,4},{1,5},{2,6},{3,7},{4,0},{5,1},{6,2},{7,3},{8,12},{9,13},{10,... | collective-permute-start | bytes 786440 | tf_op jit(solution)/shard_map/ppermute | solution.py:228
  34.6 1.2 %collective-permute-start.3 = (f32[128,256]{1,0:T(8,128)S(1)}, f32[128,256]{1,0:T(8,128)S(1)}, u32[]{:S(2)}, u32[]{:S(2)}) collective-permute-start(f32[128,256]{1,0:T(8,128)S(1)} %get-tuple-element.60.refs_1_), channel_id=1, source_target_pairs={{0,8},{1,9},{2,10},{3,11},{4,12},{5,13},{6,14},{7,15},{8,0},{9,1},... | collective-permute-start | bytes 393224 | tf_op jit(solution)/shard_map/ppermute | solution.py:228
  35.8 1.6 %collective-permute-start.1 = (f32[128,256]{1,0:T(8,128)S(1)}, f32[128,256]{1,0:T(8,128)S(1)}, u32[]{:S(2)}, u32[]{:S(2)}) collective-permute-start(f32[128,256]{1,0:T(8,128)S(1)} %get-tuple-element.60.refs_1_), channel_id=1, source_target_pairs={{0,2},{1,3},{2,0},{3,1},{4,6},{5,7},{6,4},{7,5},{8,10},{9,11},{10,... | collective-permute-start | bytes 393224 | tf_op jit(solution)/shard_map/ppermute | solution.py:228
  37.4 3.6 %time_attention.3 = (f32[2,16,16,256]{3,2,1,0:T(8,128)}, f32[256,256]{1,0:T(8,128)S(1)}) custom-call(s32[2]{0:T(128)S(1)} %copy-done.5, f32[16,2,1,16,256]{4,3,2,1,0:T(8,128)S(1)} %bitcast.6, f32[1,256]{1,0:T(1,128)S(1)} %bitcast.10, f32[256,768]{1,0:T(8,128)S(1)} %copy-done.2, f32[256,256]{1,0:T(8,128)S(1)} %copy-done.3, ...), custom_call_target="tpu_custom_call", output_to_operand_aliasing={{0}: (5, {})} | custom-call | flops 2000000000 | bytes 1837056 | tf_op jit(solution)/shard_map/time_attention/pallas_call | solution.py:279
  41.0 3.5 %collective-permute-done.7.refs_8_.refs_4_ = f32[256,256]{1,0:T(8,128)S(1)} collective-permute-done((f32[256,256]{1,0:T(8,128)S(1)}, f32[256,256]{1,0:T(8,128)S(1)}, u32[]{:S(2)}, u32[]{:S(2)}) %collective-permute-start.7) | collective-permute-done | bytes 262176 | tf_op jit(solution)/shard_map/ppermute | solution.py:228
  44.5 2.5 %collective-permute-start.2 = (f32[128,256]{1,0:T(8,128)S(1)}, f32[128,256]{1,0:T(8,128)S(1)}, u32[]{:S(2)}, u32[]{:S(2)}) collective-permute-start(f32[128,256]{1,0:T(8,128)S(1)} %get-tuple-element.61.refs_0_), channel_id=1, source_target_pairs={{0,8},{1,9},{2,10},{3,11},{4,12},{5,13},{6,14},{7,15},{8,0},{9,1},... | collective-permute-start | bytes 393224 | tf_op jit(solution)/shard_map/ppermute | solution.py:228
  47.0 1.6 %collective-permute-start = (f32[128,256]{1,0:T(8,128)S(1)}, f32[128,256]{1,0:T(8,128)S(1)}, u32[]{:S(2)}, u32[]{:S(2)}) collective-permute-start(f32[128,256]{1,0:T(8,128)S(1)} %get-tuple-element.61.refs_0_), channel_id=1, source_target_pairs={{0,2},{1,3},{2,0},{3,1},{4,6},{5,7},{6,4},{7,5},{8,10},{9,11},{10,... | collective-permute-start | bytes 393224 | tf_op jit(solution)/shard_map/ppermute | solution.py:228
  49.0 3.5 %collective-permute-done.2.refs_4_ = f32[128,256]{1,0:T(8,128)S(1)} collective-permute-done((f32[128,256]{1,0:T(8,128)S(1)}, f32[128,256]{1,0:T(8,128)S(1)}, u32[]{:S(2)}, u32[]{:S(2)}) %collective-permute-start.2) | collective-permute-done | bytes 131104 | tf_op jit(solution)/shard_map/ppermute | solution.py:228
  53.0 1.1 %collective-permute-done.5.refs_7_ = f32[128,256]{1,0:T(8,128)S(1)} collective-permute-done((f32[128,256]{1,0:T(8,128)S(1)}, f32[128,256]{1,0:T(8,128)S(1)}, u32[]{:S(2)}, u32[]{:S(2)}) %collective-permute-start.5) | collective-permute-done | bytes 131104 | tf_op jit(solution)/shard_map/ppermute | solution.py:228
  54.1 1.7 %collective-permute-start.4 = (f32[128,256]{1,0:T(8,128)S(1)}, f32[128,256]{1,0:T(8,128)S(1)}, u32[]{:S(2)}, u32[]{:S(2)}) collective-permute-start(f32[128,256]{1,0:T(8,128)S(1)} %collective-permute-done.2.refs_4_), channel_id=1, source_target_pairs={{0,2},{1,3},{2,0},{3,1},{4,6},{5,7},{6,4},{7,5},{8,10},{9,11},{10,... | collective-permute-start | bytes 393224 | tf_op jit(solution)/shard_map/ppermute | solution.py:228
  55.7 3.3 %collective-permute-done.4.refs_6_ = f32[128,256]{1,0:T(8,128)S(1)} collective-permute-done((f32[128,256]{1,0:T(8,128)S(1)}, f32[128,256]{1,0:T(8,128)S(1)}, u32[]{:S(2)}, u32[]{:S(2)}) %collective-permute-start.4) | collective-permute-done | bytes 131104 | tf_op jit(solution)/shard_map/ppermute | solution.py:228
  59.0 1.5 %scores.4 = (bf16[2,1024,256]{2,1,0:T(8,128)(2,1)S(1)}, f32[2,1,256]{2,1,0:T(1,128)S(1)}) custom-call(f32[128,256]{1,0:T(8,128)S(1)} %get-tuple-element.61.refs_0_, f32[128,256]{1,0:T(8,128)S(1)} %get-tuple-element.60.refs_1_, f32[128,256]{1,0:T(8,128)S(1)} %collective-permute-done.refs_2_, f32[128,256]{1,0:T(8,128)S(1)} %collective-permute-done.1.refs_3_, ...), custom_call_target="tpu_custom_call" | custom-call | flops 536870912 | bytes 2623488 | tf_op jit(solution)/shard_map/scores/pallas_call | solution.py:213
  60.6 1.5 %scores.5 = (bf16[2,1024,256]{2,1,0:T(8,128)(2,1)S(1)}, f32[4,1,256]{2,1,0:T(1,128)S(1)}) custom-call(f32[128,256]{1,0:T(8,128)S(1)} %get-tuple-element.61.refs_0_, f32[128,256]{1,0:T(8,128)S(1)} %get-tuple-element.60.refs_1_, f32[128,256]{1,0:T(8,128)S(1)} %collective-permute-done.refs_2_, f32[128,256]{1,0:T(8,128)S(1)} %collective-permute-done.1.refs_3_, ...), custom_call_target="tpu_custom_call" | custom-call | flops 536870912 | bytes 2627584 | tf_op jit(solution)/shard_map/scores/pallas_call | solution.py:213
  62.1 1.5 %collective-permute-start.11 = (f32[4,1,256]{2,1,0:T(1,128)S(1)}, f32[4,1,256]{2,1,0:T(1,128)S(1)}, u32[]{:S(2)}, u32[]{:S(2)}) collective-permute-start(f32[4,1,256]{2,1,0:T(1,128)S(1)} %get-tuple-element.44.refs_6_), channel_id=1, source_target_pairs={{0,5},{1,4},{2,7},{3,6},{4,1},{5,0},{6,3},{7,2},{8,13},{9,12},{10,... | collective-permute-start | bytes 12296 | tf_op jit(solution)/shard_map/ppermute | solution.py:228
  63.7 1.2 %collective-permute-start.10 = (f32[4,1,256]{2,1,0:T(1,128)S(1)}, f32[4,1,256]{2,1,0:T(1,128)S(1)}, u32[]{:S(2)}, u32[]{:S(2)}) collective-permute-start(f32[4,1,256]{2,1,0:T(1,128)S(1)} %get-tuple-element.44.refs_6_), channel_id=1, source_target_pairs={{0,4},{1,5},{2,6},{3,7},{4,0},{5,1},{6,2},{7,3},{8,12},{9,13},{10,... | collective-permute-start | bytes 12296 | tf_op jit(solution)/shard_map/ppermute | solution.py:228
  65.0 1.5 %scores.6 = (bf16[2,1024,256]{2,1,0:T(8,128)(2,1)S(1)}, f32[2,1,256]{2,1,0:T(1,128)S(1)}) custom-call(f32[128,256]{1,0:T(8,128)S(1)} %get-tuple-element.61.refs_0_, f32[128,256]{1,0:T(8,128)S(1)} %get-tuple-element.60.refs_1_, f32[128,256]{1,0:T(8,128)S(1)} %collective-permute-done.refs_2_, f32[128,256]{1,0:T(8,128)S(1)} %collective-permute-done.1.refs_3_, ...), custom_call_target="tpu_custom_call" | custom-call | flops 536870912 | bytes 2623488 | tf_op jit(solution)/shard_map/scores/pallas_call | solution.py:213
  66.5 1.5 %scores.7 = (bf16[2,1024,256]{2,1,0:T(8,128)(2,1)S(1)}, f32[4,1,256]{2,1,0:T(1,128)S(1)}) custom-call(f32[128,256]{1,0:T(8,128)S(1)} %get-tuple-element.61.refs_0_, f32[128,256]{1,0:T(8,128)S(1)} %get-tuple-element.60.refs_1_, f32[128,256]{1,0:T(8,128)S(1)} %collective-permute-done.refs_2_, f32[128,256]{1,0:T(8,128)S(1)} %collective-permute-done.1.refs_3_, ...), custom_call_target="tpu_custom_call" | custom-call | flops 536870912 | bytes 2627584 | tf_op jit(solution)/shard_map/scores/pallas_call | solution.py:213
  68.1 1.4 %collective-permute-start.17 = (f32[4,1,256]{2,1,0:T(1,128)S(1)}, f32[4,1,256]{2,1,0:T(1,128)S(1)}, u32[]{:S(2)}, u32[]{:S(2)}) collective-permute-start(f32[4,1,256]{2,1,0:T(1,128)S(1)} %get-tuple-element.50.refs_16_), channel_id=1, source_target_pairs={{0,5},{1,4},{2,7},{3,6},{4,1},{5,0},{6,3},{7,2},{8,13},{9,12},{10,... | collective-permute-start | bytes 12296 | tf_op jit(solution)/shard_map/ppermute | solution.py:228
  70.2 0.9 collective-permute-done.17.refs_19_
  71.2 1.9 %collective-permute-done.16.refs_18_ = f32[4,1,256]{2,1,0:T(1,128)S(1)} collective-permute-done((f32[4,1,256]{2,1,0:T(1,128)S(1)}, f32[4,1,256]{2,1,0:T(1,128)S(1)}, u32[]{:S(2)}, u32[]{:S(2)}) %collective-permute-start.16) | collective-permute-done | bytes 4128 | tf_op jit(solution)/shard_map/ppermute | solution.py:228
  73.1 2.5 %terms.1 = (f32[264,256]{1,0:T(8,128)S(1)}, f32[264,256]{1,0:T(8,128)S(1)}, f32[128,256]{1,0:T(8,128)S(1)}, f32[136,256]{1,0:T(8,128)S(1)}, f32[128,256]{1,0:T(8,128)S(1)}, /*index=5*/f32[136,256]{1,0:T(8,128)S(1)}) custom-call(bf16[2,1024,256]{2,1,0:T(8,128)(2,1)S(1)} %get-tuple-element.39.refs_0_, bf16[2,1024,256]{2,1,0:T(8,128)(2,1)S(1)} %get-tuple-element.43.refs_1_, ...), custom_call_target="tpu_custom_call" | custom-call | flops 1073741824 | bytes 7405568 | tf_op jit(solution)/shard_map/terms/pallas_call | solution.py:213
  75.6 1.7 %collective-permute-start.21 = (f32[136,256]{1,0:T(8,128)S(1)}, f32[136,256]{1,0:T(8,128)S(1)}, u32[]{:S(2)}, u32[]{:S(2)}) collective-permute-start(f32[136,256]{1,0:T(8,128)S(1)} %get-tuple-element.56), channel_id=1, source_target_pairs={{0,2},{1,3},{2,0},{3,1},{4,6},{5,7},{6,4},{7,5},{8,10},{9,11},{10,... | collective-permute-start | bytes 417800 | tf_op jit(solution)/shard_map/ppermute | solution.py:228
  77.7 1.7 %collective-permute-start.19 = (f32[128,256]{1,0:T(8,128)S(1)}, f32[128,256]{1,0:T(8,128)S(1)}, u32[]{:S(2)}, u32[]{:S(2)}) collective-permute-start(f32[128,256]{1,0:T(8,128)S(1)} %get-tuple-element.54), channel_id=1, source_target_pairs={{0,2},{1,3},{2,0},{3,1},{4,6},{5,7},{6,4},{7,5},{8,10},{9,11},{10,... | collective-permute-start | bytes 393224 | tf_op jit(solution)/shard_map/ppermute | solution.py:228
  79.3 2.9 %collective-permute-done.21 = f32[136,256]{1,0:T(8,128)S(1)} collective-permute-done((f32[136,256]{1,0:T(8,128)S(1)}, f32[136,256]{1,0:T(8,128)S(1)}, u32[]{:S(2)}, u32[]{:S(2)}) %collective-permute-start.21) | collective-permute-done | bytes 139296 | tf_op jit(solution)/shard_map/ppermute | solution.py:228
  82.3 1.1 %collective-permute-start.22 = (f32[136,256]{1,0:T(8,128)S(1)}, f32[136,256]{1,0:T(8,128)S(1)}, u32[]{:S(2)}, u32[]{:S(2)}) collective-permute-start(f32[136,256]{1,0:T(8,128)S(1)} %add.7), channel_id=1, source_target_pairs={{0,8},{1,9},{2,10},{3,11},{4,12},{5,13},{6,14},{7,15},{8,0},{9,1},... | collective-permute-start | bytes 417800 | tf_op jit(solution)/shard_map/ppermute | solution.py:228
  83.4 5.8 %collective-permute-done.19 = f32[128,256]{1,0:T(8,128)S(1)} collective-permute-done((f32[128,256]{1,0:T(8,128)S(1)}, f32[128,256]{1,0:T(8,128)S(1)}, u32[]{:S(2)}, u32[]{:S(2)}) %collective-permute-start.19) | collective-permute-done | bytes 131104 | tf_op jit(solution)/shard_map/ppermute | solution.py:228
  89.2 1.0 collective-permute-start.20
  90.2 6.5 %collective-permute-done.20.refs_4_ = f32[128,256]{1,0:T(8,128)S(1)} collective-permute-done((f32[128,256]{1,0:T(8,128)S(1)}, f32[128,256]{1,0:T(8,128)S(1)}, u32[]{:S(2)}, u32[]{:S(2)}) %collective-permute-start.20) | collective-permute-done | bytes 131104 | tf_op jit(solution)/shard_map/ppermute | solution.py:228
  96.7 0.9 update.1
  (41 shorter events, 2.9 us)
Async XLA Ops:
  7.1 22.0 %copy-start.2 = (f32[256,768]{1,0:T(8,128)S(1)}, f32[256,768]{1,0:T(8,128)}, u32[]{:S(2)}) copy-start(f32[256,768]{1,0:T(8,128)} %refs_3_.3) | copy-start | bytes 2359300
  7.1 22.0 %copy-start.3 = (f32[256,256]{1,0:T(8,128)S(1)}, f32[256,256]{1,0:T(8,128)}, u32[]{:S(2)}) copy-start(f32[256,256]{1,0:T(8,128)} %refs_4_.3) | copy-start | bytes 786436
  29.1 0.7 copy-start.4
  29.1 0.7 copy-start.5
  29.8 4.7 %copy-start.6 = (f32[256,256]{1,0:T(8,128)S(1)}, f32[256,256]{1,0:T(8,128)}, u32[]{:S(2)}) copy-start(f32[256,256]{1,0:T(8,128)} %get-tuple-element.37) | copy-start | bytes 786436
  33.4 11.0 %collective-permute-start.7 = (f32[256,256]{1,0:T(8,128)S(1)}, f32[256,256]{1,0:T(8,128)S(1)}, u32[]{:S(2)}, u32[]{:S(2)}) collective-permute-start(f32[256,256]{1,0:T(8,128)S(1)} %get-tuple-element.38.refs_8_.refs_2_), channel_id=1, source_target_pairs={{0,4},{1,5},{2,6},{3,7},{4,0},{5,1},{6,2},{7,3},{8,12},{9,13},{10,... | collective-permute-start | bytes 786440 | tf_op jit(solution)/shard_map/ppermute | solution.py:228
  34.6 14.0 %collective-permute-start.3 = (f32[128,256]{1,0:T(8,128)S(1)}, f32[128,256]{1,0:T(8,128)S(1)}, u32[]{:S(2)}, u32[]{:S(2)}) collective-permute-start(f32[128,256]{1,0:T(8,128)S(1)} %get-tuple-element.60.refs_1_), channel_id=1, source_target_pairs={{0,8},{1,9},{2,10},{3,11},{4,12},{5,13},{6,14},{7,15},{8,0},{9,1},... | collective-permute-start | bytes 393224 | tf_op jit(solution)/shard_map/ppermute | solution.py:228
  35.8 13.2 %collective-permute-start.1 = (f32[128,256]{1,0:T(8,128)S(1)}, f32[128,256]{1,0:T(8,128)S(1)}, u32[]{:S(2)}, u32[]{:S(2)}) collective-permute-start(f32[128,256]{1,0:T(8,128)S(1)} %get-tuple-element.60.refs_1_), channel_id=1, source_target_pairs={{0,2},{1,3},{2,0},{3,1},{4,6},{5,7},{6,4},{7,5},{8,10},{9,11},{10,... | collective-permute-start | bytes 393224 | tf_op jit(solution)/shard_map/ppermute | solution.py:228
  44.5 11.3 %collective-permute-start.13 = (f32[256,256]{1,0:T(8,128)S(1)}, f32[256,256]{1,0:T(8,128)S(1)}, u32[]{:S(2)}, u32[]{:S(2)}) collective-permute-start(f32[256,256]{1,0:T(8,128)S(1)} %get-tuple-element.45.refs_8_.refs_12_), channel_id=1, source_target_pairs={{0,4},{1,5},{2,6},{3,7},{4,0},{5,1},{6,2},{7,3},{8,12},{9,13},{10,... | collective-permute-start | bytes 786440 | tf_op jit(solution)/shard_map/ppermute | solution.py:228
  44.5 8.0 %collective-permute-start.2 = (f32[128,256]{1,0:T(8,128)S(1)}, f32[128,256]{1,0:T(8,128)S(1)}, u32[]{:S(2)}, u32[]{:S(2)}) collective-permute-start(f32[128,256]{1,0:T(8,128)S(1)} %get-tuple-element.61.refs_0_), channel_id=1, source_target_pairs={{0,8},{1,9},{2,10},{3,11},{4,12},{5,13},{6,14},{7,15},{8,0},{9,1},... | collective-permute-start | bytes 393224 | tf_op jit(solution)/shard_map/ppermute | solution.py:228
  47.0 5.7 %collective-permute-start = (f32[128,256]{1,0:T(8,128)S(1)}, f32[128,256]{1,0:T(8,128)S(1)}, u32[]{:S(2)}, u32[]{:S(2)}) collective-permute-start(f32[128,256]{1,0:T(8,128)S(1)} %get-tuple-element.61.refs_0_), channel_id=1, source_target_pairs={{0,2},{1,3},{2,0},{3,1},{4,6},{5,7},{6,4},{7,5},{8,10},{9,11},{10,... | collective-permute-start | bytes 393224 | tf_op jit(solution)/shard_map/ppermute | solution.py:228
  48.6 5.5 %collective-permute-start.5 = (f32[128,256]{1,0:T(8,128)S(1)}, f32[128,256]{1,0:T(8,128)S(1)}, u32[]{:S(2)}, u32[]{:S(2)}) collective-permute-start(f32[128,256]{1,0:T(8,128)S(1)} %collective-permute-done.3.refs_5_), channel_id=1, source_target_pairs={{0,2},{1,3},{2,0},{3,1},{4,6},{5,7},{6,4},{7,5},{8,10},{9,11},{10,... | collective-permute-start | bytes 393224 | tf_op jit(solution)/shard_map/ppermute | solution.py:228
  49.0 10.0 %collective-permute-start.6 = (f32[256,256]{1,0:T(8,128)S(1)}, f32[256,256]{1,0:T(8,128)S(1)}, u32[]{:S(2)}, u32[]{:S(2)}) collective-permute-start(f32[256,256]{1,0:T(8,128)S(1)} %get-tuple-element.38.refs_8_.refs_2_), channel_id=1, source_target_pairs={{0,1},{1,0},{2,3},{3,2},{4,5},{5,4},{6,7},{7,6},{8,9},{9,8},{10,11... | collective-permute-start | bytes 786440 | tf_op jit(solution)/shard_map/ppermute | solution.py:228
  52.4 8.1 %collective-permute-start.8 = (f32[256,256]{1,0:T(8,128)S(1)}, f32[256,256]{1,0:T(8,128)S(1)}, u32[]{:S(2)}, u32[]{:S(2)}) collective-permute-start(f32[256,256]{1,0:T(8,128)S(1)} %collective-permute-done.7.refs_8_.refs_4_), channel_id=1, source_target_pairs={{0,1},{1,0},{2,3},{3,2},{4,5},{5,4},{6,7},{7,6},{8,9},{9,8},{10,11... | collective-permute-start | bytes 786440 | tf_op jit(solution)/shard_map/ppermute | solution.py:228
  52.6 12.3 %collective-permute-start.12 = (f32[256,256]{1,0:T(8,128)S(1)}, f32[256,256]{1,0:T(8,128)S(1)}, u32[]{:S(2)}, u32[]{:S(2)}) collective-permute-start(f32[256,256]{1,0:T(8,128)S(1)} %get-tuple-element.45.refs_8_.refs_12_), channel_id=1, source_target_pairs={{0,1},{1,0},{2,3},{3,2},{4,5},{5,4},{6,7},{7,6},{8,9},{9,8},{10,11... | collective-permute-start | bytes 786440 | tf_op jit(solution)/shard_map/ppermute | solution.py:228
  54.1 5.0 %collective-permute-start.4 = (f32[128,256]{1,0:T(8,128)S(1)}, f32[128,256]{1,0:T(8,128)S(1)}, u32[]{:S(2)}, u32[]{:S(2)}) collective-permute-start(f32[128,256]{1,0:T(8,128)S(1)} %collective-permute-done.2.refs_4_), channel_id=1, source_target_pairs={{0,2},{1,3},{2,0},{3,1},{4,6},{5,7},{6,4},{7,5},{8,10},{9,11},{10,... | collective-permute-start | bytes 393224 | tf_op jit(solution)/shard_map/ppermute | solution.py:228
  55.7 10.8 %collective-permute-start.14 = (f32[256,256]{1,0:T(8,128)S(1)}, f32[256,256]{1,0:T(8,128)S(1)}, u32[]{:S(2)}, u32[]{:S(2)}) collective-permute-start(f32[256,256]{1,0:T(8,128)S(1)} %collective-permute-done.13.refs_8_.refs_14_), channel_id=1, source_target_pairs={{0,1},{1,0},{2,3},{3,2},{4,5},{5,4},{6,7},{7,6},{8,9},{9,8},{10,11... | collective-permute-start | bytes 786440 | tf_op jit(solution)/shard_map/ppermute | solution.py:228
  62.1 8.1 %collective-permute-start.11 = (f32[4,1,256]{2,1,0:T(1,128)S(1)}, f32[4,1,256]{2,1,0:T(1,128)S(1)}, u32[]{:S(2)}, u32[]{:S(2)}) collective-permute-start(f32[4,1,256]{2,1,0:T(1,128)S(1)} %get-tuple-element.44.refs_6_), channel_id=1, source_target_pairs={{0,5},{1,4},{2,7},{3,6},{4,1},{5,0},{6,3},{7,2},{8,13},{9,12},{10,... | collective-permute-start | bytes 12296 | tf_op jit(solution)/shard_map/ppermute | solution.py:228
  63.7 6.6 %collective-permute-start.10 = (f32[4,1,256]{2,1,0:T(1,128)S(1)}, f32[4,1,256]{2,1,0:T(1,128)S(1)}, u32[]{:S(2)}, u32[]{:S(2)}) collective-permute-start(f32[4,1,256]{2,1,0:T(1,128)S(1)} %get-tuple-element.44.refs_6_), channel_id=1, source_target_pairs={{0,4},{1,5},{2,6},{3,7},{4,0},{5,1},{6,2},{7,3},{8,12},{9,13},{10,... | collective-permute-start | bytes 12296 | tf_op jit(solution)/shard_map/ppermute | solution.py:228
  64.9 5.3 %collective-permute-start.9 = (f32[4,1,256]{2,1,0:T(1,128)S(1)}, f32[4,1,256]{2,1,0:T(1,128)S(1)}, u32[]{:S(2)}, u32[]{:S(2)}) collective-permute-start(f32[4,1,256]{2,1,0:T(1,128)S(1)} %get-tuple-element.44.refs_6_), channel_id=1, source_target_pairs={{0,1},{1,0},{2,3},{3,2},{4,5},{5,4},{6,7},{7,6},{8,9},{9,8},{10,11... | collective-permute-start | bytes 12296 | tf_op jit(solution)/shard_map/ppermute | solution.py:228
  68.1 3.1 %collective-permute-start.17 = (f32[4,1,256]{2,1,0:T(1,128)S(1)}, f32[4,1,256]{2,1,0:T(1,128)S(1)}, u32[]{:S(2)}, u32[]{:S(2)}) collective-permute-start(f32[4,1,256]{2,1,0:T(1,128)S(1)} %get-tuple-element.50.refs_16_), channel_id=1, source_target_pairs={{0,5},{1,4},{2,7},{3,6},{4,1},{5,0},{6,3},{7,2},{8,13},{9,12},{10,... | collective-permute-start | bytes 12296 | tf_op jit(solution)/shard_map/ppermute | solution.py:228
  69.5 3.6 %collective-permute-start.16 = (f32[4,1,256]{2,1,0:T(1,128)S(1)}, f32[4,1,256]{2,1,0:T(1,128)S(1)}, u32[]{:S(2)}, u32[]{:S(2)}) collective-permute-start(f32[4,1,256]{2,1,0:T(1,128)S(1)} %get-tuple-element.50.refs_16_), channel_id=1, source_target_pairs={{0,4},{1,5},{2,6},{3,7},{4,0},{5,1},{6,2},{7,3},{8,12},{9,13},{10,... | collective-permute-start | bytes 12296 | tf_op jit(solution)/shard_map/ppermute | solution.py:228
  70.2 2.9 %collective-permute-start.15 = (f32[4,1,256]{2,1,0:T(1,128)S(1)}, f32[4,1,256]{2,1,0:T(1,128)S(1)}, u32[]{:S(2)}, u32[]{:S(2)}) collective-permute-start(f32[4,1,256]{2,1,0:T(1,128)S(1)} %get-tuple-element.50.refs_16_), channel_id=1, source_target_pairs={{0,1},{1,0},{2,3},{3,2},{4,5},{5,4},{6,7},{7,6},{8,9},{9,8},{10,11... | collective-permute-start | bytes 12296 | tf_op jit(solution)/shard_map/ppermute | solution.py:228
  75.6 6.7 %collective-permute-start.21 = (f32[136,256]{1,0:T(8,128)S(1)}, f32[136,256]{1,0:T(8,128)S(1)}, u32[]{:S(2)}, u32[]{:S(2)}) collective-permute-start(f32[136,256]{1,0:T(8,128)S(1)} %get-tuple-element.56), channel_id=1, source_target_pairs={{0,2},{1,3},{2,0},{3,1},{4,6},{5,7},{6,4},{7,5},{8,10},{9,11},{10,... | collective-permute-start | bytes 417800 | tf_op jit(solution)/shard_map/ppermute | solution.py:228
  77.3 19.3 %collective-permute-start.18 = (f32[264,256]{1,0:T(8,128)S(1)}, f32[264,256]{1,0:T(8,128)S(1)}, u32[]{:S(2)}, u32[]{:S(2)}) collective-permute-start(f32[264,256]{1,0:T(8,128)S(1)} %get-tuple-element.52), channel_id=1, source_target_pairs={{0,2},{1,3},{2,0},{3,1},{4,6},{5,7},{6,4},{7,5},{8,10},{9,11},{10,... | collective-permute-start | bytes 811016 | tf_op jit(solution)/shard_map/ppermute | solution.py:228
  77.7 11.5 %collective-permute-start.19 = (f32[128,256]{1,0:T(8,128)S(1)}, f32[128,256]{1,0:T(8,128)S(1)}, u32[]{:S(2)}, u32[]{:S(2)}) collective-permute-start(f32[128,256]{1,0:T(8,128)S(1)} %get-tuple-element.54), channel_id=1, source_target_pairs={{0,2},{1,3},{2,0},{3,1},{4,6},{5,7},{6,4},{7,5},{8,10},{9,11},{10,... | collective-permute-start | bytes 393224 | tf_op jit(solution)/shard_map/ppermute | solution.py:228
  82.3 14.4 %copy-start = (f32[256,256]{1,0:T(8,128)S(1)}, f32[256,256]{1,0:T(8,128)}, u32[]{:S(2)}) copy-start(f32[256,256]{1,0:T(8,128)} %refs_0_.5) | copy-start | bytes 786436
  82.3 14.4 %collective-permute-start.22 = (f32[136,256]{1,0:T(8,128)S(1)}, f32[136,256]{1,0:T(8,128)S(1)}, u32[]{:S(2)}, u32[]{:S(2)}) collective-permute-start(f32[136,256]{1,0:T(8,128)S(1)} %add.7), channel_id=1, source_target_pairs={{0,8},{1,9},{2,10},{3,11},{4,12},{5,13},{6,14},{7,15},{8,0},{9,1},... | collective-permute-start | bytes 417800 | tf_op jit(solution)/shard_map/ppermute | solution.py:228
  89.2 7.5 %copy-start.1 = (f32[256]{0:T(256)S(1)}, f32[256]{0:T(256)}, u32[]{:S(2)}) copy-start(f32[256]{0:T(256)} %param.19) | copy-start | bytes 3076
  89.2 7.5 %collective-permute-start.20 = (f32[128,256]{1,0:T(8,128)S(1)}, f32[128,256]{1,0:T(8,128)S(1)}, u32[]{:S(2)}, u32[]{:S(2)}) collective-permute-start(f32[128,256]{1,0:T(8,128)S(1)} %add.6), channel_id=1, source_target_pairs={{0,8},{1,9},{2,10},{3,11},{4,12},{5,13},{6,14},{7,15},{8,0},{9,1},... | collective-permute-start | bytes 393224 | tf_op jit(solution)/shard_map/ppermute | solution.py:228

commit v4 on v3

--- a/solution.py
+++ b/solution.py
@@ -74,18 +74,21 @@
     return x + dot3(split(sums / totals), w_out)
 
 
-def first_kernel(video, gain, w_qkv, w_out, sums, counts, codes_ref, out_ref, *scratch):
-    refs, sem = scratch[:-1], scratch[-1]
-    sources = (sums, counts, video, gain, w_qkv, w_out)
-    copies = [pltpu.make_async_copy(a, b, sem.at[i]) for i, (a, b) in enumerate(zip(sources, refs))]
-    for copy in copies:
+def first_kernel(*refs, names):
+    sources = dict(zip(names, refs))
+    codes_ref, out_ref, start_ref, gain_ref, *weight_refs = refs[len(names) : -len(names) - 1]
+    held, sem = dict(zip(names, refs[-len(names) - 1 : -1])), refs[-1]
+    copies = {n: pltpu.make_async_copy(sources[n], held[n], sem.at[i]) for i, n in enumerate(names)}
+    for copy in copies.values():
         copy.start()
-    for copy in copies[:2]:
-        copy.wait()
-    sums, counts, x, gain, w_qkv, w_out = refs
-    code_kernel(sums, counts, codes_ref)
-    for copy in copies[2:]:
-        copy.wait()
+
+    def take(*wanted):
+        for n in wanted:
+            copies[n].wait()
+        return [held[n] for n in wanted]
+
+    code_kernel(*take("code_sums", "code_counts"), codes_ref)
+    x, gain, w_qkv, w_out = take("video", "gain_space", "qkv_space", "out_space")
     clips, local_frames = x.shape[:2]
     places, width = out_ref.shape[2:]
     w_qkv, w_out = split(w_qkv[...]), split(w_out[...])
@@ -93,22 +96,34 @@
         for f in range(local_frames):
             y = attend(x[c, f], gain[...], w_qkv, w_out, None)
             out_ref[:, c * local_frames + f] = y.reshape(-1, places, width)
-
-
-def time_kernel(start_ref, x_ref, gain_ref, w_qkv_ref, w_out_ref, *rest, clip):
-    latents_ref, unit_ref = rest[-2:]
+    start, gain, w_qkv, w_out = take("clip_start", "gain_time", "qkv_time", "out_time")
+    for c in range(clips):
+        start_ref[c] = jnp.full(start_ref.shape[1:], start[c], jnp.int32)
+    gain_ref[...] = gain[...]
+    for ref, part in zip(weight_refs, split(w_qkv[...]) + split(w_out[...])):
+        ref[...] = part
+
+
+def time_kernel(start_ref, x_ref, gain_ref, *refs, clip):
+    weights, (latents_ref, unit_ref) = [ref[...] for ref in refs[:4]], refs[-2:]
     senders, _, local_frames, places, width = x_ref.shape
     tokens = senders * local_frames * places
-    x = x_ref[...].reshape(tokens, width)
+    x = x_ref[:, clip].reshape(tokens, width)
     row = lax.broadcasted_iota(jnp.int32, (tokens, 1), 0)
     col = lax.broadcasted_iota(jnp.int32, (1, tokens), 1)
     later, earlier = row // places, col // places
     mask = ((row - later * places) == (col - earlier * places)) & (
-        (earlier == later) | ((earlier < later) & (earlier >= start_ref[clip]))
+        (earlier == later) | ((earlier < later) & (earlier >= start_ref[clip, :1, :1]))
     )
-    y = attend(x, gain_ref[...], split(w_qkv_ref[...]), split(w_out_ref[...]), mask)
-    latents_ref[...] = y.reshape(latents_ref.shape)
+    y = attend(x, gain_ref[...], weights[:2], weights[2:], mask)
     unit_ref[...] = y * lax.rsqrt(jnp.sum(y * y, -1, keepdims=True) + EPSILON)
+    for i, ref in enumerate(refs[4:-2]):
+        latents_ref[i] = ref[...]
+    y = y.reshape(latents_ref.shape[-3:])
+    if latents_ref.ndim == 4:
+        latents_ref[clip] = y
+    else:
+        latents_ref[...] = y
 
 
 def column(row, lanes):
@@ -139,7 +154,7 @@
         totals_ref[before + j] = totals
 
 
-def term_kernel(*refs, blocks, clips):
+def term_kernel(*refs, blocks, clips, which):
     each = 2 + 2 * SHARERS
     out_refs = refs[each * clips :]
     width = refs[2].shape[1]
@@ -161,8 +176,8 @@
             pair = jnp.where(index == 0, high.astype(F32), jnp.where(index == 1, low.astype(F32), 0.0))
             shares.append(pair.astype(BF16))
             ws.append((near, far)[j // 2].at[j % 2])
-    for r in reversed(range(blocks)):
-        pieces = out_refs[:1] if r == 0 else out_refs[1:2] if r == 1 else out_refs[2 * r - 2 : 2 * r]
+    for r in which:
+        pieces, out_refs = out_refs[: 1 + (r > 1)], out_refs[1 + (r > 1) :]
         sums = jnp.zeros((rows, width), F32)
         counts = jnp.zeros((16, rows), F32)
         for w_ref, unit, share in zip(ws, scaled, shares):
@@ -248,65 +263,77 @@
         counts_row = code_counts[None]
 
         hbm = pl.BlockSpec(memory_space=pltpu.HBM)
-        operands = (video, gain_space, qkv_space, out_space, code_sums, counts_row)
-        held = (code_sums, counts_row, video, gain_space, qkv_space, out_space)
-        codes, spaced = pl.pallas_call(
-            first_kernel,
+        operands = {
+            "code_sums": code_sums,
+            "code_counts": counts_row,
+            "video": video,
+            "gain_space": gain_space,
+            "qkv_space": qkv_space,
+            "out_space": out_space,
+            "clip_start": clip_start,
+            "gain_time": gain_time,
+            "qkv_time": qkv_time,
+            "out_time": out_time,
+        }
+        codes, spaced, *time_operands = pl.pallas_call(
+            lambda *refs: first_kernel(*refs, names=list(operands)),
             in_specs=[hbm] * len(operands),
-            out_shape=[shape(code_rows, width), shape(devices, clips * local_frames, places, width)],
-            scratch_shapes=[pltpu.VMEM(a.shape, a.dtype) for a in held]
-            + [pltpu.SemaphoreType.DMA((len(held),))],
+            out_shape=[
+                shape(code_rows, width),
+                shape(devices, clips * local_frames, places, width),
+                shape(clips, 8, 128, dtype=jnp.int32),
+                shape(1, width),
+            ]
+            + [shape(*w.shape, dtype=BF16) for w in (qkv_time, qkv_time, out_time, out_time)],
+            scratch_shapes=[
+                (pltpu.SMEM if name == "clip_start" else pltpu.VMEM)(a.shape, a.dtype)
+                for name, a in operands.items()
+            ]
+            + [pltpu.SemaphoreType.DMA((len(operands),))],
             compiler_params=params(FIRST_VMEM_BYTES),
-            cost_estimate=cost(clips * 2e9, *held),
+            cost_estimate=cost(clips * 2e9, *operands.values()),
             name="first_space",
-        )(*operands)
-
-        by_place = lax.all_to_all(spaced, "frames", split_axis=0, concat_axis=0, tiled=True)
-        codes, by_place = lax.optimization_barrier((codes, by_place))
-        by_place = by_place.reshape(devices, clips, local_frames, places, width)
-
-        half = code_rows // 2
-        halves = {0: [codes[:half], codes[half:]]}
+        )(*operands.values())
+        start, gain, *weights = time_operands
+
+        code_blocks = {0: codes}
         for bit in reversed(range((blocks - 1).bit_length())):
             step = 1 << bit
-            halves |= {r ^ step: [swap(part, block_bits[step]) for part in block] for r, block in halves.items()}
-        code_blocks = [part for r in range(blocks) for part in halves[r]]
-
-        latents = None
+            code_blocks |= {r ^ step: swap(block, block_bits[step]) for r, block in code_blocks.items()}
+
+        by_place = lax.all_to_all(spaced, "frames", split_axis=0, concat_axis=0, tiled=True)
+        if blocks > 2:
+            by_place, code_blocks[2] = lax.optimization_barrier((by_place, code_blocks[2]))
+        by_place = by_place.reshape(devices, clips, local_frames, places, width)
+        code_blocks = [code_blocks[r] for r in range(blocks)]
+
+        latents = []
         units = []
         for c in range(clips):
-            before = [] if latents is None else [latents]
-            latents, unit = pl.pallas_call(
+            last = c == clips - 1
+            of_clip, unit = simple_call(
                 lambda *refs, c=c: time_kernel(*refs, clip=c),
-                grid=(1,),
-                in_specs=[
-                    pl.BlockSpec(memory_space=pltpu.SMEM),
-                    pl.BlockSpec((devices, 1, local_frames, places, width), lambda i, c=c: (0, c, 0, 0, 0)),
-                    whole(gain_time),
-                    whole(qkv_time),
-                    whole(out_time),
-                ]
-                + [pl.BlockSpec(memory_space=pl.ANY)] * len(before),
-                out_specs=(
-                    pl.BlockSpec((1, frames, places, width), lambda i, c=c: (c, 0, 0, 0)),
-                    pl.BlockSpec((tokens, width), lambda i: (0, 0)),
-                ),
-                out_shape=(shape(clips, frames, places, width), shape(tokens, width)),
-                input_output_aliases={5: 0} if before else {},
-                compiler_params=params(),
-                cost_estimate=cost(2e9, *held),
+                (shape(*([clips] * last), frames, places, width), shape(tokens, width)),
+                start,
+                by_place,
+                gain,
+                *weights,
+                *(latents if last else []),
+                flops=2e9,
                 name="time_attention",
-            )(clip_start, by_place, gain_time, qkv_time, out_time, *before)
+            )
+            latents.append(of_clip)
 
             if units:
                 unit, units[-1][2] = lax.optimization_barrier((unit, units[-1][2]))
             far = swap(unit, sharer_bits[2])
             units.append([unit, swap(unit, 1), far, swap(far, 1)])
+        latents = latents[-1]
 
         def score(chunk_units, *before):
             n, m = len(chunk_units), len(before) * 2
             return simple_call(
-                lambda *refs: score_kernel(*refs, blocks=2 * blocks, chunks=n, before=m),
+                lambda *refs: score_kernel(*refs, blocks=blocks, chunks=n, before=m),
                 (shape(n, blocks * code_rows, tokens, dtype=BF16), shape(m + n, 1, tokens)),
                 *code_blocks,
                 *chunk_units,
@@ -325,25 +352,36 @@
             operands += [swap(clip_totals, sharer_bits[m]) for m in range(1, sharers)]
 
         half = code_rows // 2
-        one, two = [shape(code_rows + 8, width)], [shape(half, width), shape(code_rows + 8 - half, width)]
-        terms = simple_call(
-            lambda *refs: term_kernel(*refs, blocks=blocks, clips=clips),
-            one * 2 + two * (blocks - 2),
-            *operands,
-            flops=2 * sharers * blocks * code_rows * clips * tokens * width,
-            name="terms",
-        )
-        terms = [[terms[0]], [terms[1]]] + [list(terms[2 * r - 2 : 2 * r]) for r in range(2, blocks)]
-
-        arrivals = [terms[0]]
+        whole_term, pieces = [shape(code_rows + 8, width)], [shape(half, width), shape(code_rows + 8 - half, width)]
+        terms = {}
+        for which in ([blocks - 1], list(reversed(range(blocks - 1)))):
+            made = simple_call(
+                lambda *refs, which=which: term_kernel(*refs, blocks=blocks, clips=clips, which=which),
+                [a for r in which for a in (pieces if r > 1 else whole_term)],
+                *operands,
+                flops=2 * sharers * len(which) * code_rows * clips * tokens * width,
+                name="terms",
+            )
+            for r in which:
+                terms[r], made = list(made[: 1 + (r > 1)]), made[1 + (r > 1) :]
+
+        arrivals = []
         for bit in range((blocks - 1).bit_length()):
             step = 1 << bit
+            ahead = None
             for r in reversed(range(step, blocks, 2 * step)):
-                came = [swap(piece, block_bits[step]) for piece in terms[r]]
+                came = []
+                for piece in terms[r]:
+                    if ahead is not None:
+                        piece, ahead, terms[0][0] = lax.optimization_barrier((piece, ahead, terms[0][0]))
+                        came[-1:] = [ahead] if came else []
+                    ahead = swap(piece, block_bits[step])
+                    came.append(ahead)
                 if r == step:
                     arrivals.append(came)
                 else:
                     terms[r - step] = [a + b for a, b in zip(terms[r - step], came)]
+        arrivals.insert(0, terms[0])
         new_sums, new_counts, new_codebook = simple_call(
             lambda *refs: update_kernel(*refs, arrivals=[len(pieces) for pieces in arrivals]),
             (shape(code_rows, width), shape(1, code_rows), shape(code_rows, width)),

time: 97.8 us -> 95.7 us (0.979)
  blocking collectives: 22 us -> 0 us
  waiting for transfers between devices: 29.5 us -> 48.5 us
  Pallas kernels: 23.2 us -> 19.3 us
  starting transfers between devices: 21.3 us -> 24.3 us
  local copies, waits for them, and re-layouts: 0.72 us -> 2.49 us
    all_to_all x1 -> x0, blocking collectives: 22 us -> none  [local(): lax.all_to_all(spaced, 'frames', split_axis=0, concat_axis=0, tiled=True)]
    ppermute x23 -> x20, waiting for transfers between devices: 29.5 us -> 48.5 us  [swap(): return lax.ppermute(x, 'frames', [(i, i ^ bits) for i in range(devices)])]
    all_to_all x0 -> x1, starting transfers between devices: none -> 7.53 us  [local(): lax.all_to_all(spaced, 'frames', split_axis=0, concat_axis=0, tiled=True)]
    pallas_call x3 -> x1, Pallas kernels: 13.7 us -> 6.99 us  [local(): pl.pallas_call(lambda *refs: first_kernel(*refs, names=list(operands)), i...]
    ppermute x23 -> x20, starting transfers between devices: 21.3 us -> 16.7 us  [swap(): return lax.ppermute(x, 'frames', [(i, i ^ bits) for i in range(devices)])]
    pallas_call x6 -> x9, Pallas kernels: 9.51 us -> 12.3 us  [simple_call(): pl.pallas_call(kernel, out_shape=outs, compiler_params=params(), cost_est...]
    unnamed x14 -> x18, local copies, waits for them, and re-layouts: 0.7 us -> 2.49 us
  transfers between devices with their start and end apart: 23 -> 21, of which waited for: 10 -> 10; matrix products, arithmetic and copies ran while one was open for 0% -> 0% of each run, Pallas kernels for 10% -> 9%
where the time goes in v4:
time: 95.7 us; the launch traced here: 95.3 us
  waiting for transfers between devices  48.5 us (51%)
  starting transfers between devices  24.3 us (25%)
  Pallas kernels  19.3 us (20%)
  local copies, waits for them, and re-layouts  2.49 us (3%)
    ppermute x20, waiting for transfers between devices, swap(): return lax.ppermute(x, 'frames', [(i, i ^ bits) for i in range(devices)])  48.5 us
    ppermute x20, starting transfers between devices, swap(): return lax.ppermute(x, 'frames', [(i, i ^ bits) for i in range(devices)])  16.7 us
    pallas_call x9, Pallas kernels, simple_call(): pl.pallas_call(kernel, out_shape=outs, compiler_params=params(), cost_est...  12.3 us
    all_to_all x1, starting transfers between devices, local(): lax.all_to_all(spaced, 'frames', split_axis=0, concat_axis=0, tiled=True)  7.53 us
    pallas_call x1, Pallas kernels, local(): pl.pallas_call(lambda *refs: first_kernel(*refs, names=list(operands)), i...  6.99 us
    unnamed x18, local copies, waits for them, and re-layouts  2.49 us
  transfers between devices with their start and end apart: 21, of which 10 were waited for; matrix products, arithmetic and copies ran while one was open for 0% of the time, Pallas kernels for 9%

profile of v4, /device:TPU:0, one launch (start us, length us, event | category | flops | bytes accessed | tf_op | source)
XLA Modules:
  0.0 95.3 jit_solution(4655222906093446600)
XLA Ops:
  0.6 7.0 %first_space.1 = (f32[256,256]{1,0:T(8,128)}, f32[16,2,16,256]{3,2,1,0:T(8,128)}, s32[2,8,128]{2,1,0:T(8,128)}, f32[1,256]{1,0:T(1,128)}, bf16[256,768]{1,0:T(8,...) custom-call(f32[256,256]{1,0:T(8,128)} %refs_0_.3, f32[1,256]{1,0:T(1,128)} %bitcast.7, ...), custom_call_target="tpu_custom_call" | custom-call | flops 4000000000 | bytes 2886664 | tf_op jit(solution)/shard_map/first_space/pallas_call | solution.py:278
  7.7 7.5 %all-to-all-start = ((f32[16,2,16,256]{3,2,1,0:T(8,128)}), f32[16,2,16,256]{3,2,1,0:T(8,128)S(1)}, u32[]{:S(2)}, u32[]{:S(2)}) async-start(f32[16,2,16,256]{3,2,1,0:T(8,128)} %get-tuple-element.47), calls=%async_computation | async-start | bytes 1048576 | tf_op jit(solution)/shard_map/all_to_all | solution.py:304
  15.2 2.9 %collective-permute-start = (f32[256,256]{1,0:T(8,128)S(1)}, f32[256,256]{1,0:T(8,128)S(1)}, u32[]{:S(2)}, u32[]{:S(2)}) collective-permute-start(f32[256,256]{1,0:T(8,128)S(1)} %copy-done.2), channel_id=1, source_target_pairs={{0,8},{1,9},{2,10},{3,11},{4,12},{5,13},{6,14},{7,15},{8,0},{9,1},... | collective-permute-start | bytes 786440 | tf_op jit(solution)/shard_map/ppermute | solution.py:243
  18.1 23.6 %collective-permute-done.refs_2_ = f32[256,256]{1,0:T(8,128)S(1)} collective-permute-done((f32[256,256]{1,0:T(8,128)S(1)}, f32[256,256]{1,0:T(8,128)S(1)}, u32[]{:S(2)}, u32[]{:S(2)}) %collective-permute-start) | collective-permute-done | bytes 262176 | tf_op jit(solution)/shard_map/ppermute | solution.py:243
  42.4 0.9 copy-done.5
  43.3 0.9 copy-done.6
  44.2 2.4 %time_attention.2 = (f32[16,16,256]{2,1,0:T(8,128)S(1)}, f32[256,256]{1,0:T(8,128)S(1)}) custom-call(s32[2,8,128]{2,1,0:T(8,128)S(1)} %copy-done.7, f32[16,2,1,16,256]{4,3,2,1,0:T(8,128)S(1)} %bitcast.5, f32[1,256]{1,0:T(1,128)S(1)} %copy-done.8, bf16[256,768]{1,0:T(8,128)(2,1)S(1)} %copy-done.3, bf16[256,768]{1,0:T(8,128)(2,1)S(1)} %copy-done.4, ...), custom_call_target="tpu_custom_call" | custom-call | flops 2000000000 | bytes 2106368 | tf_op jit(solution)/shard_map/time_attention/pallas_call | solution.py:228
  46.7 1.5 %collective-permute-start.1 = (f32[256,256]{1,0:T(8,128)S(1)}, f32[256,256]{1,0:T(8,128)S(1)}, u32[]{:S(2)}, u32[]{:S(2)}) collective-permute-start(f32[256,256]{1,0:T(8,128)S(1)} %copy-done.2), channel_id=1, source_target_pairs={{0,2},{1,3},{2,0},{3,1},{4,6},{5,7},{6,4},{7,5},{8,10},{9,11},{10,... | collective-permute-start | bytes 786440 | tf_op jit(solution)/shard_map/ppermute | solution.py:243
  48.2 3.2 %time_attention.3 = (f32[2,16,16,256]{3,2,1,0:T(8,128)}, f32[256,256]{1,0:T(8,128)S(1)}) custom-call(s32[2,8,128]{2,1,0:T(8,128)S(1)} %copy-done.7, f32[16,2,1,16,256]{4,3,2,1,0:T(8,128)S(1)} %bitcast.6, f32[1,256]{1,0:T(1,128)S(1)} %copy-done.8, bf16[256,768]{1,0:T(8,128)(2,1)S(1)} %copy-done.3, bf16[256,768]{1,0:T(8,128)(2,1)S(1)} %copy-done.4, ...), custom_call_target="tpu_custom_call" | custom-call | flops 2000000000 | bytes 2630656 | tf_op jit(solution)/shard_map/time_attention/pallas_call | solution.py:228
  51.4 3.1 %collective-permute-done.4.refs_4_ = f32[256,256]{1,0:T(8,128)S(1)} collective-permute-done((f32[256,256]{1,0:T(8,128)S(1)}, f32[256,256]{1,0:T(8,128)S(1)}, u32[]{:S(2)}, u32[]{:S(2)}) %collective-permute-start.4) | collective-permute-done | bytes 262176 | tf_op jit(solution)/shard_map/ppermute | solution.py:243
  54.8 1.5 %collective-permute-start.2 = (f32[256,256]{1,0:T(8,128)S(1)}, f32[256,256]{1,0:T(8,128)S(1)}, u32[]{:S(2)}, u32[]{:S(2)}) collective-permute-start(f32[256,256]{1,0:T(8,128)S(1)} %collective-permute-done.refs_2_), channel_id=1, source_target_pairs={{0,2},{1,3},{2,0},{3,1},{4,6},{5,7},{6,4},{7,5},{8,10},{9,11},{10,... | collective-permute-start | bytes 786440 | tf_op jit(solution)/shard_map/ppermute | solution.py:243
  56.8 4.7 %collective-permute-done.10.refs_4_.refs_14_ = f32[256,256]{1,0:T(8,128)S(1)} collective-permute-done((f32[256,256]{1,0:T(8,128)S(1)}, f32[256,256]{1,0:T(8,128)S(1)}, u32[]{:S(2)}, u32[]{:S(2)}) %collective-permute-start.10) | collective-permute-done | bytes 262176 | tf_op jit(solution)/shard_map/ppermute | solution.py:243
  61.8 0.8 scores.4
  62.6 0.8 scores.5
  63.9 1.4 %collective-permute-start.7 = (f32[4,1,256]{2,1,0:T(1,128)S(1)}, f32[4,1,256]{2,1,0:T(1,128)S(1)}, u32[]{:S(2)}, u32[]{:S(2)}) collective-permute-start(f32[4,1,256]{2,1,0:T(1,128)S(1)} %get-tuple-element.64.refs_6_), channel_id=1, source_target_pairs={{0,4},{1,5},{2,6},{3,7},{4,0},{5,1},{6,2},{7,3},{8,12},{9,13},{10,... | collective-permute-start | bytes 12296 | tf_op jit(solution)/shard_map/ppermute | solution.py:243
  65.3 0.8 scores.6
  66.2 0.8 scores.7
  66.9 1.1 %collective-permute-start.14 = (f32[4,1,256]{2,1,0:T(1,128)S(1)}, f32[4,1,256]{2,1,0:T(1,128)S(1)}, u32[]{:S(2)}, u32[]{:S(2)}) collective-permute-start(f32[4,1,256]{2,1,0:T(1,128)S(1)} %get-tuple-element.70.refs_16_), channel_id=1, source_target_pairs={{0,5},{1,4},{2,7},{3,6},{4,1},{5,0},{6,3},{7,2},{8,13},{9,12},{10,... | collective-permute-start | bytes 12296 | tf_op jit(solution)/shard_map/ppermute | solution.py:243
  68.0 1.1 %collective-permute-start.13 = (f32[4,1,256]{2,1,0:T(1,128)S(1)}, f32[4,1,256]{2,1,0:T(1,128)S(1)}, u32[]{:S(2)}, u32[]{:S(2)}) collective-permute-start(f32[4,1,256]{2,1,0:T(1,128)S(1)} %get-tuple-element.70.refs_16_), channel_id=1, source_target_pairs={{0,4},{1,5},{2,6},{3,7},{4,0},{5,1},{6,2},{7,3},{8,12},{9,13},{10,... | collective-permute-start | bytes 12296 | tf_op jit(solution)/shard_map/ppermute | solution.py:243
  69.1 0.9 collective-permute-done.14.refs_19_
  70.0 1.6 %collective-permute-done.13.refs_18_ = f32[4,1,256]{2,1,0:T(1,128)S(1)} collective-permute-done((f32[4,1,256]{2,1,0:T(1,128)S(1)}, f32[4,1,256]{2,1,0:T(1,128)S(1)}, u32[]{:S(2)}, u32[]{:S(2)}) %collective-permute-start.13) | collective-permute-done | bytes 4128 | tf_op jit(solution)/shard_map/ppermute | solution.py:243
  71.7 0.8 terms.3
  72.4 1.6 %collective-permute-start.15 = (f32[128,256]{1,0:T(8,128)S(1)}, f32[128,256]{1,0:T(8,128)S(1)}, u32[]{:S(2)}, u32[]{:S(2)}) collective-permute-start(f32[128,256]{1,0:T(8,128)S(1)} %get-tuple-element.73), channel_id=1, source_target_pairs={{0,2},{1,3},{2,0},{3,1},{4,6},{5,7},{6,4},{7,5},{8,10},{9,11},{10,... | collective-permute-start | bytes 393224 | tf_op jit(solution)/shard_map/ppermute | solution.py:243
  74.0 1.9 %terms.2 = (f32[128,256]{1,0:T(8,128)S(1)}, f32[136,256]{1,0:T(8,128)S(1)}, f32[264,256]{1,0:T(8,128)S(1)}, f32[264,256]{1,0:T(8,128)S(1)}) custom-call(bf16[2,1024,256]{2,1,0:T(8,128)(2,1)S(1)} %get-tuple-element.59.refs_0_, bf16[2,1024,256]{2,1,0:T(8,128)(2,1)S(1)} %get-tuple-element.63.refs_1_, f32[256,256]{1,0:T(8,128)S(1)} %get-tuple-element.58.refs_4_.refs_2_, ...), custom_call_target="tpu_custom_call" | custom-call | flops 805306368 | bytes 7135232 | tf_op jit(solution)/shard_map/terms/pallas_call | solution.py:228
  75.9 1.6 %collective-permute-done.15 = f32[128,256]{1,0:T(8,128)S(1)} collective-permute-done((f32[128,256]{1,0:T(8,128)S(1)}, f32[128,256]{1,0:T(8,128)S(1)}, u32[]{:S(2)}, u32[]{:S(2)}) %collective-permute-start.15) | collective-permute-done | bytes 131104 | tf_op jit(solution)/shard_map/ppermute | solution.py:243
  77.5 1.5 %collective-permute-start.16 = (f32[136,256]{1,0:T(8,128)S(1)}, f32[136,256]{1,0:T(8,128)S(1)}, u32[]{:S(2)}, u32[]{:S(2)}) collective-permute-start(f32[136,256]{1,0:T(8,128)S(1)} %get-tuple-element.75), channel_id=1, source_target_pairs={{0,2},{1,3},{2,0},{3,1},{4,6},{5,7},{6,4},{7,5},{8,10},{9,11},{10,... | collective-permute-start | bytes 417800 | tf_op jit(solution)/shard_map/ppermute | solution.py:243
  79.0 1.3 %collective-permute-start.17 = (f32[128,256]{1,0:T(8,128)S(1)}, f32[128,256]{1,0:T(8,128)S(1)}, u32[]{:S(2)}, u32[]{:S(2)}) collective-permute-start(f32[128,256]{1,0:T(8,128)S(1)} %add.7), channel_id=1, source_target_pairs={{0,8},{1,9},{2,10},{3,11},{4,12},{5,13},{6,14},{7,15},{8,0},{9,1},... | collective-permute-start | bytes 393224 | tf_op jit(solution)/shard_map/ppermute | solution.py:243
  80.3 2.5 %collective-permute-done.16 = f32[136,256]{1,0:T(8,128)S(1)} collective-permute-done((f32[136,256]{1,0:T(8,128)S(1)}, f32[136,256]{1,0:T(8,128)S(1)}, u32[]{:S(2)}, u32[]{:S(2)}) %collective-permute-start.16) | collective-permute-done | bytes 139296 | tf_op jit(solution)/shard_map/ppermute | solution.py:243
  82.9 1.5 %collective-permute-start.18 = (f32[264,256]{1,0:T(8,128)S(1)}, f32[264,256]{1,0:T(8,128)S(1)}, u32[]{:S(2)}, u32[]{:S(2)}) collective-permute-start(f32[264,256]{1,0:T(8,128)S(1)} %get-tuple-element.82), channel_id=1, source_target_pairs={{0,2},{1,3},{2,0},{3,1},{4,6},{5,7},{6,4},{7,5},{8,10},{9,11},{10,... | collective-permute-start | bytes 811016 | tf_op jit(solution)/shard_map/ppermute | solution.py:243
  84.4 4.1 %collective-permute-done.17.refs_4_ = f32[128,256]{1,0:T(8,128)S(1)} collective-permute-done((f32[128,256]{1,0:T(8,128)S(1)}, f32[128,256]{1,0:T(8,128)S(1)}, u32[]{:S(2)}, u32[]{:S(2)}) %collective-permute-start.17) | collective-permute-done | bytes 131104 | tf_op jit(solution)/shard_map/ppermute | solution.py:243
  88.5 6.0 %collective-permute-done.19.refs_5_ = f32[136,256]{1,0:T(8,128)S(1)} collective-permute-done((f32[136,256]{1,0:T(8,128)S(1)}, f32[136,256]{1,0:T(8,128)S(1)}, u32[]{:S(2)}, u32[]{:S(2)}) %collective-permute-start.19) | collective-permute-done | bytes 139296 | tf_op jit(solution)/shard_map/ppermute | solution.py:243
  94.5 0.9 update.1
  (40 shorter events, 2.5 us)
Async XLA Ops:
  7.6 7.6 %copy-start.2 = (f32[256,256]{1,0:T(8,128)S(1)}, f32[256,256]{1,0:T(8,128)}, u32[]{:S(2)}) copy-start(f32[256,256]{1,0:T(8,128)} %get-tuple-element.48.refs_0_) | copy-start | bytes 786436
  7.6 34.1 %copy-start.3 = (bf16[256,768]{1,0:T(8,128)(2,1)S(1)}, bf16[256,768]{1,0:T(8,128)(2,1)}, u32[]{:S(2)}) copy-start(bf16[256,768]{1,0:T(8,128)(2,1)} %get-tuple-element.51.refs_3_) | copy-start | bytes 1179652
  7.7 34.1 %copy-start.4 = (bf16[256,768]{1,0:T(8,128)(2,1)S(1)}, bf16[256,768]{1,0:T(8,128)(2,1)}, u32[]{:S(2)}) copy-start(bf16[256,768]{1,0:T(8,128)(2,1)} %get-tuple-element.52.refs_4_) | copy-start | bytes 1179652
  7.7 34.1 %all-to-all-start = ((f32[16,2,16,256]{3,2,1,0:T(8,128)}), f32[16,2,16,256]{3,2,1,0:T(8,128)S(1)}, u32[]{:S(2)}, u32[]{:S(2)}) async-start(f32[16,2,16,256]{3,2,1,0:T(8,128)} %get-tuple-element.47), calls=%async_computation | async-start | bytes 1048576 | tf_op jit(solution)/shard_map/all_to_all | solution.py:304
  15.2 26.5 %copy-start.7 = (s32[2,8,128]{2,1,0:T(8,128)S(1)}, s32[2,8,128]{2,1,0:T(8,128)}, u32[]{:S(2)}) copy-start(s32[2,8,128]{2,1,0:T(8,128)} %get-tuple-element.46.refs_0_) | copy-start | bytes 24580
  15.2 26.5 %collective-permute-start = (f32[256,256]{1,0:T(8,128)S(1)}, f32[256,256]{1,0:T(8,128)S(1)}, u32[]{:S(2)}, u32[]{:S(2)}) collective-permute-start(f32[256,256]{1,0:T(8,128)S(1)} %copy-done.2), channel_id=1, source_target_pairs={{0,8},{1,9},{2,10},{3,11},{4,12},{5,13},{6,14},{7,15},{8,0},{9,1},... | collective-permute-start | bytes 786440 | tf_op jit(solution)/shard_map/ppermute | solution.py:243
  41.7 0.7 copy-start.8
  42.4 0.9 copy-start.5
  43.3 0.9 copy-start.6
  46.6 7.9 %collective-permute-start.4 = (f32[256,256]{1,0:T(8,128)S(1)}, f32[256,256]{1,0:T(8,128)S(1)}, u32[]{:S(2)}, u32[]{:S(2)}) collective-permute-start(f32[256,256]{1,0:T(8,128)S(1)} %get-tuple-element.58.refs_4_.refs_2_), channel_id=1, source_target_pairs={{0,4},{1,5},{2,6},{3,7},{4,0},{5,1},{6,2},{7,3},{8,12},{9,13},{10,... | collective-permute-start | bytes 786440 | tf_op jit(solution)/shard_map/ppermute | solution.py:243
  46.7 10.1 %collective-permute-start.1 = (f32[256,256]{1,0:T(8,128)S(1)}, f32[256,256]{1,0:T(8,128)S(1)}, u32[]{:S(2)}, u32[]{:S(2)}) collective-permute-start(f32[256,256]{1,0:T(8,128)S(1)} %copy-done.2), channel_id=1, source_target_pairs={{0,2},{1,3},{2,0},{3,1},{4,6},{5,7},{6,4},{7,5},{8,10},{9,11},{10,... | collective-permute-start | bytes 786440 | tf_op jit(solution)/shard_map/ppermute | solution.py:243
  54.5 6.9 %collective-permute-start.10 = (f32[256,256]{1,0:T(8,128)S(1)}, f32[256,256]{1,0:T(8,128)S(1)}, u32[]{:S(2)}, u32[]{:S(2)}) collective-permute-start(f32[256,256]{1,0:T(8,128)S(1)} %get-tuple-element.65.refs_4_.refs_12_), channel_id=1, source_target_pairs={{0,4},{1,5},{2,6},{3,7},{4,0},{5,1},{6,2},{7,3},{8,12},{9,13},{10,... | collective-permute-start | bytes 786440 | tf_op jit(solution)/shard_map/ppermute | solution.py:243
  54.8 7.0 %collective-permute-start.2 = (f32[256,256]{1,0:T(8,128)S(1)}, f32[256,256]{1,0:T(8,128)S(1)}, u32[]{:S(2)}, u32[]{:S(2)}) collective-permute-start(f32[256,256]{1,0:T(8,128)S(1)} %collective-permute-done.refs_2_), channel_id=1, source_target_pairs={{0,2},{1,3},{2,0},{3,1},{4,6},{5,7},{6,4},{7,5},{8,10},{9,11},{10,... | collective-permute-start | bytes 786440 | tf_op jit(solution)/shard_map/ppermute | solution.py:243
  56.3 5.5 %collective-permute-start.3 = (f32[256,256]{1,0:T(8,128)S(1)}, f32[256,256]{1,0:T(8,128)S(1)}, u32[]{:S(2)}, u32[]{:S(2)}) collective-permute-start(f32[256,256]{1,0:T(8,128)S(1)} %get-tuple-element.58.refs_4_.refs_2_), channel_id=1, source_target_pairs={{0,1},{1,0},{2,3},{3,2},{4,5},{5,4},{6,7},{7,6},{8,9},{9,8},{10,11... | collective-permute-start | bytes 786440 | tf_op jit(solution)/shard_map/ppermute | solution.py:243
  56.3 6.3 %collective-permute-start.5 = (f32[256,256]{1,0:T(8,128)S(1)}, f32[256,256]{1,0:T(8,128)S(1)}, u32[]{:S(2)}, u32[]{:S(2)}) collective-permute-start(f32[256,256]{1,0:T(8,128)S(1)} %collective-permute-done.4.refs_4_), channel_id=1, source_target_pairs={{0,1},{1,0},{2,3},{3,2},{4,5},{5,4},{6,7},{7,6},{8,9},{9,8},{10,11... | collective-permute-start | bytes 786440 | tf_op jit(solution)/shard_map/ppermute | solution.py:243
  56.8 8.5 %collective-permute-start.9 = (f32[256,256]{1,0:T(8,128)S(1)}, f32[256,256]{1,0:T(8,128)S(1)}, u32[]{:S(2)}, u32[]{:S(2)}) collective-permute-start(f32[256,256]{1,0:T(8,128)S(1)} %get-tuple-element.65.refs_4_.refs_12_), channel_id=1, source_target_pairs={{0,1},{1,0},{2,3},{3,2},{4,5},{5,4},{6,7},{7,6},{8,9},{9,8},{10,11... | collective-permute-start | bytes 786440 | tf_op jit(solution)/shard_map/ppermute | solution.py:243
  61.5 4.7 %collective-permute-start.11 = (f32[256,256]{1,0:T(8,128)S(1)}, f32[256,256]{1,0:T(8,128)S(1)}, u32[]{:S(2)}, u32[]{:S(2)}) collective-permute-start(f32[256,256]{1,0:T(8,128)S(1)} %collective-permute-done.10.refs_4_.refs_14_), channel_id=1, source_target_pairs={{0,1},{1,0},{2,3},{3,2},{4,5},{5,4},{6,7},{7,6},{8,9},{9,8},{10,11... | collective-permute-start | bytes 786440 | tf_op jit(solution)/shard_map/ppermute | solution.py:243
  63.4 5.7 %collective-permute-start.8 = (f32[4,1,256]{2,1,0:T(1,128)S(1)}, f32[4,1,256]{2,1,0:T(1,128)S(1)}, u32[]{:S(2)}, u32[]{:S(2)}) collective-permute-start(f32[4,1,256]{2,1,0:T(1,128)S(1)} %get-tuple-element.64.refs_6_), channel_id=1, source_target_pairs={{0,5},{1,4},{2,7},{3,6},{4,1},{5,0},{6,3},{7,2},{8,13},{9,12},{10,... | collective-permute-start | bytes 12296 | tf_op jit(solution)/shard_map/ppermute | solution.py:243
  63.9 5.2 %collective-permute-start.7 = (f32[4,1,256]{2,1,0:T(1,128)S(1)}, f32[4,1,256]{2,1,0:T(1,128)S(1)}, u32[]{:S(2)}, u32[]{:S(2)}) collective-permute-start(f32[4,1,256]{2,1,0:T(1,128)S(1)} %get-tuple-element.64.refs_6_), channel_id=1, source_target_pairs={{0,4},{1,5},{2,6},{3,7},{4,0},{5,1},{6,2},{7,3},{8,12},{9,13},{10,... | collective-permute-start | bytes 12296 | tf_op jit(solution)/shard_map/ppermute | solution.py:243
  65.3 3.8 %collective-permute-start.6 = (f32[4,1,256]{2,1,0:T(1,128)S(1)}, f32[4,1,256]{2,1,0:T(1,128)S(1)}, u32[]{:S(2)}, u32[]{:S(2)}) collective-permute-start(f32[4,1,256]{2,1,0:T(1,128)S(1)} %get-tuple-element.64.refs_6_), channel_id=1, source_target_pairs={{0,1},{1,0},{2,3},{3,2},{4,5},{5,4},{6,7},{7,6},{8,9},{9,8},{10,11... | collective-permute-start | bytes 12296 | tf_op jit(solution)/shard_map/ppermute | solution.py:243
  66.9 3.1 %collective-permute-start.14 = (f32[4,1,256]{2,1,0:T(1,128)S(1)}, f32[4,1,256]{2,1,0:T(1,128)S(1)}, u32[]{:S(2)}, u32[]{:S(2)}) collective-permute-start(f32[4,1,256]{2,1,0:T(1,128)S(1)} %get-tuple-element.70.refs_16_), channel_id=1, source_target_pairs={{0,5},{1,4},{2,7},{3,6},{4,1},{5,0},{6,3},{7,2},{8,13},{9,12},{10,... | collective-permute-start | bytes 12296 | tf_op jit(solution)/shard_map/ppermute | solution.py:243
  68.0 3.6 %collective-permute-start.13 = (f32[4,1,256]{2,1,0:T(1,128)S(1)}, f32[4,1,256]{2,1,0:T(1,128)S(1)}, u32[]{:S(2)}, u32[]{:S(2)}) collective-permute-start(f32[4,1,256]{2,1,0:T(1,128)S(1)} %get-tuple-element.70.refs_16_), channel_id=1, source_target_pairs={{0,4},{1,5},{2,6},{3,7},{4,0},{5,1},{6,2},{7,3},{8,12},{9,13},{10,... | collective-permute-start | bytes 12296 | tf_op jit(solution)/shard_map/ppermute | solution.py:243
  69.1 2.5 %collective-permute-start.12 = (f32[4,1,256]{2,1,0:T(1,128)S(1)}, f32[4,1,256]{2,1,0:T(1,128)S(1)}, u32[]{:S(2)}, u32[]{:S(2)}) collective-permute-start(f32[4,1,256]{2,1,0:T(1,128)S(1)} %get-tuple-element.70.refs_16_), channel_id=1, source_target_pairs={{0,1},{1,0},{2,3},{3,2},{4,5},{5,4},{6,7},{7,6},{8,9},{9,8},{10,11... | collective-permute-start | bytes 12296 | tf_op jit(solution)/shard_map/ppermute | solution.py:243
  72.4 5.0 %collective-permute-start.15 = (f32[128,256]{1,0:T(8,128)S(1)}, f32[128,256]{1,0:T(8,128)S(1)}, u32[]{:S(2)}, u32[]{:S(2)}) collective-permute-start(f32[128,256]{1,0:T(8,128)S(1)} %get-tuple-element.73), channel_id=1, source_target_pairs={{0,2},{1,3},{2,0},{3,1},{4,6},{5,7},{6,4},{7,5},{8,10},{9,11},{10,... | collective-permute-start | bytes 393224 | tf_op jit(solution)/shard_map/ppermute | solution.py:243
  77.5 5.4 %collective-permute-start.16 = (f32[136,256]{1,0:T(8,128)S(1)}, f32[136,256]{1,0:T(8,128)S(1)}, u32[]{:S(2)}, u32[]{:S(2)}) collective-permute-start(f32[136,256]{1,0:T(8,128)S(1)} %get-tuple-element.75), channel_id=1, source_target_pairs={{0,2},{1,3},{2,0},{3,1},{4,6},{5,7},{6,4},{7,5},{8,10},{9,11},{10,... | collective-permute-start | bytes 417800 | tf_op jit(solution)/shard_map/ppermute | solution.py:243
  79.0 15.5 %copy-start = (f32[256,256]{1,0:T(8,128)S(1)}, f32[256,256]{1,0:T(8,128)}, u32[]{:S(2)}) copy-start(f32[256,256]{1,0:T(8,128)} %refs_0_.3) | copy-start | bytes 786436
  79.0 9.5 %collective-permute-start.17 = (f32[128,256]{1,0:T(8,128)S(1)}, f32[128,256]{1,0:T(8,128)S(1)}, u32[]{:S(2)}, u32[]{:S(2)}) collective-permute-start(f32[128,256]{1,0:T(8,128)S(1)} %add.7), channel_id=1, source_target_pairs={{0,8},{1,9},{2,10},{3,11},{4,12},{5,13},{6,14},{7,15},{8,0},{9,1},... | collective-permute-start | bytes 393224 | tf_op jit(solution)/shard_map/ppermute | solution.py:243
  82.9 11.6 %collective-permute-start.18 = (f32[264,256]{1,0:T(8,128)S(1)}, f32[264,256]{1,0:T(8,128)S(1)}, u32[]{:S(2)}, u32[]{:S(2)}) collective-permute-start(f32[264,256]{1,0:T(8,128)S(1)} %get-tuple-element.82), channel_id=1, source_target_pairs={{0,2},{1,3},{2,0},{3,1},{4,6},{5,7},{6,4},{7,5},{8,10},{9,11},{10,... | collective-permute-start | bytes 811016 | tf_op jit(solution)/shard_map/ppermute | solution.py:243
  84.4 10.1 %copy-start.1 = (f32[256]{0:T(256)S(1)}, f32[256]{0:T(256)}, u32[]{:S(2)}) copy-start(f32[256]{0:T(256)} %param.19) | copy-start | bytes 3076
  88.5 6.0 %collective-permute-start.19 = (f32[136,256]{1,0:T(8,128)S(1)}, f32[136,256]{1,0:T(8,128)S(1)}, u32[]{:S(2)}, u32[]{:S(2)}) collective-permute-start(f32[136,256]{1,0:T(8,128)S(1)} %add.6), channel_id=1, source_target_pairs={{0,8},{1,9},{2,10},{3,11},{4,12},{5,13},{6,14},{7,15},{8,0},{9,1},... | collective-permute-start | bytes 417800 | tf_op jit(solution)/shard_map/ppermute | solution.py:243
